TPU v7x, 32 devices: a whole 2x2x4 slice. The times are simulated.
32 devices in a mesh: dp: 4 (over y, x), ep: 8 (over z, core).
Axes of the slice: x: 2, y: 2, z: 4, core: 2. Of those that a mesh axis runs over, the one named last changes fastest.
Arguments:
- tokens: bfloat16 [24576, 1024], P(('dp', 'ep')), may hold values from -6 to 6
- lengths: int32 [32], P(('dp', 'ep')), may hold values from 256 to 768, as said below
- key_mask: int32 [24576], P(('dp', 'ep')), may hold values 0 or 1
- routes: int32 [24576, 1], P(('dp', 'ep')), may hold values from 0 to 7; in each aligned block of 768 rows (0 to 767, 768 to 1535, ...) at most 120 rows name the same one
- norm1_gain: float32 [1024], replicated, may hold values from 0.5 to 1.5
- norm1_bias: float32 [1024], replicated, may hold values from -2.5 to 2.5
- qkv_weight: bfloat16 [1024, 3072], replicated, may hold values from -0.1875 to 0.1875
- out_weight: bfloat16 [1024, 1024], replicated, may hold values from -1.5 to 1.5
- norm2_gain: float32 [1024], replicated, may hold values from 0.5 to 1.5
- norm2_bias: float32 [1024], replicated, may hold values from -2.5 to 2.5
- up_weight: bfloat16 [1024, 4096], replicated, may hold values from -0.1875 to 0.1875
- down_weight: bfloat16 [4096, 1024], replicated, may hold values from -0.09375 to 0.09375
- router_weight: bfloat16 [1024, 8], replicated, may hold values from -0.125 to 0.125
- mix_weight: bfloat16 [1024, 2], replicated, may hold values from -0.125 to 0.125
- expert_up: bfloat16 [8, 1024, 4096], P('ep'), may hold values from -0.1875 to 0.1875
- expert_down: bfloat16 [8, 4096, 1024], P('ep'), may hold values from -0.75 to 0.75
- cotangent: bfloat16 [24576, 1024], P(('dp', 'ep')), may hold values from -6 to 6
Outputs:
- outputs: bfloat16 [24576, 1024], P(('dp', 'ep'))
- grad_inputs: bfloat16 [24576, 1024], P(('dp', 'ep'))
- grad_norm1_gain: float32 [1024], P(('dp', 'ep'))
- grad_norm1_bias: float32 [1024], P(('dp', 'ep'))
- grad_qkv_weight: float32 [1024, 3072], P(None, ('dp', 'ep'))
- grad_out_weight: float32 [1024, 1024], P(('dp', 'ep'))
- grad_norm2_gain: float32 [1024], P(('dp', 'ep'))
- grad_norm2_bias: float32 [1024], P(('dp', 'ep'))
- grad_up_weight: float32 [1024, 4096], P('ep', 'dp')
- grad_down_weight: float32 [4096, 1024], P('dp', 'ep')
- grad_router_weight: float32 [1024, 8], P(('dp', 'ep'))
- grad_mix_weight: float32 [1024, 2], P(('dp', 'ep'))
- grad_expert_up: float32 [8, 1024, 4096], P('ep', None, 'dp')
- grad_expert_down: float32 [8, 4096, 1024], P('ep', 'dp')
Inputs may be any that keep to these rules, and one draw needn't show every extreme that they name: `lengths`: each slot holds one sequence of that many tokens from its start; the rest of the slot is padding. `routes`: among the rows of one device, at most 120 name the same expert.
All inputs are finite; a program needn't handle non-finite values. No bound on the sum of `key_mask` on one device may be relied on, other than what follows from the above.
Results may differ from a plain program's by a relative error of at most 0.015.
Values may be sent and summed in bfloat16 or wider, within the bound.
No kernel may reach another device: no remote copies, remote signals or barrier semaphores. Data moves between devices by JAX's collectives and lax.ppermute only.
A program may use at most 384 MiB of HBM per device.

v0:
```python
import jax
import jax.numpy as jnp
from jax import lax
from jax.sharding import PartitionSpec as P

D = 1024
HEADS = 16
HEAD_DIM = 64


epsilon = 1e-05
precise = lax.Precision.HIGHEST
masked_score = -1e30


def layer_norm(values, norm_gain, norm_bias):
    average = jnp.mean(values, axis=-1, keepdims=True)
    centered = values - average
    variance = jnp.mean(centered * centered, axis=-1, keepdims=True)
    return centered * lax.rsqrt(variance + epsilon) * norm_gain + norm_bias


def smooth_gate(values):
    return jax.nn.gelu(values, approximate=True)


def softmax_rows(values):
    row_top = jnp.max(values, axis=-1, keepdims=True)
    raised = jnp.exp(values - row_top)
    return raised / jnp.sum(raised, axis=-1, keepdims=True)


def allowed_keys(length, mask_slot):
    row_count = mask_slot.shape[0]
    position = jnp.arange(row_count)
    earlier = position[None, :] <= position[:, None]
    usable = (position < length) & (mask_slot == 1)
    itself = position[None, :] == position[:, None]
    return earlier & (usable[None, :] | itself)


def split_heads(qkv_slot):
    row_count = qkv_slot.shape[0]
    queries = qkv_slot[:, :D].reshape(row_count, HEADS, HEAD_DIM)
    key_rows = qkv_slot[:, D : 2 * D].reshape(row_count, HEADS, HEAD_DIM)
    value_rows = qkv_slot[:, 2 * D :].reshape(row_count, HEADS, HEAD_DIM)
    return (queries, key_rows, value_rows)


def attend_forward(packed):
    qkv_slot, length, mask_slot = packed
    row_count = qkv_slot.shape[0]
    queries, key_rows, value_rows = split_heads(qkv_slot)
    score_scale = HEAD_DIM ** (-0.5)
    scores = (
        jnp.einsum("qhd,khd->hqk", queries, key_rows, preferred_element_type=jnp.float32)
        * score_scale
    )
    masked = jnp.where(allowed_keys(length, mask_slot)[None], scores, masked_score)
    row_top = jnp.max(masked, axis=-1, keepdims=True)
    raised = jnp.exp(masked - row_top)
    row_total = jnp.sum(raised, axis=-1, keepdims=True)
    weights_low = (raised / row_total).astype(jnp.bfloat16)
    context = jnp.einsum(
        "hqk,khd->qhd", weights_low, value_rows, preferred_element_type=jnp.float32
    )
    return (context.astype(jnp.bfloat16).reshape(row_count, D), row_top + jnp.log(row_total))


def attend_backward(packed):
    qkv_slot, length, mask_slot, log_total, grad_context = packed
    row_count = qkv_slot.shape[0]
    queries, key_rows, value_rows = split_heads(qkv_slot)
    score_scale = HEAD_DIM ** (-0.5)
    scores = (
        jnp.einsum("qhd,khd->hqk", queries, key_rows, preferred_element_type=jnp.float32)
        * score_scale
    )
    weights = jnp.where(allowed_keys(length, mask_slot)[None], jnp.exp(scores - log_total), 0.0)
    weights_low = weights.astype(jnp.bfloat16)
    grad_heads = grad_context.reshape(row_count, HEADS, HEAD_DIM)
    grad_values = jnp.einsum(
        "hqk,qhd->khd", weights_low, grad_heads, preferred_element_type=jnp.float32
    )
    grad_weights = jnp.einsum(
        "qhd,khd->hqk", grad_heads, value_rows, preferred_element_type=jnp.float32
    )
    grad_scores = weights * (grad_weights - jnp.sum(grad_weights * weights, axis=-1, keepdims=True))
    grad_scores = grad_scores.astype(jnp.bfloat16)
    grad_queries = (
        jnp.einsum("hqk,khd->qhd", grad_scores, key_rows, preferred_element_type=jnp.float32)
        * score_scale
    )
    grad_keys = (
        jnp.einsum("hqk,qhd->khd", grad_scores, queries, preferred_element_type=jnp.float32)
        * score_scale
    )
    return jnp.concatenate(
        [
            grad_queries.reshape(row_count, D),
            grad_keys.reshape(row_count, D),
            grad_values.reshape(row_count, D),
        ],
        axis=1,
    )


def shards(
    tokens,
    lengths,
    key_mask,
    routes,
    norm1_gain,
    norm1_bias,
    qkv_weight,
    out_weight,
    norm2_gain,
    norm2_bias,
    up_weight,
    down_weight,
    router_weight,
    mix_weight,
    expert_up,
    expert_down,
    cotangent,
):
    device_rows = tokens.shape[0]
    slot_count = lengths.shape[0]
    slot_rows = device_rows // slot_count
    local_experts = expert_up.shape[0]
    groups = lax.axis_size("ep")
    experts = local_experts * groups
    capacity = (5 * device_rows + 4 * experts - 1) // (4 * experts)
    buffer_rows = experts * capacity
    inputs = tokens.astype(jnp.float32)
    row_live = jnp.arange(device_rows) % slot_rows < jnp.repeat(
        lengths, slot_rows, total_repeat_length=device_rows
    )
    live_scale = row_live.astype(jnp.float32)
    flat_routes = routes[:, 0]
    onehot = (flat_routes[:, None] == jnp.arange(experts)[None, :]).astype(jnp.float32)
    routed = onehot * live_scale[:, None]
    rows_ahead = jnp.cumsum(routed, axis=0) - routed
    slot_place = jnp.sum(rows_ahead * routed, axis=1).astype(jnp.int32)
    target = jnp.where(row_live, flat_routes * capacity + slot_place, buffer_rows)

    def scatter_rows(values):
        empty = jnp.zeros((buffer_rows, D), jnp.bfloat16)
        return (
            empty.at[target].set(values, mode="drop").reshape(groups, local_experts * capacity, D)
        )

    def gather_rows(values):
        flat_rows = values.reshape(buffer_rows, D)
        return jnp.take(flat_rows, target, axis=0, mode="fill", fill_value=0).astype(jnp.float32)

    normed1, norm1_back = jax.vjp(layer_norm, inputs, norm1_gain, norm1_bias)
    first_low = normed1.astype(jnp.bfloat16)
    qkv_low = jnp.dot(first_low, qkv_weight, preferred_element_type=jnp.float32).astype(
        jnp.bfloat16
    )
    per_slot = qkv_low.reshape(slot_count, slot_rows, 3 * D)
    mask_slots = key_mask.reshape(slot_count, slot_rows)
    context_slots, log_totals = lax.map(attend_forward, (per_slot, lengths, mask_slots))
    context_low = context_slots.reshape(device_rows, D)
    middle = inputs + jnp.dot(context_low, out_weight, preferred_element_type=jnp.float32)
    normed2, norm2_back = jax.vjp(layer_norm, middle, norm2_gain, norm2_bias)
    second_low = normed2.astype(jnp.bfloat16)
    dense_pre = jnp.dot(second_low, up_weight, preferred_element_type=jnp.float32)
    dense_hidden, dense_gate_back = jax.vjp(smooth_gate, dense_pre)
    hidden_low = dense_hidden.astype(jnp.bfloat16)
    dense_out = jnp.dot(hidden_low, down_weight, preferred_element_type=jnp.float32)
    router_probs = softmax_rows(
        jnp.dot(second_low, router_weight, preferred_element_type=jnp.float32)
    )
    chosen = jnp.sum(router_probs * onehot, axis=1) * live_scale
    mixing = softmax_rows(jnp.dot(second_low, mix_weight, preferred_element_type=jnp.float32))
    received = lax.all_to_all(
        scatter_rows(second_low), "ep", split_axis=0, concat_axis=0, tiled=True
    )
    arriving = received.reshape(groups, local_experts, capacity, D)
    expert_pre = jnp.einsum(
        "secd,edf->secf", arriving, expert_up, preferred_element_type=jnp.float32
    )
    expert_hidden, expert_gate_back = jax.vjp(smooth_gate, expert_pre)
    expert_low = expert_hidden.astype(jnp.bfloat16)
    expert_out = jnp.einsum(
        "secf,efd->secd", expert_low, expert_down, preferred_element_type=jnp.float32
    ).astype(jnp.bfloat16)
    returned = lax.all_to_all(
        expert_out.reshape(groups, local_experts * capacity, D),
        "ep",
        split_axis=0,
        concat_axis=0,
        tiled=True,
    )
    expert_rows = gather_rows(returned)
    expert_term = chosen[:, None] * expert_rows
    mixed = mixing[:, 0:1] * dense_out + mixing[:, 1:2] * expert_term
    outputs = (middle + mixed).astype(jnp.bfloat16)
    grad_out = cotangent.astype(jnp.float32)
    grad_mixing = jnp.stack(
        [jnp.sum(grad_out * dense_out, axis=1), jnp.sum(grad_out * expert_term, axis=1)], axis=1
    )
    grad_mix_logits = mixing * (grad_mixing - jnp.sum(grad_mixing * mixing, axis=1, keepdims=True))
    grad_term = mixing[:, 1:2] * grad_out
    grad_chosen = jnp.sum(grad_term * expert_rows, axis=1) * live_scale
    grad_probs = onehot * grad_chosen[:, None]
    grad_router_logits = router_probs * (
        grad_probs - jnp.sum(grad_probs * router_probs, axis=1, keepdims=True)
    )
    grad_rows_low = (chosen[:, None] * grad_term).astype(jnp.bfloat16)
    grad_arriving = lax.all_to_all(
        scatter_rows(grad_rows_low), "ep", split_axis=0, concat_axis=0, tiled=True
    )
    grad_arriving = grad_arriving.reshape(groups, local_experts, capacity, D)
    grad_expert_hidden = jnp.einsum(
        "secd,efd->secf", grad_arriving, expert_down, preferred_element_type=jnp.float32
    )
    grad_expert_pre = expert_gate_back(grad_expert_hidden)[0].astype(jnp.bfloat16)
    grad_expert_down = jnp.einsum(
        "secf,secd->efd", expert_low, grad_arriving, preferred_element_type=jnp.float32
    )
    grad_expert_up = jnp.einsum(
        "secd,secf->edf", arriving, grad_expert_pre, preferred_element_type=jnp.float32
    )
    grad_sent_back = jnp.einsum(
        "secf,edf->secd", grad_expert_pre, expert_up, preferred_element_type=jnp.float32
    ).astype(jnp.bfloat16)
    grad_returned = lax.all_to_all(
        grad_sent_back.reshape(groups, local_experts * capacity, D),
        "ep",
        split_axis=0,
        concat_axis=0,
        tiled=True,
    )
    grad_expert_in = gather_rows(grad_returned)
    grad_dense_low = (mixing[:, 0:1] * grad_out).astype(jnp.bfloat16)
    grad_dense_hidden = jnp.dot(grad_dense_low, down_weight.T, preferred_element_type=jnp.float32)
    grad_dense_pre = dense_gate_back(grad_dense_hidden)[0].astype(jnp.bfloat16)
    second_wide = second_low.T.astype(jnp.float32)
    grad_router_weight = jnp.dot(second_wide, grad_router_logits, precision=precise)
    grad_mix_weight = jnp.dot(second_wide, grad_mix_logits, precision=precise)
    grad_second = (
        jnp.dot(grad_dense_pre, up_weight.T, preferred_element_type=jnp.float32) + grad_expert_in
    )
    grad_second = grad_second + jnp.dot(
        grad_router_logits, router_weight.T.astype(jnp.float32), precision=precise
    )
    grad_second = grad_second + jnp.dot(
        grad_mix_logits, mix_weight.T.astype(jnp.float32), precision=precise
    )
    grad_middle_norm, grad_norm2_gain, grad_norm2_bias = norm2_back(grad_second)
    second_all, grad_dense_all = (
        lax.all_gather(second_low, "dp", axis=0, tiled=True),
        lax.all_gather(grad_dense_low, "dp", axis=0, tiled=True),
    )
    pre_columns, hidden_columns = (
        lax.all_to_all(grad_dense_pre, "dp", split_axis=1, concat_axis=0, tiled=True),
        lax.all_to_all(hidden_low, "dp", split_axis=1, concat_axis=0, tiled=True),
    )
    grad_up_block = jnp.dot(second_all.T, pre_columns, preferred_element_type=jnp.float32)
    grad_down_block = jnp.dot(hidden_columns.T, grad_dense_all, preferred_element_type=jnp.float32)
    grad_middle = grad_out + grad_middle_norm
    grad_attended = grad_middle.astype(jnp.bfloat16)
    grad_context = jnp.dot(grad_attended, out_weight.T, preferred_element_type=jnp.float32).astype(
        jnp.bfloat16
    )
    grad_qkv = lax.map(
        attend_backward,
        (per_slot, lengths, mask_slots, log_totals, grad_context.reshape(slot_count, slot_rows, D)),
    )
    grad_qkv_low = grad_qkv.reshape(device_rows, 3 * D).astype(jnp.bfloat16)
    grad_first = jnp.dot(grad_qkv_low, qkv_weight.T, preferred_element_type=jnp.float32)
    grad_input_norm, grad_norm1_gain, grad_norm1_bias = norm1_back(grad_first)
    grad_inputs = (grad_middle + grad_input_norm).astype(jnp.bfloat16)
    first_all, grad_attended_all = (
        lax.all_gather(first_low, "dp", axis=0, tiled=True),
        lax.all_gather(grad_attended, "dp", axis=0, tiled=True),
    )
    qkv_columns, context_columns = (
        lax.all_to_all(grad_qkv_low, "dp", split_axis=1, concat_axis=0, tiled=True),
        lax.all_to_all(context_low, "dp", split_axis=1, concat_axis=0, tiled=True),
    )
    grad_qkv_block = jnp.dot(first_all.T, qkv_columns, preferred_element_type=jnp.float32)
    grad_out_block = jnp.dot(
        context_columns.T, grad_attended_all, preferred_element_type=jnp.float32
    )
    expert_summed = (
        lax.psum_scatter(
            grad_expert_up.astype(jnp.bfloat16), "dp", scatter_dimension=2, tiled=True
        ).astype(jnp.float32),
        lax.psum_scatter(
            grad_expert_down.astype(jnp.bfloat16), "dp", scatter_dimension=1, tiled=True
        ).astype(jnp.float32),
    )
    small_summed = (
        lax.psum_scatter(grad_norm1_gain, ("dp", "ep"), scatter_dimension=0, tiled=True),
        lax.psum_scatter(grad_norm1_bias, ("dp", "ep"), scatter_dimension=0, tiled=True),
        lax.psum_scatter(grad_norm2_gain, ("dp", "ep"), scatter_dimension=0, tiled=True),
        lax.psum_scatter(grad_norm2_bias, ("dp", "ep"), scatter_dimension=0, tiled=True),
        lax.psum_scatter(grad_router_weight, ("dp", "ep"), scatter_dimension=0, tiled=True),
        lax.psum_scatter(grad_mix_weight, ("dp", "ep"), scatter_dimension=0, tiled=True),
    )
    qkv_sum, out_sum, up_sum, down_sum = (
        lax.psum_scatter(
            grad_qkv_block.astype(jnp.bfloat16), "ep", scatter_dimension=1, tiled=True
        ).astype(jnp.float32),
        lax.psum_scatter(
            grad_out_block.astype(jnp.bfloat16), "ep", scatter_dimension=0, tiled=True
        ).astype(jnp.float32),
        lax.psum_scatter(
            grad_up_block.astype(jnp.bfloat16), "ep", scatter_dimension=0, tiled=True
        ).astype(jnp.float32),
        lax.psum_scatter(
            grad_down_block.astype(jnp.bfloat16), "ep", scatter_dimension=1, tiled=True
        ).astype(jnp.float32),
    )
    return (
        outputs,
        grad_inputs,
        small_summed[0],
        small_summed[1],
        qkv_sum,
        out_sum,
        small_summed[2],
        small_summed[3],
        up_sum,
        down_sum,
        small_summed[4],
        small_summed[5],
        expert_summed[0],
        expert_summed[1],
    )


def solution(mesh):
    return jax.shard_map(
        shards,
        mesh=mesh,
        in_specs=(
            P(("dp", "ep"), None),
            P(("dp", "ep")),
            P(("dp", "ep")),
            P(("dp", "ep"), None),
            P(),
            P(),
            P(),
            P(),
            P(),
            P(),
            P(),
            P(),
            P(),
            P(),
            P("ep", None, None),
            P("ep", None, None),
            P(("dp", "ep"), None),
        ),
        out_specs=(
            P(("dp", "ep"), None),
            P(("dp", "ep"), None),
            P(("dp", "ep")),
            P(("dp", "ep")),
            P(None, ("dp", "ep")),
            P(("dp", "ep"), None),
            P(("dp", "ep")),
            P(("dp", "ep")),
            P("ep", "dp"),
            P("dp", "ep"),
            P(("dp", "ep"), None),
            P(("dp", "ep"), None),
            P("ep", None, "dp"),
            P("ep", "dp", None),
        ),
        check_vma=False,
    )
```

profile of v0, /device:TPU:0, one launch (start us, length us, event | category | flops | bytes accessed | tf_op | source)
XLA Modules:
  0.0 1110.4 jit_solution(724244046838816050)
XLA Ops:
  31.5 16.7 %select_reduce_fusion = (f32[16,768]{1,0:T(8,128)S(1)}, f32[16,768,768]{1,2,0:T(8,128)}) fusion(pred[768,768]{0,1:T(8,128)(4,1)S(1)} %fusion.65, bf16[768,16,64]{0,2,1:T(8,128)(2,1)} %bitcast.197, bf16[768,16,64]{0,2,1:T(8,128)(2,1)} %bitcast.199), kind=kOutput, calls=%fused_computation.9 | convolution fusion | flops 1236258816 | bytes 41533440 | tf_op jit(solution)/shard_map/while/body/eval_jaxpr/qhd,khd->hqk/dot_general | solution.py:56
  48.3 16.9 %fusion = f32[16,768]{1,0:T(8,128)S(1)} fusion(f32[16,768,768]{1,2,0:T(8,128)} %get-tuple-element.107, f32[16,768]{1,0:T(8,128)S(1)} %get-tuple-element.106, pred[768,768]{0,1:T(8,128)(4,1)S(1)} %fusion.65), kind=kLoop, calls=%fused_computation.10 | loop fusion | flops 37736448 | bytes 38436864 | tf_op jit(solution)/shard_map/while/body/eval_jaxpr/reduce_sum | solution.py:62
  67.8 18.7 %fusion.80 = bf16[16,64,768]{2,1,0:T(8,128)(2,1)} fusion(bf16[768,16,64]{0,2,1:T(8,128)(2,1)} %bitcast.205, f32[16,768,768]{1,2,0:T(8,128)} %get-tuple-element.107, f32[16,768]{1,0:T(8,128)S(1)} %fusion, f32[16,768]{1,0:T(8,128)S(1)} %get-tuple-element.106, pred[768,768]{0,1:T(8,128)(4,1)S(1)} %fusion.65), kind=kOutput, calls=%fused_computation.111 | convolution fusion | flops 1255931904 | bytes 41582592 | tf_op jit(solution)/shard_map/while/body/eval_jaxpr/hqk,khd->qhd/dot_general | solution.py:64
  120.4 12.2 %fusion.140 = f32[768,4096]{1,0:T(8,128)} fusion(bf16[768,1024]{1,0:T(8,128)(2,1)} %fusion.62, bf16[4096,1024]{1,0:T(8,128)(2,1)} %param.34), kind=kOutput, calls=%fused_computation.199 | convolution fusion | flops 6442450944 | bytes 22544384 | tf_op jit(solution)/shard_map/dot_general | solution.py:239
  141.8 21.7 %fusion.23 = (bf16[768,4096]{1,0:T(8,128)(2,1)}, bf16[768,4096]{1,0:T(8,128)(2,1)}) fusion(f32[768,4096]{1,0:T(8,128)} %fusion.140, bf16[768,1024]{1,0:T(8,128)(2,1)} %add_convert_fusion.1, bf16[1024,4096]{1,0:T(8,128)(2,1)} %param.33), kind=kOutput, calls=%fused_computation.41 | convolution fusion | flops 6511656960 | bytes 35127296 | tf_op jit(solution)/shard_map/dot_general | solution.py:169
  171.3 11.3 %fusion.30 = f32[8,120,4096]{2,1,0:T(8,128)S(1)} fusion(bf16[8,120,1024]{2,1,0:T(8,128)(2,1)} %all-to-all-done, bf16[1,1024,4096]{2,1,0:T(8,128)(2,1)} %param.37), kind=kOutput, calls=%fused_computation.50 | convolution fusion | flops 8053063680 | bytes 26083328 | tf_op jit(solution)/shard_map/secd,edf->secf/dot_general | solution.py:182
  188.3 14.6 %fusion.75 = bf16[8,120,1024]{2,1,0:T(8,128)(2,1)} fusion(bf16[1,4096,1024]{2,1,0:T(8,128)(2,1)} %param.38, f32[8,120,4096]{2,1,0:T(8,128)S(1)} %fusion.30), kind=kOutput, calls=%fused_computation.110 | convolution fusion | flops 8089436160 | bytes 26083328 | tf_op jit(solution)/shard_map/secf,efd->secd/dot_general | solution.py:187
  202.8 14.7 %all-to-all-done.2 = bf16[8,120,1024]{2,1,0:T(8,128)(2,1)} async-done(((bf16[8,120,1024]{2,1,0:T(8,128)(2,1)}), bf16[8,120,1024]{2,1,0:T(8,128)(2,1)}, u32[]{:S(2)}, u32[]{:S(2)}) %all-to-all-start.2) | async-done | bytes 1966112 | tf_op jit(solution)/shard_map/all_to_all | solution.py:213
  222.1 23.5 %fusion.12 = bf16[8,1,120,4096]{3,2,0,1:T(8,128)(2,1)} fusion(f32[8,120,4096]{2,1,0:T(8,128)} %copy-done.69, bf16[8,120,1024]{2,1,0:T(8,128)(2,1)} %all-to-all-done.2, bf16[1,4096,1024]{2,1,0:T(8,128)(2,1)} %param.38), kind=kOutput, calls=%fused_computation.27 | convolution fusion | flops 8131706880 | bytes 33947648 | tf_op jit(solution)/shard_map/secd,efd->secf/dot_general | solution.py:217
  245.6 14.0 %fusion.70 = bf16[8,120,1024]{2,1,0:T(8,128)(2,1)} fusion(bf16[1,1024,4096]{2,1,0:T(8,128)(2,1)} %param.37, bf16[8,1,120,4096]{3,2,0,1:T(8,128)(2,1)} %fusion.12), kind=kOutput, calls=%fused_computation.109 | convolution fusion | flops 8054046720 | bytes 18219008 | tf_op jit(solution)/shard_map/secf,edf->secd/dot_general | solution.py:227
  272.8 12.6 %fusion.141 = f32[768,1024]{1,0:T(8,128)} fusion(bf16[768,4096]{1,0:T(8,128)(2,1)} %get-tuple-element.100, bf16[1024,4096]{1,0:T(8,128)(2,1)} %param.33), kind=kOutput, calls=%fused_computation.200 | convolution fusion | flops 6442450944 | bytes 17825792 | tf_op jit(solution)/shard_map/dot_general | solution.py:245
  291.8 15.0 %fusion.64 = (f32[768]{0:T(1024)S(1)}, f32[768]{0:T(1024)S(1)}, f32[768]{0:T(1024)S(1)}, bf16[768,1024]{1,0:T(8,128)(2,1)}) fusion(bf16[768,1024]{1,0:T(8,128)(2,1)} %param.39, f32[768]{0:T(1024)S(1)} %fusion.108, bf16[768,1024]{1,0:T(8,128)(2,1)} %gather_fusion, pred[768]{0:T(1024)(128)(4,1)S(1)} %get-tuple-element.98, f32[768]{0:T(1024)S(1)} %get-tuple-element.89, ...), kind=kOutput, calls=%fused_computation.93 | convolution fusion | flops 6455031808 | bytes 22563584 | tf_op jit(solution)/shard_map/dot_general | solution.py:172
  306.7 12.3 %all-to-all-done.3 = bf16[8,120,1024]{2,1,0:T(8,128)(2,1)} async-done(((bf16[8,120,1024]{2,1,0:T(8,128)(2,1)}), bf16[8,120,1024]{2,1,0:T(8,128)(2,1)}, u32[]{:S(2)}, u32[]{:S(2)}) %all-to-all-start.3) | async-done | bytes 1966112 | tf_op jit(solution)/shard_map/all_to_all | solution.py:230
  344.9 32.2 %multiply_reduce_fusion = (f32[16,768]{1,0:T(8,128)S(1)}, f32[16,768,768]{1,2,0:T(8,128)}) fusion(f32[16,768,768]{1,2,0:T(8,128)} %get-tuple-element.107, f32[16,768]{1,0:T(8,128)S(1)} %copy-done.20, pred[768,768]{0,1:T(8,128)(4,1)S(1)} %copy-done.9, bf16[768,16,64]{0,2,1:T(8,128)(2,1)} %bitcast.207, bf16[768,16,64]{0,2,1:T(8,128)(2,1)S(1)} %bitcast.206), kind=kOutput, calls=%fused_computation.5 | convolution fusion | flops 1255133184 | bytes 79331328 | tf_op jit(solution)/shard_map/while/body/eval_jaxpr/qhd,khd->hqk/dot_general | solution.py:85
  377.1 31.3 %multiply_convert_fusion = bf16[16,768,768]{1,2,0:T(8,128)(2,1)} fusion(f32[16,768,768]{1,2,0:T(8,128)} %get-tuple-element.116, f32[16,768,768]{1,2,0:T(8,128)} %get-tuple-element.107, f32[16,768]{1,0:T(8,128)S(1)} %get-tuple-element.115, f32[16,768]{1,0:T(8,128)S(1)} %copy-done.20, pred[768,768]{0,1:T(8,128)(4,1)S(1)} %copy-done.9), kind=kLoop, calls=%fused_computation.4 | loop fusion | flops 56623104 | bytes 95059968 | tf_op jit(solution)/shard_map/while/body/eval_jaxpr/convert_element_type | solution.py:89
  408.4 10.4 convolution_multiply_fusion
  429.2 15.3 %fusion.2 = bf16[16,64,768]{2,1,0:T(8,128)(2,1)S(1)} fusion(bf16[768,16,64]{0,2,1:T(8,128)(2,1)S(1)} %bitcast.208, f32[16,768,768]{1,2,0:T(8,128)} %get-tuple-element.107, f32[16,768]{1,0:T(8,128)S(1)} %copy-done.20, pred[768,768]{0,1:T(8,128)(4,1)S(1)} %copy-done.9), kind=kOutput, calls=%fused_computation.14 | convolution fusion | flops 1245708288 | bytes 41533440 | tf_op jit(solution)/shard_map/while/body/eval_jaxpr/hqk,qhd->khd/dot_general | solution.py:82
  458.6 46.4 %all-to-all-done.4 = bf16[768,4,768]{0,2,1:T(8,128)(2,1)} async-done(((bf16[768,4,768]{0,2,1:T(8,128)(2,1)}), bf16[768,4,768]{0,2,1:T(8,128)(2,1)}, u32[]{:S(2)}, u32[]{:S(2)}) %all-to-all-start.4) | async-done | bytes 4718624 | tf_op jit(solution)/shard_map/all_to_all | solution.py:282
  538.7 42.4 %all-to-all-done.7 = bf16[768,4,1024]{2,0,1:T(8,128)(2,1)} async-done(((bf16[768,4,1024]{2,0,1:T(8,128)(2,1)}), bf16[768,4,1024]{2,0,1:T(8,128)(2,1)}, u32[]{:S(2)}, u32[]{:S(2)}) %all-to-all-start.7) | async-done | bytes 6291488 | tf_op jit(solution)/shard_map/all_to_all | solution.py:260
  586.4 10.7 convolution_convert_fusion.1
  599.7 57.2 %all-to-all-done.6 = bf16[768,4,1024]{2,0,1:T(8,128)(2,1)} async-done(((bf16[768,4,1024]{2,0,1:T(8,128)(2,1)}), bf16[768,4,1024]{2,0,1:T(8,128)(2,1)}, u32[]{:S(2)}, u32[]{:S(2)}) %all-to-all-start.6) | async-done | bytes 6291488 | tf_op jit(solution)/shard_map/all_to_all | solution.py:259
  656.9 11.7 %convolution_convert_fusion.2 = bf16[1024,1024]{1,0:T(8,128)(2,1)} fusion(bf16[3072,1024]{1,0:T(8,128)(2,1)} %all-gather.9.cloned.1.call-done, bf16[3072,1024]{1,0:T(8,128)(2,1)} %bitcast.43), kind=kOutput, calls=%fused_computation.106 | convolution fusion | flops 6443499520 | bytes 14680064 | tf_op jit(solution)/shard_map/dot_general | solution.py:262
  671.5 23.1 %all_to_all.93 = bf16[768,4,256]{2,0,1:T(8,128)(2,1)S(1)} all-to-all(bf16[768,4,256]{2,0,1:T(8,128)(2,1)} %copy.83), channel_id=1, replica_groups=mesh['dp'=4,'ep'=8] {'dp'}, dimensions={1} | all-to-all | bytes 3145728 | tf_op jit(solution)/shard_map/all_to_all | solution.py:283
  700.1 14.2 %fusion.36 = bf16[1,1024,4096]{2,1,0:T(8,128)(2,1)} fusion(bf16[8,120,1024]{2,1,0:T(8,128)(2,1)} %all-to-all-done, bf16[8,1,120,4096]{3,2,0,1:T(8,128)(2,1)} %fusion.12), kind=kOutput, calls=%fused_computation.56 | convolution fusion | flops 8057257984 | bytes 18219008 | tf_op jit(solution)/shard_map/secd,secf->edf/dot_general | solution.py:224
  714.4 17.0 %fusion.39 = bf16[1,4096,1024]{2,1,0:T(8,128)(2,1)} fusion(bf16[8,120,1024]{2,1,0:T(8,128)(2,1)} %all-to-all-done.2, f32[8,120,4096]{2,1,0:T(8,128)} %copy-done.69), kind=kOutput, calls=%fused_computation.57 | convolution fusion | flops 8092647424 | bytes 26083328 | tf_op jit(solution)/shard_map/secf,secd->efd/dot_general | solution.py:221
  745.7 37.4 %all-reduce.4 = (f32[1024]{0:T(1024)S(1)}, f32[1024]{0:T(1024)S(1)}, f32[1024]{0:T(1024)S(1)}, f32[1024]{0:T(1024)S(1)}) all-reduce(f32[1024]{0:T(1024)S(1)} %get-tuple-element.80, f32[1024]{0:T(1024)S(1)} %get-tuple-element.85, f32[1024]{0:T(1024)S(1)} %copy-done.64, ...), channel_id=2, replica_groups=mesh['dp'=4,'ep'=8] {'dp','ep'}, use_global_device_ids=true, to_apply=%region_27.29.clone | all-reduce | flops 4096 | bytes 32768
  793.1 24.4 %reduce-scatter.15.cloned.1.call-done = bf16[1024,96]{0,1:T(8,128)(2,1)} async-done(((bf16[1024,768]{0,1:T(8,128)(2,1)}), bf16[1024,96]{0,1:T(8,128)(2,1)}) %reduce-scatter.15.cloned.1.call-update) | async-done | bytes 196624 | tf_op jit(solution)/shard_map/reduce_scatter | solution.py:306
  819.2 34.5 %reduce-scatter.25.cloned.1.call-done = bf16[128,1024]{1,0:T(8,128)(2,1)} async-done(((bf16[1024,1024]{1,0:T(8,128)(2,1)}), bf16[128,1024]{1,0:T(8,128)(2,1)}) %reduce-scatter.25.cloned.1.call-update) | async-done | bytes 262160
  855.6 34.7 %reduce-scatter.19.cloned.1.call-done = bf16[128,1024]{1,0:T(8,128)(2,1)} async-done(((bf16[1024,1024]{1,0:T(8,128)(2,1)}), bf16[128,1024]{1,0:T(8,128)(2,1)}) %reduce-scatter.19.cloned.1.call-update) | async-done | bytes 262160 | tf_op jit(solution)/shard_map/reduce_scatter | solution.py:312
  892.1 30.0 %reduce-scatter.17.cloned.1.call-done = bf16[32,1024]{1,0:T(8,128)(2,1)} async-done(((bf16[256,1024]{1,0:T(8,128)(2,1)}), bf16[32,1024]{1,0:T(8,128)(2,1)}) %reduce-scatter.17.cloned.1.call-update) | async-done | bytes 65552 | tf_op jit(solution)/shard_map/reduce_scatter | solution.py:309
  923.6 86.1 %reduce-scatter.21.cloned.1.call-done = bf16[1,1024,1024]{2,1,0:T(8,128)(2,1)} async-done(((bf16[1,1024,4096]{2,1,0:T(8,128)(2,1)}), bf16[1,1024,1024]{2,1,0:T(8,128)(2,1)}) %reduce-scatter.21.cloned.1.call-update) | async-done | bytes 2097168 | tf_op jit(solution)/shard_map/reduce_scatter | solution.py:290
  1013.9 85.0 %reduce-scatter.23.cloned.1.call-done = bf16[1,1024,1024]{2,1,0:T(8,128)(2,1)} async-done(((bf16[1,4096,1024]{2,1,0:T(8,128)(2,1)}), bf16[1,1024,1024]{2,1,0:T(8,128)(2,1)}) %reduce-scatter.23.cloned.1.call-update) | async-done | bytes 2097168 | tf_op jit(solution)/shard_map/reduce_scatter | solution.py:293
  (264 shorter events, 245.1 us)
Async XLA Ops:
  8.0 78.5 %copy-start = (bf16[1024,1024]{1,0:T(8,128)(2,1)S(1)}, bf16[1024,1024]{1,0:T(8,128)(2,1)}, u32[]{:S(2)}) copy-start(bf16[1024,1024]{1,0:T(8,128)(2,1)} %param.30) | copy-start | bytes 6291460
  8.1 514.7 %all-gather.5.cloned.1.call-start = ((), (), s32[]{:S(2)}) async-start(), calls=%async_computation.16 | async-start | bytes 7864320 | tf_op jit(solution)/shard_map/all_gather | solution.py:278
  15.0 571.4 %all-gather.11.cloned.1.call-start = ((), (), s32[]{:S(2)}) async-start(), calls=%async_computation.22 | async-start | bytes 7864320 | tf_op jit(solution)/shard_map/all_gather | solution.py:256
  16.0 51.8 %copy-start.8 = (pred[768,768]{0,1:T(8,128)(4,1)}, pred[768,768]{0,1:T(8,128)(4,1)S(1)}, u32[]{:S(2)}) copy-start(pred[768,768]{0,1:T(8,128)(4,1)S(1)} %fusion.65) | copy-start | bytes 1769476
  90.5 14.2 %copy-start.27 = (f32[768]{0:T(1024)}, f32[768]{0:T(1024)S(1)}, u32[]{:S(2)}) copy-start(f32[768]{0:T(1024)S(1)} %broadcast_multiply_fusion) | copy-start | bytes 9220
  92.1 12.6 %copy-start.33 = (f32[768]{0:T(1024)}, f32[768]{0:T(1024)S(1)}, u32[]{:S(2)}) copy-start(f32[768]{0:T(1024)S(1)} %fusion.112) | copy-start | bytes 9220
  98.9 558.0 %all-gather.9.cloned.1.call-start = ((), (), s32[]{:S(2)}) async-start(), calls=%async_computation.20 | async-start | bytes 7864320 | tf_op jit(solution)/shard_map/all_gather | solution.py:255
  99.8 13.8 %copy-start.23 = (s32[768]{0:T(1024)}, s32[768]{0:T(1024)S(1)}, u32[]{:S(2)}) copy-start(s32[768]{0:T(1024)S(1)} %reduce.6) | copy-start | bytes 9220
  113.6 53.1 %all-to-all-start = ((bf16[8,120,1024]{2,1,0:T(8,128)(2,1)}), bf16[8,120,1024]{2,1,0:T(8,128)(2,1)}, u32[]{:S(2)}, u32[]{:S(2)}) async-start(bf16[8,120,1024]{2,1,0:T(8,128)(2,1)} %bitcast.214), calls=%async_computation | async-start | bytes 3932160 | tf_op jit(solution)/shard_map/all_to_all | solution.py:178
  166.7 50.8 %all-to-all-start.2 = ((bf16[8,120,1024]{2,1,0:T(8,128)(2,1)}), bf16[8,120,1024]{2,1,0:T(8,128)(2,1)}, u32[]{:S(2)}, u32[]{:S(2)}) async-start(bf16[8,120,1024]{2,1,0:T(8,128)(2,1)} %bitcast.215), calls=%async_computation.2 | async-start | bytes 3932160 | tf_op jit(solution)/shard_map/all_to_all | solution.py:213
  217.5 50.9 %all-to-all-start.1 = ((bf16[8,120,1024]{2,1,0:T(8,128)(2,1)}), bf16[8,120,1024]{2,1,0:T(8,128)(2,1)}, u32[]{:S(2)}, u32[]{:S(2)}) async-start(bf16[8,120,1024]{2,1,0:T(8,128)(2,1)} %fusion.75), calls=%async_computation.1 | async-start | bytes 3932160 | tf_op jit(solution)/shard_map/all_to_all | solution.py:190
  259.6 13.2 %copy-start.24 = (s32[768]{0:T(1024)S(1)}, s32[768]{0:T(1024)}, u32[]{:S(2)}) copy-start(s32[768]{0:T(1024)} %copy-done.23) | copy-start | bytes 9220
  259.6 13.2 %copy-start.54 = (f32[768]{0:T(1024)S(1)}, f32[768]{0:T(1024)}, u32[]{:S(2)}) copy-start(f32[768]{0:T(1024)} %copy-done.53) | copy-start | bytes 9220
  268.4 50.6 %all-to-all-start.3 = ((bf16[8,120,1024]{2,1,0:T(8,128)(2,1)}), bf16[8,120,1024]{2,1,0:T(8,128)(2,1)}, u32[]{:S(2)}, u32[]{:S(2)}) async-start(bf16[8,120,1024]{2,1,0:T(8,128)(2,1)} %fusion.70), calls=%async_computation.3 | async-start | bytes 3932160 | tf_op jit(solution)/shard_map/all_to_all | solution.py:230
  272.7 421.9 %all-gather.7.cloned.1.call-start = ((), (), s32[]{:S(2)}) async-start(), calls=%async_computation.18 | async-start | bytes 7864320 | tf_op jit(solution)/shard_map/all_gather | solution.py:279
  377.1 31.3 %copy-start.7 = (bf16[768,1024]{0,1:T(8,128)(2,1)S(1)}, bf16[768,1024]{0,1:T(8,128)(2,1)}, u32[]{:S(2)}) copy-start(bf16[768,1024]{0,1:T(8,128)(2,1)} %copy.73) | copy-start | bytes 4718596
  418.8 25.7 %copy-start.16 = (bf16[16,64,768]{2,1,0:T(8,128)(2,1)}, bf16[16,64,768]{2,1,0:T(8,128)(2,1)S(1)}, u32[]{:S(2)}) copy-start(bf16[16,64,768]{2,1,0:T(8,128)(2,1)S(1)} %convolution_multiply_fusion) | copy-start | bytes 4718596
  429.2 15.4 %copy-start.17 = (bf16[16,64,768]{2,1,0:T(8,128)(2,1)}, bf16[16,64,768]{2,1,0:T(8,128)(2,1)S(1)}, u32[]{:S(2)}) copy-start(bf16[16,64,768]{2,1,0:T(8,128)(2,1)S(1)} %convolution_multiply_fusion.1) | copy-start | bytes 4718596
  447.2 57.8 %all-to-all-start.4 = ((bf16[768,4,768]{0,2,1:T(8,128)(2,1)}), bf16[768,4,768]{0,2,1:T(8,128)(2,1)}, u32[]{:S(2)}, u32[]{:S(2)}) async-start(bf16[768,4,768]{0,2,1:T(8,128)(2,1)} %bitcast.203), calls=%async_computation.4 | async-start | bytes 9437184 | tf_op jit(solution)/shard_map/all_to_all | solution.py:282
  505.1 76.0 %all-to-all-start.7 = ((bf16[768,4,1024]{2,0,1:T(8,128)(2,1)}), bf16[768,4,1024]{2,0,1:T(8,128)(2,1)}, u32[]{:S(2)}, u32[]{:S(2)}) async-start(bf16[768,4,1024]{2,0,1:T(8,128)(2,1)} %bitcast.201), calls=%async_computation.10 | async-start | bytes 12582912 | tf_op jit(solution)/shard_map/all_to_all | solution.py:260
  510.4 280.0 %reduce-scatter.29.cloned.1.call-start = ((), (), s32[]{:S(2)}) async-start(), calls=%async_computation.27 | async-start | bytes 540672
  513.1 278.7 %reduce-scatter.27.cloned.1.call-start = ((), (), s32[]{:S(2)}) async-start(), calls=%async_computation.26 | async-start | bytes 540672
  515.7 301.8 %reduce-scatter.15.cloned.1.call-start = ((), (), s32[]{:S(2)}) async-start(), calls=%async_computation.17 | async-start | bytes 1769472 | tf_op jit(solution)/shard_map/reduce_scatter | solution.py:306
  581.0 75.9 %all-to-all-start.6 = ((bf16[768,4,1024]{2,0,1:T(8,128)(2,1)}), bf16[768,4,1024]{2,0,1:T(8,128)(2,1)}, u32[]{:S(2)}, u32[]{:S(2)}) async-start(bf16[768,4,1024]{2,0,1:T(8,128)(2,1)} %bitcast.202), calls=%async_computation.8 | async-start | bytes 12582912 | tf_op jit(solution)/shard_map/all_to_all | solution.py:259
  586.3 267.4 %reduce-scatter.25.cloned.1.call-start = ((), (), s32[]{:S(2)}) async-start(), calls=%async_computation.25 | async-start | bytes 2359296
  599.7 290.6 %reduce-scatter.19.cloned.1.call-start = ((), (), s32[]{:S(2)}) async-start(), calls=%async_computation.21 | async-start | bytes 2359296 | tf_op jit(solution)/shard_map/reduce_scatter | solution.py:312
  668.6 253.5 %reduce-scatter.17.cloned.1.call-start = ((), (), s32[]{:S(2)}) async-start(), calls=%async_computation.19 | async-start | bytes 589824 | tf_op jit(solution)/shard_map/reduce_scatter | solution.py:309
  700.1 309.6 %reduce-scatter.21.cloned.1.call-start = ((), (), s32[]{:S(2)}) async-start(), calls=%async_computation.23 | async-start | bytes 10485760 | tf_op jit(solution)/shard_map/reduce_scatter | solution.py:290
  714.4 384.6 %reduce-scatter.23.cloned.1.call-start = ((), (), s32[]{:S(2)}) async-start(), calls=%async_computation.24 | async-start | bytes 10485760 | tf_op jit(solution)/shard_map/reduce_scatter | solution.py:293
  732.8 11.1 %copy-start.42 = (f32[768]{0:T(1024)S(1)}, f32[768]{0:T(1024)}, u32[]{:S(2)}) copy-start(f32[768]{0:T(1024)} %copy-done.41) | copy-start | bytes 9220
  742.3 43.2 %copy-start.58 = (f32[768]{0:T(1024)S(1)}, f32[768]{0:T(1024)}, u32[]{:S(2)}) copy-start(f32[768]{0:T(1024)} %copy-done.57) | copy-start | bytes 9220
  1009.7 93.3 %copy-start.1 = (bf16[1024,1024]{1,0:T(8,128)(2,1)S(1)}, bf16[1024,1024]{1,0:T(8,128)(2,1)}, u32[]{:S(2)}) copy-start(bf16[1024,1024]{1,0:T(8,128)(2,1)} %param.30) | copy-start | bytes 6291460
  (57 other events, 235.4 us)
Sparse Core Ops, SparseCore 0:
  15.1 72.8 all-gather.4
  99.0 72.7 all-gather.10
  173.7 70.1 all-gather.8
  342.2 69.0 all-gather.6
Sparse Core Ops, SparseCore 1:
  513.7 138.1 reduce-scatter.28
  654.7 130.4 reduce-scatter.26
  787.4 30.1 reduce-scatter.14
  819.8 33.8 reduce-scatter.24
  856.0 34.2 reduce-scatter.18
  892.6 29.5 reduce-scatter.16
  925.3 84.3 reduce-scatter.20
  1012.6 86.2 reduce-scatter.22
where the time goes:
time: 1120 us; the launch traced here: 1110 us
  waiting for transfers between devices  480 us (43%)
  matrix products  339 us (30%)
  other arithmetic  105 us (9%)
  local copies, waits for them, and re-layouts  71.3 us (6%)
  blocking collectives  60.5 us (5%)
  starting transfers between devices  36.4 us (3%)
  between operations  17.2 us (2%)
    reduce_scatter x1, waiting for transfers between devices, shards(): lax.psum_scatter(grad_expert_up.astype(jnp.bfloat16), 'dp', scatter_dimen...  86.1 us
    reduce_scatter x1, waiting for transfers between devices, shards(): lax.psum_scatter(grad_expert_down.astype(jnp.bfloat16), 'dp', scatter_dim...  85 us
    all_to_all x1, waiting for transfers between devices, shards(): lax.all_to_all(grad_dense_pre, 'dp', split_axis=1, concat_axis=0, tiled=T...  57.2 us
    all_to_all x1, waiting for transfers between devices, shards(): lax.all_to_all(grad_qkv_low, 'dp', split_axis=1, concat_axis=0, tiled=True)  46.4 us
    all_to_all x1, waiting for transfers between devices, shards(): lax.all_to_all(hidden_low, 'dp', split_axis=1, concat_axis=0, tiled=True)  42.4 us
    unnamed x1, blocking collectives  37.4 us
    unnamed x15, waiting for transfers between devices  35.4 us
    reduce_scatter x1, waiting for transfers between devices, shards(): lax.psum_scatter(grad_up_block.astype(jnp.bfloat16), 'ep', scatter_dimens...  34.7 us
  transfers between devices with their start and end apart: 19, of which 13 were waited for; matrix products, arithmetic and copies ran while one was open for 44% of the time, Pallas kernels for 0%

commit v1 on v0

v1 whole, which is shorter than its diff:
```python
import functools

import jax
import jax.numpy as jnp
from jax import lax
from jax.experimental import pallas as pl
from jax.experimental.pallas import tpu as pltpu
from jax.sharding import PartitionSpec as P

HEAD_DIM = 64
EPSILON = 1e-05
MASKED = -1e30
ROW_BLOCK = 256
CHUNKS = 2
LANES = 128
GELU_ROOT = 0.7978845608028654
GELU_CUBE = 0.044715

f32 = jnp.float32
bf16 = jnp.bfloat16


def dot_nn(a, b):
    return lax.dot_general(a, b, (((1,), (0,)), ((), ())), preferred_element_type=f32)


def dot_nt(a, b):
    return lax.dot_general(a, b, (((1,), (1,)), ((), ())), preferred_element_type=f32)


def call(kernel, grid, in_specs, out_specs, out_shape, flops, scratch=(), prefetch=0, name=None):
    spec = pltpu.PrefetchScalarGridSpec(
        num_scalar_prefetch=prefetch,
        grid=grid,
        in_specs=in_specs,
        out_specs=out_specs,
        scratch_shapes=list(scratch),
    )
    return pl.pallas_call(
        kernel,
        grid_spec=spec,
        out_shape=out_shape,
        compiler_params=pltpu.CompilerParams(
            dimension_semantics=("arbitrary",) * len(grid), vmem_limit_bytes=56 * 1024 * 1024
        ),
        cost_estimate=pl.CostEstimate(
            flops=int(flops), bytes_accessed=int(flops / 400), transcendentals=0
        ),
        name=name,
    )


def fixed(shape):
    return pl.BlockSpec(
        shape, lambda *_: (0,) * len(shape), pipeline_mode=pl.Buffered(buffer_count=1)
    )


def kept(shape):
    return pl.BlockSpec(shape, lambda *_: (0,) * len(shape))


def rows_of(height, width):
    return pl.BlockSpec((height, width), lambda i, *_: (i, 0))


def shape_of(shape, dtype):
    return jax.ShapeDtypeStruct(shape, dtype)


def normalized(values):
    average = jnp.mean(values, axis=1, keepdims=True)
    centered = values - average
    root = lax.rsqrt(jnp.mean(centered * centered, axis=1, keepdims=True) + EPSILON)
    return centered * root, root


def gelu_pair(v):
    square = v * v
    t = jnp.tanh(v * (GELU_ROOT + (GELU_ROOT * GELU_CUBE) * square))
    half = 0.5 + 0.5 * t
    slope = half + (v * (0.5 - 0.5 * (t * t))) * (
        GELU_ROOT + (3.0 * GELU_ROOT * GELU_CUBE) * square
    )
    return v * half, slope


def ln_qkv_kernel(x_ref, g_ref, b_ref, w_ref, first_ref, qkv_ref):
    @pl.when(pl.program_id(0) == 0)
    def _():
        def some_rows(i, carry):
            at = pl.ds(pl.multiple_of(i * LANES, LANES), LANES)
            n, _ = normalized(x_ref[at, :].astype(f32))
            first_ref[at, :] = (n * g_ref[...] + b_ref[...]).astype(bf16)
            return carry

        lax.fori_loop(0, x_ref.shape[0] // LANES, some_rows, 0)

    qkv_ref[...] = dot_nn(first_ref[...], w_ref[...]).astype(bf16)


def ln_qkv(tokens, gain, bias, weight):
    rows, d = tokens.shape
    width = weight.shape[1]
    block = 512
    return call(
        ln_qkv_kernel,
        (width // block,),
        [
            fixed((rows, d)),
            fixed((1, d)),
            fixed((1, d)),
            pl.BlockSpec((d, block), lambda i: (0, i)),
        ],
        [kept((rows, d)), pl.BlockSpec((rows, block), lambda i: (0, i))],
        [shape_of((rows, d), bf16), shape_of((rows, width), bf16)],
        2 * rows * d * width,
        name="ln_qkv",
    )(tokens, gain, bias, weight)


def diagonal_bias(bias_rows):
    size = bias_rows.shape[0]
    key_at = lax.broadcasted_iota(jnp.int32, (size, size), 0)
    query_at = lax.broadcasted_iota(jnp.int32, (size, size), 1)
    return jnp.where(
        key_at == query_at, 0.0, jnp.where(key_at < query_at, bias_rows, MASKED)
    )


def head_lanes(values, head):
    lane = lax.broadcasted_iota(jnp.int32, values.shape, 1)
    inside = (lane >= head * HEAD_DIM) & (lane < (head + 1) * HEAD_DIM)
    return jnp.where(inside, values, jnp.zeros_like(values))


def attend_kernel(bias_ref, q_ref, k_ref, v_ref, ctx_ref, ctx_t_ref, lse_ref):
    rows = q_ref.shape[0]
    v_t = v_ref[...].T
    for i in range(rows // ROW_BLOCK):
        low, high = i * ROW_BLOCK, (i + 1) * ROW_BLOCK
        edge = diagonal_bias(bias_ref[low:high, :])
        q = q_ref[low:high, :] * jnp.asarray(HEAD_DIM**-0.5, bf16)
        sides = []
        for head in range(2):
            q_head = head_lanes(q, head)
            inner = dot_nt(k_ref[low:high, :], q_head) + edge
            top = jnp.max(inner, axis=0, keepdims=True)
            if i:
                outer = dot_nt(k_ref[:low, :], q_head) + bias_ref[:low, :]
                top = jnp.maximum(top, jnp.max(outer, axis=0, keepdims=True))
            inner = jnp.exp(inner - top)
            total = jnp.sum(inner, axis=0, keepdims=True)
            v_head = v_t[head * HEAD_DIM : (head + 1) * HEAD_DIM, :]
            side = dot_nn(v_head[:, low:high], inner.astype(bf16))
            if i:
                outer = jnp.exp(outer - top)
                total = total + jnp.sum(outer, axis=0, keepdims=True)
                side = side + dot_nn(v_head[:, :low], outer.astype(bf16))
            sides.append(side / total)
            lse_ref[0, head : head + 1, low:high] = top + jnp.log(total)
        both = jnp.concatenate(sides, axis=0)
        ctx_t_ref[:, low:high] = both.astype(bf16)
        ctx_ref[low:high, :] = both.T.astype(bf16)


def attend(qkv, bias):
    rows, d = qkv.shape[0], qkv.shape[1] // 3
    pairs = d // LANES

    def third(n):
        return pl.BlockSpec((rows, LANES), lambda h: (0, n * pairs + h))

    return call(
        attend_kernel,
        (pairs,),
        [fixed((rows, 1)), third(0), third(1), third(2)],
        [
            third(0),
            pl.BlockSpec((LANES, rows), lambda h: (h, 0)),
            pl.BlockSpec((1, 8, rows), lambda h: (h, 0, 0)),
        ],
        [
            shape_of((rows, d), bf16),
            shape_of((d, rows), bf16),
            shape_of((pairs, 8, rows), f32),
        ],
        8 * rows * rows * d,
        name="attend",
    )(bias, qkv, qkv, qkv)


def attend_back_kernel(
    bias_ref, lse_ref, q_ref, k_ref, v_ref, do_ref, g_ref, g_t_ref, gk_acc, gv_acc
):
    rows = q_ref.shape[0]
    scale = HEAD_DIM**-0.5
    k_t = k_ref[...].T
    gk_acc[...] = jnp.zeros_like(gk_acc)
    gv_acc[...] = jnp.zeros_like(gv_acc)
    for i in range(rows // ROW_BLOCK):
        low, high = i * ROW_BLOCK, (i + 1) * ROW_BLOCK
        edge = diagonal_bias(bias_ref[low:high, :])
        q = q_ref[low:high, :] * jnp.asarray(scale, bf16)
        do = do_ref[low:high, :]
        sides = []
        for head in range(2):
            q_head = head_lanes(q, head)
            do_head = head_lanes(do, head)
            lse = lse_ref[0, head : head + 1, low:high]
            spans = [(low, high, edge)]
            if i:
                spans.append((0, low, bias_ref[:low, :]))
            probs, grads = [], []
            dots = 0.0
            for start, stop, bias in spans:
                p = jnp.exp(dot_nt(k_ref[start:stop, :], q_head) + bias - lse)
                gp = dot_nt(v_ref[start:stop, :], do_head)
                dots = dots + jnp.sum(p * gp, axis=0, keepdims=True)
                probs.append(p)
                grads.append(gp)
            side = 0.0
            k_head = k_t[head * HEAD_DIM : (head + 1) * HEAD_DIM, :]
            for (start, stop, _), p, gp in zip(spans, probs, grads):
                ds = (p * (gp - dots)).astype(bf16)
                gv_acc[start:stop, :] += dot_nn(p.astype(bf16), do_head)
                gk_acc[start:stop, :] += dot_nn(ds, q_head)
                side = side + dot_nn(k_head[:, start:stop], ds)
            sides.append(side * scale)
        both = jnp.concatenate(sides, axis=0)
        g_t_ref[0, :, low:high] = both.astype(bf16)
        g_ref[0, low:high, :] = both.T.astype(bf16)
    for n, acc in ((1, gk_acc), (2, gv_acc)):
        g_ref[n] = acc[...].astype(bf16)
        g_t_ref[n] = acc[...].T.astype(bf16)


def attend_back(qkv, bias, lse, grad_context):
    rows, d = grad_context.shape
    pairs = d // LANES

    def third(n):
        return pl.BlockSpec((rows, LANES), lambda h: (0, n * pairs + h))

    return call(
        attend_back_kernel,
        (pairs,),
        [
            fixed((rows, 1)),
            pl.BlockSpec((1, 8, rows), lambda h: (h, 0, 0)),
            third(0),
            third(1),
            third(2),
            third(0),
        ],
        [
            pl.BlockSpec((3, rows, LANES), lambda h: (0, 0, h)),
            pl.BlockSpec((3, LANES, rows), lambda h: (0, h, 0)),
        ],
        [shape_of((3, rows, d), bf16), shape_of((3, d, rows), bf16)],
        20 * rows * rows * d,
        scratch=[pltpu.VMEM((rows, LANES), f32), pltpu.VMEM((rows, LANES), f32)],
        name="attend_back",
    )(bias, lse, qkv, qkv, qkv, grad_context)


def after_kernel(
    rb, core_ref, x_ref, ctx_ref, cot_ref, w_ref, g_ref, b_ref, mix_ref,
    middle_ref, second_ref, second_t_ref, gdl_ref, gdl_t_ref, mixing_ref,
):
    d = x_ref.shape[1]
    middle = x_ref[...].astype(f32) + dot_nn(ctx_ref[...], w_ref[...])
    middle_ref[...] = middle
    n, _ = normalized(middle)
    second = (n * g_ref[...] + b_ref[...]).astype(bf16)
    second_ref[...] = second
    logits = dot_nn(second, mix_ref[...])
    gap = logits[:, 1:2] - logits[:, 0:1]
    first_share = 1.0 / (1.0 + jnp.exp(gap))
    other_share = 1.0 / (1.0 + jnp.exp(-gap))
    lane = lax.broadcasted_iota(jnp.int32, mixing_ref.shape, 1)
    mixing_ref[...] = jnp.where(lane == 0, first_share, other_share)
    gdl = (first_share * cot_ref[...].astype(f32)).astype(bf16)
    gdl_ref[...] = gdl
    core = core_ref[0]
    for values, target in ((second, second_t_ref), (gdl, gdl_t_ref)):
        turned = values.astype(f32).T.astype(bf16)
        for piece in range(d // rb):
            place = ((piece % 2) ^ core) * (d // (2 * rb)) + piece // 2
            target[pl.ds(pl.multiple_of(place * rb, rb), rb), :] = turned[
                piece * rb : (piece + 1) * rb, :
            ]


def after(core, tokens, context, cotangent, weight, gain, bias, mix_padded, rb):
    rows, d = tokens.shape
    block = rows_of(ROW_BLOCK, d)
    turned = pl.BlockSpec((d, ROW_BLOCK), lambda i, *_: (0, i))
    return call(
        functools.partial(after_kernel, rb),
        (rows // ROW_BLOCK,),
        [block, block, block, fixed((d, d)), fixed((1, d)), fixed((1, d)), fixed((d, LANES))],
        [block, block, turned, block, turned, rows_of(ROW_BLOCK, LANES)],
        [
            shape_of((rows, d), f32),
            shape_of((rows, d), bf16),
            shape_of((d, rows), bf16),
            shape_of((rows, d), bf16),
            shape_of((d, rows), bf16),
            shape_of((rows, LANES), f32),
        ],
        2 * rows * d * d,
        prefetch=1,
        name="after",
    )(core, tokens, context, cotangent, weight, gain, bias, mix_padded)


def dense_kernel(
    owner_ref, place_ref, second_ref, second_t_ref, gdl_ref, gdl_t_ref, up_ref, down_ref,
    out_ref, gsec_ref, up_keep_ref, up_send_ref, down_keep_ref, down_send_ref, hidden, gpre,
):
    rows = second_ref.shape[0]
    half = second_t_ref.shape[0] // 2

    @pl.when(pl.program_id(0) == 0)
    def _():
        out_ref[...] = jnp.zeros_like(out_ref)
        gsec_ref[...] = jnp.zeros_like(gsec_ref)

    for low in range(0, rows, ROW_BLOCK):
        at = slice(low, low + ROW_BLOCK)
        value, slope = gelu_pair(dot_nn(second_ref[at, :], up_ref[...]))
        h = value.astype(bf16)
        g = (dot_nt(gdl_ref[at, :], down_ref[...]) * slope).astype(bf16)
        hidden[at, :] = h
        gpre[at, :] = g
        out_ref[at, :] += dot_nn(h, down_ref[...])
        gsec_ref[at, :] += dot_nt(g, up_ref[...])
    up_keep_ref[0] = dot_nn(second_t_ref[:half, :], gpre[...]).astype(bf16)
    up_send_ref[0] = dot_nn(second_t_ref[half:, :], gpre[...]).astype(bf16)
    down_keep_ref[0] = dot_nn(gdl_t_ref[:half, :], hidden[...]).astype(bf16)
    down_send_ref[0] = dot_nn(gdl_t_ref[half:, :], hidden[...]).astype(bf16)


def dense(chunk, owners, places, second, second_t, gdl, gdl_t, up, down):
    rows, d = second.shape
    n = owners.shape[0]
    width = up.shape[1] // (n * CHUNKS)

    def piece(ordered):
        def at(t, owner, place):
            return (place[t] if ordered else t, 0, 0)

        return pl.BlockSpec((1, d // 2, width), at)

    return call(
        dense_kernel,
        (n,),
        [
            fixed((rows, d)),
            fixed((d, rows)),
            fixed((rows, d)),
            fixed((d, rows)),
            pl.BlockSpec((d, width), lambda t, owner, place: (0, owner[t] * CHUNKS + chunk)),
            pl.BlockSpec((width, d), lambda t, owner, place: (owner[t] * CHUNKS + chunk, 0)),
        ],
        [kept((rows, d)), kept((rows, d)), piece(False), piece(False), piece(True), piece(True)],
        [shape_of((rows, d), f32)] * 2 + [shape_of((n, d // 2, width), bf16)] * 4,
        12 * rows * d * n * width,
        scratch=[pltpu.VMEM((rows, width), bf16), pltpu.VMEM((rows, width), bf16)],
        prefetch=2,
        name="dense",
    )(owners, places, second, second_t, gdl, gdl_t, up, down)


def expert_kernel(
    experts, me_ref, arr_ref, cot_ref, gate_ref, up_ref, down_ref,
    hidden_ref, gpre_ref, sent_ref, gin_ref, garr_ref, gate_grad_ref,
    out_acc, gin_acc, logit_acc,
):
    rows = arr_ref.shape[0]
    step = rows // 3
    t = pl.program_id(0)
    lane = lax.broadcasted_iota(jnp.int32, (step, LANES), 1)

    def shares(logits):
        def softmax(inside):
            held = jnp.where(inside, logits, MASKED)
            raised = jnp.where(
                inside, jnp.exp(held - jnp.max(held, axis=1, keepdims=True)), 0.0
            )
            return raised / jnp.sum(raised, axis=1, keepdims=True)

        def pick(values, at):
            return jnp.sum(jnp.where(lane == at, values, 0.0), axis=1, keepdims=True)

        gates = softmax(lane < experts)
        mixing = softmax((lane >= experts) & (lane < experts + 2))
        return gates, pick(gates, me_ref[0]), pick(mixing, experts), pick(mixing, experts + 1)

    @pl.when(t == 0)
    def _():
        out_acc[...] = jnp.zeros_like(out_acc)
        gin_acc[...] = jnp.zeros_like(gin_acc)
        for low in range(0, rows, step):
            at = slice(low, low + step)
            logits = dot_nn(arr_ref[at, :], gate_ref[...])
            logit_acc[at, :] = logits
            _, chosen, _, mix1 = shares(logits)
            garr_ref[at, :] = ((chosen * mix1) * cot_ref[at, :].astype(f32)).astype(bf16)

    for low in range(0, rows, step):
        at = slice(low, low + step)
        value, slope = gelu_pair(dot_nn(arr_ref[at, :], up_ref[...]))
        h = value.astype(bf16)
        g = (dot_nt(garr_ref[at, :], down_ref[...]) * slope).astype(bf16)
        gpre_ref[at, :] = g
        out_acc[at, :] += dot_nn(h, down_ref[...])
        gin_acc[at, :] += dot_nt(g, up_ref[...])
        hidden_ref[at, :] = h

    @pl.when(t == pl.num_programs(0) - 1)
    def _():
        gate_grad = 0.0
        for low in range(0, rows, step):
            at = slice(low, low + step)
            gates, chosen, mix0, mix1 = shares(logit_acc[at, :])
            out = out_acc[at, :]
            sent_ref[at, :] = ((chosen * mix1) * out).astype(bf16)
            met = jnp.sum(cot_ref[at, :].astype(f32) * out, axis=1, keepdims=True)
            grad_chosen = mix1 * met
            swing = chosen * met * mix0 * mix1
            grad = gates * grad_chosen * (jnp.where(lane == me_ref[0], 1.0, 0.0) - chosen)
            grad = grad + jnp.where(lane == experts + 1, swing, 0.0)
            grad = grad - jnp.where(lane == experts, swing, 0.0)
            low_grad = grad.astype(bf16)
            gin_ref[at, :] = (gin_acc[at, :] + dot_nt(low_grad, gate_ref[...])).astype(bf16)
            gate_grad = gate_grad + dot_nn(grad.T.astype(bf16), arr_ref[at, :])
        gate_grad_ref[...] = gate_grad


def expert(me, arriving, cot, gate_padded, up, down, experts):
    rows, d = arriving.shape
    hidden = up.shape[1]
    width = 512
    columns = pl.BlockSpec((rows, width), lambda t, *_: (0, t))
    return call(
        functools.partial(expert_kernel, experts),
        (hidden // width,),
        [
            fixed((rows, d)),
            fixed((rows, d)),
            fixed((d, LANES)),
            pl.BlockSpec((d, width), lambda t, *_: (0, t)),
            pl.BlockSpec((width, d), lambda t, *_: (t, 0)),
        ],
        [columns, columns] + [kept((rows, d))] * 3 + [kept((LANES, d))],
        [shape_of((rows, hidden), bf16)] * 2
        + [shape_of((rows, d), bf16)] * 3
        + [shape_of((LANES, d), f32)],
        8 * rows * d * hidden,
        scratch=[
            pltpu.VMEM((rows, d), f32),
            pltpu.VMEM((rows, d), f32),
            pltpu.VMEM((rows, LANES), f32),
        ],
        prefetch=1,
        name="expert",
    )(me, arriving, cot, gate_padded, up, down)


def between_kernel(
    target_ref, gin_ref, gs0_ref, gs1_ref, do0_ref, do1_ref, middle_ref, mixing_ref, cot_ref,
    second_ref, mix_t_ref, g_ref, w_ref, gatt_ref, gctx_ref, sums_ref,
):
    @pl.when(pl.program_id(0) == 0)
    def _():
        sums_ref[...] = jnp.zeros_like(sums_ref)

    slots = gin_ref.shape[0]
    lane = lax.broadcasted_iota(jnp.int32, (ROW_BLOCK, slots), 1)
    pick = jnp.where(target_ref[...] == lane, 1.0, 0.0).astype(bf16)
    grad = gs0_ref[...] + gs1_ref[...] + dot_nn(pick, gin_ref[...])
    go = cot_ref[...].astype(f32)
    met = jnp.sum(go * (do0_ref[...] + do1_ref[...]), axis=1, keepdims=True)
    swing = met * mixing_ref[:, 0:1] * mixing_ref[:, 1:2]
    grad = grad + swing * (mix_t_ref[0:1, :] - mix_t_ref[1:2, :])
    n, root = normalized(middle_ref[...])
    sums_ref[0:1, :] += jnp.sum(grad * n, axis=0, keepdims=True)
    sums_ref[1:2, :] += jnp.sum(grad, axis=0, keepdims=True)
    sums_ref[2:3, :] += jnp.sum(second_ref[...].astype(f32) * swing, axis=0, keepdims=True)
    u = grad * g_ref[...]
    u_mean = jnp.mean(u, axis=1, keepdims=True)
    un_mean = jnp.mean(u * n, axis=1, keepdims=True)
    gatt = (go + root * (u - u_mean - n * un_mean)).astype(bf16)
    gatt_ref[...] = gatt
    gctx_ref[...] = dot_nt(gatt, w_ref[...]).astype(bf16)


def between(target, gin, gs, do, middle, mixing, cotangent, second, mix_t, gain, weight):
    rows, d = middle.shape
    slots = gin.shape[0]
    block = rows_of(ROW_BLOCK, d)
    return call(
        between_kernel,
        (rows // ROW_BLOCK,),
        [
            rows_of(ROW_BLOCK, 1), fixed((slots, d)), block, block, block, block, block,
            rows_of(ROW_BLOCK, LANES), block, block, fixed((2, d)), fixed((1, d)), fixed((d, d)),
        ],
        [block, block, kept((8, d))],
        [shape_of((rows, d), bf16), shape_of((rows, d), bf16), shape_of((8, d), f32)],
        2 * rows * d * (d + slots),
        name="between",
    )(
        target, gin, gs[0], gs[1], do[0], do[1], middle, mixing, cotangent, second, mix_t, gain,
        weight,
    )


def out_kernel(target_ref, back_ref, do0_ref, do1_ref, middle_ref, mixing_ref, out_ref):
    slots = back_ref.shape[0]
    lane = lax.broadcasted_iota(jnp.int32, (ROW_BLOCK, slots), 1)
    pick = jnp.where(target_ref[...] == lane, 1.0, 0.0).astype(bf16)
    mixed = mixing_ref[:, 0:1] * (do0_ref[...] + do1_ref[...]) + dot_nn(pick, back_ref[...])
    out_ref[...] = (middle_ref[...] + mixed).astype(bf16)


def outputs_of(target, back, do, middle, mixing):
    rows, d = middle.shape
    slots = back.shape[0]
    block = rows_of(ROW_BLOCK, d)
    return call(
        out_kernel,
        (rows // ROW_BLOCK,),
        [
            rows_of(ROW_BLOCK, 1), fixed((slots, d)), block, block, block,
            rows_of(ROW_BLOCK, LANES),
        ],
        block,
        shape_of((rows, d), bf16),
        2 * rows * d * slots,
        name="outputs",
    )(target, back, do[0], do[1], middle, mixing)


def first_back_kernel(g_ref, w_ref, x_ref, gatt_ref, gain_ref, gx_ref, sums_ref):
    d = x_ref.shape[1]

    @pl.when(pl.program_id(0) == 0)
    def _():
        sums_ref[...] = jnp.zeros_like(sums_ref)

    grad = dot_nt(g_ref[0], w_ref[:, :d])
    grad = grad + dot_nt(g_ref[1], w_ref[:, d : 2 * d])
    grad = grad + dot_nt(g_ref[2], w_ref[:, 2 * d :])
    n, root = normalized(x_ref[...].astype(f32))
    sums_ref[0:1, :] += jnp.sum(grad * n, axis=0, keepdims=True)
    sums_ref[1:2, :] += jnp.sum(grad, axis=0, keepdims=True)
    u = grad * gain_ref[...]
    u_mean = jnp.mean(u, axis=1, keepdims=True)
    un_mean = jnp.mean(u * n, axis=1, keepdims=True)
    gx_ref[...] = (gatt_ref[...].astype(f32) + root * (u - u_mean - n * un_mean)).astype(bf16)


def first_back(grad_qkv, weight, tokens, gatt, gain):
    rows, d = tokens.shape
    block = rows_of(ROW_BLOCK, d)
    return call(
        first_back_kernel,
        (rows // ROW_BLOCK,),
        [
            pl.BlockSpec((3, ROW_BLOCK, d), lambda i: (0, i, 0)),
            fixed((d, 3 * d)),
            block,
            block,
            fixed((1, d)),
        ],
        [block, kept((8, d))],
        [shape_of((rows, d), bf16), shape_of((8, d), f32)],
        6 * rows * d * d,
        name="first_back",
    )(grad_qkv, weight, tokens, gatt, gain)


def expert_grad_kernel(owner_ref, a_ref, b_ref, out_ref):
    out_ref[0] = dot_nn(a_ref[...], b_ref[...]).astype(bf16)


def up_grad(owners, a, b, n):
    d, rows = a.shape
    width = b.shape[1] // n
    m = owners.shape[0]
    return call(
        expert_grad_kernel,
        (m,),
        [fixed((d, rows)), pl.BlockSpec((rows, width), lambda t, owner: (0, owner[t]))],
        pl.BlockSpec((1, d, width), lambda t, owner: (t, 0, 0)),
        shape_of((m, d, width), bf16),
        2 * rows * d * width * m,
        prefetch=1,
        name="up_grad",
    )(owners, a, b)


def down_grad_kernel(owner_ref, a_ref, b_ref, out_ref):
    out_ref[0] = lax.dot_general(
        a_ref[...], b_ref[...], (((0,), (0,)), ((), ())), preferred_element_type=f32
    ).astype(bf16)


def down_grad(owners, a, b, n):
    rows, d = b.shape
    width = a.shape[1] // n
    m = owners.shape[0]
    return call(
        down_grad_kernel,
        (m,),
        [pl.BlockSpec((rows, width), lambda t, owner: (0, owner[t])), fixed((rows, d))],
        pl.BlockSpec((1, width, d), lambda t, owner: (t, 0, 0)),
        shape_of((m, width, d), bf16),
        2 * rows * d * width * m,
        prefetch=1,
        name="down_grad",
    )(owners, a, b)


def swap(values, axis, bit):
    n = lax.axis_size(axis)
    return lax.ppermute(values, axis, [(i, i ^ bit) for i in range(n)])


def plus(a, b):
    return (a.astype(f32) + b.astype(f32)).astype(bf16)


def halve(keep, send, axis, bits):
    summed = plus(keep, swap(send, axis, bits[0]))
    if len(bits) == 1:
        return summed
    m = summed.shape[0] // 2
    return halve(summed[:m], summed[m:], axis, bits[1:])


def halve_absolute(values, axis, bits, me):
    for bit in bits:
        m = values.shape[0] // 2
        axis_at = 0 if bits[0] >= bits[-1] else 1
        split = values.reshape(((2, m), (m, 2))[axis_at] + values.shape[1:])
        mine = (me // bit) % 2
        keep = lax.dynamic_index_in_dim(split, mine, axis_at, keepdims=False)
        send = lax.dynamic_index_in_dim(split, 1 - mine, axis_at, keepdims=False)
        values = plus(keep, swap(send, axis, bit))
    return values[0]


def reversed_bits(value, count):
    return sum(((value >> i) & 1) << (count - 1 - i) for i in range(count))


def shards(
    tokens, lengths, key_mask, routes, norm1_gain, norm1_bias, qkv_weight, out_weight,
    norm2_gain, norm2_bias, up_weight, down_weight, router_weight, mix_weight, expert_up,
    expert_down, cotangent,
):
    rows, d = tokens.shape
    groups, copies = lax.axis_size("ep"), lax.axis_size("dp")
    experts = expert_up.shape[0] * groups
    capacity = (5 * rows + 4 * experts - 1) // (4 * experts)
    slots = experts * capacity
    ep, dp = lax.axis_index("ep"), lax.axis_index("dp")
    core, level, levels = ep % 2, ep // 2, groups // 2
    count = copies.bit_length() - 1
    up_bits = [1 << i for i in reversed(range(count))]
    down_bits = [1 << i for i in range(count)]
    level_groups = [[2 * z + c for z in range(levels)] for c in range(2)]
    order = jnp.arange(copies, dtype=jnp.int32)
    back_order = jnp.array([reversed_bits(t, count) for t in range(copies)], jnp.int32)
    owners = dp.astype(jnp.int32) ^ order
    back_owners = dp.astype(jnp.int32) ^ back_order
    core_scalar = core.astype(jnp.int32).reshape(1)

    row_at = jnp.arange(rows, dtype=jnp.int32)
    live = row_at < lengths[0]
    flat_routes = routes[:, 0]
    routed = (flat_routes[:, None] == jnp.arange(experts)[None, :]) & live[:, None]
    ahead = dot_nn(
        (row_at[None, :] < row_at[:, None]).astype(bf16), routed.astype(bf16)
    )
    place = jnp.sum(jnp.where(routed, ahead, 0.0), axis=1).astype(jnp.int32)
    target = jnp.where(live, flat_routes * capacity + place, slots)
    target_column = target[:, None]
    pick = (jnp.arange(slots, dtype=jnp.int32)[:, None] == target[None, :]).astype(bf16)

    def exchange(values):
        return lax.all_to_all(
            values.reshape(groups, slots // groups, d), "ep", 0, 0, tiled=True
        ).reshape(slots, d)

    def dispatch(values):
        return exchange(dot_nn(pick, values).astype(bf16))

    cot_arriving = dispatch(cotangent)
    usable = live & (key_mask == 1)
    bias = jnp.where(usable, 0.0, MASKED).astype(f32)[:, None]
    first, qkv = ln_qkv(tokens, norm1_gain[None], norm1_bias[None], qkv_weight)
    context, context_t, lse = attend(qkv, bias)
    mix_padded = jnp.pad(mix_weight, ((0, 0), (0, LANES - 2)))
    gate_padded = jnp.pad(
        jnp.concatenate([router_weight, mix_weight], axis=1),
        ((0, 0), (0, LANES - 2 - experts)),
    )
    middle, second, second_t, gdl, gdl_t, mixing = after(
        core_scalar, tokens, context, cotangent, out_weight, norm2_gain[None], norm2_bias[None],
        mix_padded, d // groups,
    )
    arriving = dispatch(second)

    dense_parts = [
        dense(chunk, owners, back_order, second, second_t, gdl, gdl_t, up_weight, down_weight)
        for chunk in range(CHUNKS)
    ]
    dense_out = [part[0] for part in dense_parts]
    grad_second = [part[1] for part in dense_parts]
    up_pieces, down_pieces = [], []
    m = copies // 2
    for _, _, up_keep, up_send, down_keep, down_send in dense_parts:
        up_pair = plus(up_keep, swap(up_send, "ep", 1))
        down_pair = plus(down_keep, swap(down_send, "ep", 1))
        up_pieces.append(halve(up_pair[:m], up_pair[m:], "dp", up_bits)[0])
        down_pieces.append(halve(down_pair[:m], down_pair[m:], "dp", down_bits)[0])
    dense_square = jnp.stack(
        [jnp.concatenate(up_pieces, axis=1), jnp.concatenate(down_pieces, axis=1)]
    ).reshape(2, levels, d // groups, -1)
    dense_sum = lax.psum_scatter(
        dense_square.transpose(1, 0, 2, 3), "ep", scatter_dimension=0, tiled=True,
        axis_index_groups=level_groups,
    )[0].astype(f32)
    up_sum, down_sum = dense_sum[0], dense_sum[1].T

    hidden, gpre, sent, gin, garr, gate_grad = expert(
        ep.astype(jnp.int32).reshape(1), arriving, cot_arriving, gate_padded, expert_up[0],
        expert_down[0], experts,
    )
    grad_back = exchange(gin)
    expert_back = exchange(sent)
    arriving_t = arriving.T
    up_send = up_grad(owners[m:], arriving_t, gpre, copies)
    down_send = down_grad(back_owners[m:], hidden, garr, copies)
    up_keep = up_grad(owners[:m], arriving_t, gpre, copies)
    down_keep = down_grad(back_owners[:m], hidden, garr, copies)
    expert_up_sum = halve(up_keep, up_send, "dp", up_bits).astype(f32)
    expert_down_sum = halve(down_keep, down_send, "dp", down_bits).astype(f32)

    gatt, grad_context, sums2 = between(
        target_column, grad_back, grad_second, dense_out, middle, mixing, cotangent, second,
        mix_weight.T.astype(f32), norm2_gain[None], out_weight,
    )
    outputs = outputs_of(target_column, expert_back, dense_out, middle, mixing)

    def owned(values, me_dp):
        height = values.shape[0] // (copies * groups)
        split = values.reshape(copies, levels, 2, height, -1)
        keep = lax.dynamic_index_in_dim(split, core, 2, keepdims=False)
        send = lax.dynamic_index_in_dim(split, 1 - core, 2, keepdims=False)
        pair = plus(keep, swap(send, "ep", 1))
        half = pair.shape[-1] // 2
        left = halve_absolute(pair[..., :half], "dp", up_bits, me_dp)
        right = halve_absolute(pair[..., half:], "dp", down_bits, me_dp)
        whole = jnp.concatenate([left, right], axis=-1)
        return lax.psum_scatter(
            whole, "ep", scatter_dimension=0, tiled=True, axis_index_groups=level_groups
        )[0].astype(f32)

    out_sum = owned(dot_nn(context_t, gatt).astype(bf16), dp)
    grad_qkv, grad_qkv_t = attend_back(qkv, bias, lse, grad_context)
    grad_inputs, sums1 = first_back(grad_qkv, qkv_weight, tokens, gatt, norm1_gain[None])
    qkv_sum = owned(dot_nn(grad_qkv_t.reshape(3 * d, rows), first).astype(bf16), dp).T

    home_mix = jnp.concatenate(
        [jnp.zeros((experts, d), f32), sums2[2:3], -sums2[2:3]], axis=0
    )
    small = jnp.concatenate(
        [sums1[:2], sums2[:2], gate_grad[: experts + 2] + home_mix], axis=0
    )
    small = lax.psum_scatter(small.T, ("dp", "ep"), scatter_dimension=0, tiled=True)
    return (
        outputs, grad_inputs, small[:, 0], small[:, 1], qkv_sum, out_sum, small[:, 2],
        small[:, 3], up_sum, down_sum, small[:, 4 : 4 + experts], small[:, 4 + experts :],
        expert_up_sum, expert_down_sum,
    )


def solution(mesh):
    split = ("dp", "ep")
    return jax.shard_map(
        shards,
        mesh=mesh,
        in_specs=(
            P(split, None), P(split), P(split), P(split, None), P(), P(), P(), P(), P(), P(),
            P(), P(), P(), P(), P("ep", None, None), P("ep", None, None), P(split, None),
        ),
        out_specs=(
            P(split, None), P(split, None), P(split), P(split), P(None, split), P(split, None),
            P(split), P(split), P("ep", "dp"), P("dp", "ep"), P(split, None), P(split, None),
            P("ep", None, "dp"), P("ep", "dp", None),
        ),
        check_vma=False,
    )
```

time: 1120 us -> 656 us (0.59)
  matrix products: 339 us -> 18.5 us
  waiting for transfers between devices: 480 us -> 217 us
  Pallas kernels: 0 us -> 248 us
  blocking collectives: 60.5 us -> 0 us
  other arithmetic: 105 us -> 60.2 us
  local copies, waits for them, and re-layouts: 71.3 us -> 40.2 us
    dot_general x28 -> x5, matrix products: 334 us -> 18.5 us  [dot_nn(): lax.dot_general(a, b, (((1,), (0,)), ((), ())), preferred_element_type=f32)]
    pallas_call x0 -> x14, Pallas kernels: none -> 248 us  [the longest x2 57.4 us: dense(): call(dense_kernel, (n,), [fixed((rows, d)), fixed((d, rows)), fixed((rows...]
    reduce_scatter x5 -> x3, waiting for transfers between devices: 260 us -> 17.8 us  [the longest x2 17.8 us: owned(): lax.psum_scatter(whole, 'ep', scatter_dimension=0, tiled=True, axis_index...]
    all_to_all x7 -> x4, waiting for transfers between devices: 185 us -> 0.01 us  [exchange(): lax.all_to_all(values.reshape(groups, slots // groups, d), 'ep', 0, 0, ti...]
    unnamed x15 -> x5, waiting for transfers between devices: 35.4 us -> 121 us
    ppermute x0 -> x26, waiting for transfers between devices: none -> 77.8 us  [swap(): return lax.ppermute(values, axis, [(i, i ^ bit) for i in range(n)])]
    unnamed x1 -> x0, blocking collectives: 37.4 us -> none
    reduce_sum x11 -> x0, other arithmetic: 24 us -> none  [the longest x1 16.9 us: attend_forward(): row_total = jnp.sum(raised, axis=-1, keepdims=True)]
  transfers between devices with their start and end apart: 19 -> 34, of which waited for: 13 -> 10; matrix products, arithmetic and copies ran while one was open for 44% -> 16% of each run, Pallas kernels for 0% -> 38%
where the time goes in v1:
time: 656 us; the launch traced here: 645 us
  Pallas kernels  248 us (38%)
  waiting for transfers between devices  217 us (33%)
  other arithmetic  60.2 us (9%)
  starting transfers between devices  45.2 us (7%)
  local copies, waits for them, and re-layouts  40.2 us (6%)
  matrix products  18.5 us (3%)
  between operations  15.7 us (2%)
    unnamed x5, waiting for transfers between devices  121 us
    ppermute x26, waiting for transfers between devices, swap(): return lax.ppermute(values, axis, [(i, i ^ bit) for i in range(n)])  77.8 us
    pallas_call x2, Pallas kernels, dense(): call(dense_kernel, (n,), [fixed((rows, d)), fixed((d, rows)), fixed((rows...  57.4 us
    pallas_call x1, Pallas kernels, expert(): call(functools.partial(expert_kernel, experts), (hidden // width,), [fixe...  48.6 us
    convert_element_type x20, other arithmetic, plus(): return (a.astype(f32) + b.astype(f32)).astype(bf16)  36.2 us
    pallas_call x1, Pallas kernels, attend_back(): call(attend_back_kernel, (pairs,), [fixed((rows, 1)), pl.BlockSpec((1, 8,...  28.6 us
    ppermute x26, starting transfers between devices, swap(): return lax.ppermute(values, axis, [(i, i ^ bit) for i in range(n)])  22.5 us
    pallas_call x1, Pallas kernels, attend(): call(attend_kernel, (pairs,), [fixed((rows, 1)), third(0), third(1), thir...  22.5 us
  transfers between devices with their start and end apart: 34, of which 10 were waited for; matrix products, arithmetic and copies ran while one was open for 16% of the time, Pallas kernels for 38%

profile of v1, /device:TPU:0, one launch (start us, length us, event | category | flops | bytes accessed | tf_op | source)
XLA Modules:
  0.0 644.8 jit_solution(5746491279480112915)
XLA Ops:
  8.9 4.4 fusion.8
  13.3 6.5 %all-to-all-start.1 = ((bf16[8,120,1024]{2,1,0:T(8,128)(2,1)}), bf16[8,120,1024]{2,1,0:T(8,128)(2,1)S(1)}, u32[]{:S(2)}, u32[]{:S(2)}) async-start(bf16[8,120,1024]{2,1,0:T(8,128)(2,1)} %bitcast.139), calls=%async_computation.1 | async-start | bytes 3932160 | tf_op jit(solution)/shard_map/all_to_all | solution.py:696
  21.7 11.4 %ln_qkv.1 = (bf16[768,1024]{1,0:T(8,128)(2,1)}, bf16[768,3072]{1,0:T(8,128)(2,1)}) custom-call(bf16[768,1024]{1,0:T(8,128)(2,1)} %x_ref.5, f32[1,1024]{1,0:T(1,128)} %bitcast.150, f32[1,1024]{1,0:T(1,128)} %bitcast.149, bf16[1024,3072]{1,0:T(8,128)(2,1)} %w_ref.7), custom_call_target="tpu_custom_call" | custom-call | flops 4831838208 | bytes 12079595 | tf_op jit(solution)/shard_map/ln_qkv/pallas_call | solution.py:106
  33.1 22.5 %attend.1 = (bf16[768,1024]{1,0:T(8,128)(2,1)}, bf16[1024,768]{1,0:T(8,128)(2,1)}, f32[8,8,768]{2,1,0:T(8,128)}) custom-call(f32[768,1]{1,0:T(8,128)} %broadcast_in_dim.56.bias_ref, bf16[768,3072]{1,0:T(8,128)(2,1)} %get-tuple-element.50.q_ref.k_ref.v_ref, bf16[768,3072]{1,0:T(8,128)(2,1)} %get-tuple-element.50.q_ref.k_ref.v_ref, ...), custom_call_target="tpu_custom_call" | custom-call | flops 4831838208 | bytes 12079595 | tf_op jit(solution)/shard_map/attend/pallas_call | solution.py:174
  55.6 9.7 %after.1 = (f32[768,1024]{1,0:T(8,128)}, bf16[768,1024]{1,0:T(8,128)(2,1)}, bf16[1024,768]{1,0:T(8,128)(2,1)}, bf16[768,1024]{1,0:T(8,128)(2,1)}, bf16[1024,768]{1,0:T(8,128)(2,1)}, /*index=5*/f32[768,128]{1,0:T(8,128)}) custom-call(s32[1]{0:T(128)} %bitcast.2.core_ref, bf16[768,1024]{1,0:T(8,128)(2,1)} %x_ref.5, ...), custom_call_target="tpu_custom_call" | custom-call | flops 1610612736 | bytes 4026531 | tf_op jit(solution)/shard_map/after/pallas_call | solution.py:299
  65.9 29.4 %dense.3 = (f32[768,1024]{1,0:T(8,128)}, f32[768,1024]{1,0:T(8,128)}, bf16[4,512,512]{2,1,0:T(8,128)(2,1)}, bf16[4,512,512]{2,1,0:T(8,128)(2,1)}, bf16[4,512,512...) custom-call(s32[4]{0:T(128)} %get-tuple-element.146.owner_ref, s32[4]{0:T(128)} %constant.152.clone.place_ref, ...), custom_call_target="tpu_custom_call" | custom-call | flops 19327352832 | bytes 48318384 | tf_op jit(solution)/shard_map/dense/pallas_call | solution.py:356
  98.9 5.3 all-to-all-start
  104.2 28.0 %dense.2 = (f32[768,1024]{1,0:T(8,128)}, f32[768,1024]{1,0:T(8,128)}, bf16[4,512,512]{2,1,0:T(8,128)(2,1)}, bf16[4,512,512]{2,1,0:T(8,128)(2,1)}, bf16[4,512,512...) custom-call(s32[4]{0:T(128)} %get-tuple-element.146.owner_ref, s32[4]{0:T(128)} %constant.152.clone.place_ref, ...), custom_call_target="tpu_custom_call" | custom-call | flops 19327352832 | bytes 48318384 | tf_op jit(solution)/shard_map/dense/pallas_call | solution.py:356
  154.6 10.5 %collective-permute-done.14 = bf16[2,512,512]{2,1,0:T(8,128)(2,1)S(1)} collective-permute-done((bf16[2,512,512]{2,1,0:T(8,128)(2,1)S(1)}, bf16[2,512,512]{2,1,0:T(8,128)(2,1)S(1)}, u32[]{:S(2)}, u32[]{:S(2)}) %collective-permute-start.14) | collective-permute-done | bytes 1048608 | tf_op jit(solution)/shard_map/ppermute | solution.py:630
  167.8 48.6 %expert.1 = (bf16[960,4096]{1,0:T(8,128)(2,1)}, bf16[960,4096]{1,0:T(8,128)(2,1)}, bf16[960,1024]{1,0:T(8,128)(2,1)}, bf16[960,1024]{1,0:T(8,128)(2,1)}, bf16[960,1024]{1,0:T(8,128)(2,1)}, /*index=5*/f32[128,1024]{1,0:T(8,128)}) custom-call(s32[1]{0:T(128)} %bitcast.1.me_ref, bf16[960,1024]{1,0:T(8,128)(2,1)} %bitcast.8.arr_ref, ...), custom_call_target="tpu_custom_call" | custom-call | flops 32212254720 | bytes 80530640 | tf_op jit(solution)/shard_map/expert/pallas_call | solution.py:447
  216.4 5.3 all-to-all-start.3
  232.5 3.9 copy.86
  236.4 8.9 %up_grad.3 = bf16[2,1024,1024]{2,1,0:T(8,128)(2,1)} custom-call(s32[2]{0:T(128)} %get-tuple-element.145.owner_ref, bf16[1024,960]{1,0:T(8,128)(2,1)} %bitcast.125, bf16[960,4096]{1,0:T(8,128)(2,1)} %get-tuple-element.83.b_ref), custom_call_target="tpu_custom_call" | custom-call | flops 4026531840 | bytes 10066329 | tf_op jit(solution)/shard_map/up_grad/pallas_call | solution.py:594
  245.3 8.9 %up_grad.2 = bf16[2,1024,1024]{2,1,0:T(8,128)(2,1)} custom-call(s32[2]{0:T(128)} %get-tuple-element.144.owner_ref, bf16[1024,960]{1,0:T(8,128)(2,1)} %bitcast.126, bf16[960,4096]{1,0:T(8,128)(2,1)} %get-tuple-element.83.b_ref), custom_call_target="tpu_custom_call" | custom-call | flops 4026531840 | bytes 10066329 | tf_op jit(solution)/shard_map/up_grad/pallas_call | solution.py:594
  254.1 8.9 %down_grad.3 = bf16[2,1024,1024]{2,1,0:T(8,128)(2,1)} custom-call(s32[2]{0:T(128)} %get-tuple-element.143.owner_ref, bf16[960,4096]{1,0:T(8,128)(2,1)} %get-tuple-element.84.a_ref, bf16[960,1024]{1,0:T(8,128)(2,1)} %get-tuple-element.85.b_ref), custom_call_target="tpu_custom_call" | custom-call | flops 4026531840 | bytes 10066329 | tf_op jit(solution)/shard_map/down_grad/pallas_call | solution.py:616
  264.6 9.1 %down_grad.2 = bf16[2,1024,1024]{2,1,0:T(8,128)(2,1)} custom-call(s32[2]{0:T(128)} %get-tuple-element.142.owner_ref, bf16[960,4096]{1,0:T(8,128)(2,1)} %get-tuple-element.84.a_ref, bf16[960,1024]{1,0:T(8,128)(2,1)} %get-tuple-element.85.b_ref), custom_call_target="tpu_custom_call" | custom-call | flops 4026531840 | bytes 10066329 | tf_op jit(solution)/shard_map/down_grad/pallas_call | solution.py:616
  281.4 5.1 all-to-all-start.2
  286.5 14.1 %between.1 = (bf16[768,1024]{1,0:T(8,128)(2,1)}, bf16[768,1024]{1,0:T(8,128)(2,1)}, f32[8,1024]{1,0:T(8,128)}) custom-call(s32[768,1]{1,0:T(8,128)} %fusion.19.target_ref, bf16[960,1024]{1,0:T(8,128)(2,1)} %bitcast.16.gin_ref, f32[768,1024]{1,0:T(8,128)} %get-tuple-element.63.gs0_ref, f32[768,1024]{1,0:T(8,128)} %get-tuple-element.64.gs1_ref, ...), custom_call_target="tpu_custom_call" | custom-call | flops 3120562176 | bytes 7801405 | tf_op jit(solution)/shard_map/between/pallas_call | solution.py:504
  306.7 28.6 %attend_back.1 = (bf16[3,768,1024]{2,1,0:T(8,128)(2,1)}, bf16[3,1024,768]{2,1,0:T(8,128)(2,1)}) custom-call(f32[768,1]{1,0:T(8,128)} %broadcast_in_dim.56.bias_ref, f32[8,8,768]{2,1,0:T(8,128)} %get-tuple-element.61.lse_ref, bf16[768,3072]{1,0:T(8,128)(2,1)} %get-tuple-element.50.q_ref.k_ref.v_ref, bf16[768,3072]{1,0:T(8,128)(2,1)} %get-tuple-element.50.q_ref.k_ref.v_ref, ...), custom_call_target="tpu_custom_call" | custom-call | flops 12079595520 | bytes 30198988 | tf_op jit(solution)/shard_map/attend_back/pallas_call | solution.py:245
  335.3 7.6 %convolution_convert_fusion = bf16[3072,1024]{1,0:T(8,128)(2,1)S(1)} fusion(bf16[3072,768]{1,0:T(8,128)(2,1)} %bitcast.152, bf16[768,1024]{1,0:T(8,128)(2,1)S(1)} %copy-done.30), kind=kOutput, calls=%fused_computation.4 | convolution fusion | flops 4834983936 | bytes 12582912 | tf_op jit(solution)/shard_map/dot_general | solution.py:24
  347.5 11.6 %first_back.1 = (bf16[768,1024]{1,0:T(8,128)(2,1)}, f32[8,1024]{1,0:T(8,128)}) custom-call(bf16[3,768,1024]{2,1,0:T(8,128)(2,1)} %get-tuple-element.66.g_ref, bf16[1024,3072]{1,0:T(8,128)(2,1)} %w_ref.7, bf16[768,1024]{1,0:T(8,128)(2,1)} %x_ref.5, bf16[768,1024]{1,0:T(8,128)(2,1)} %get-tuple-element.67.gatt_ref, f32[1,1024]{1,0:T(1,128)} %bitcast.151), custom_call_target="tpu_custom_call" | custom-call | flops 4831838208 | bytes 12079595 | tf_op jit(solution)/shard_map/first_back/pallas_call | solution.py:569
  368.2 8.3 %outputs.1 = bf16[768,1024]{1,0:T(8,128)(2,1)} custom-call(s32[768,1]{1,0:T(8,128)} %fusion.19.target_ref, bf16[960,1024]{1,0:T(8,128)(2,1)} %bitcast.114, f32[768,1024]{1,0:T(8,128)} %get-tuple-element.57.do0_ref, f32[768,1024]{1,0:T(8,128)} %get-tuple-element.58.do1_ref, f32[768,1024]{1,0:T(8,128)} %get-tuple-element.59.middle_ref, ...), custom_call_target="tpu_custom_call" | custom-call | flops 1509949440 | bytes 3774873 | tf_op jit(solution)/shard_map/outputs/pallas_call | solution.py:533
  376.5 121.3 %reduce-scatter.13.cloned.1.call-done = f32[32,14]{1,0:T(8,128)} async-done(((f32[1024,14]{1,0:T(8,128)}), f32[32,14]{1,0:T(8,128)}) %reduce-scatter.13.cloned.1.call-update) | async-done | bytes 1808
  500.7 6.0 add_convert_fusion
  513.6 4.3 add_convert_fusion.1
  522.7 34.4 %collective-permute-done.6 = bf16[2,4,32,512]{3,2,1,0:T(8,128)(2,1)S(1)} collective-permute-done((bf16[2,4,32,512]{3,2,1,0:T(8,128)(2,1)S(1)}, bf16[2,4,32,512]{3,2,1,0:T(8,128)(2,1)S(1)}, u32[]{:S(2)}, u32[]{:S(2)}) %collective-permute-start.6) | collective-permute-done | bytes 262176 | tf_op jit(solution)/shard_map/ppermute | solution.py:630
  563.1 11.8 %collective-permute-done.8 = bf16[2,4,32,512]{3,2,1,0:T(8,128)(2,1)S(1)} collective-permute-done((bf16[2,4,32,512]{3,2,1,0:T(8,128)(2,1)S(1)}, bf16[2,4,32,512]{3,2,1,0:T(8,128)(2,1)S(1)}, u32[]{:S(2)}, u32[]{:S(2)}) %collective-permute-start.8) | collective-permute-done | bytes 262176 | tf_op jit(solution)/shard_map/ppermute | solution.py:630
  578.8 13.3 %collective-permute-done.3 = bf16[2,4,96,512]{3,2,1,0:T(8,128)(2,1)S(1)} collective-permute-done((bf16[2,4,96,512]{3,2,1,0:T(8,128)(2,1)S(1)}, bf16[2,4,96,512]{3,2,1,0:T(8,128)(2,1)S(1)}, u32[]{:S(2)}, u32[]{:S(2)}) %collective-permute-start.3) | collective-permute-done | bytes 786464 | tf_op jit(solution)/shard_map/ppermute | solution.py:630
  606.9 5.3 reduce-scatter.9.cloned.1.call-done
  613.7 5.3 fusion.5
  619.0 4.5 fusion.4
  623.5 12.6 %reduce-scatter.7.cloned.1.call-done = bf16[1,96,1024]{2,1,0:T(8,128)(2,1)} async-done(((bf16[4,96,1024]{2,1,0:T(8,128)(2,1)}), bf16[1,96,1024]{2,1,0:T(8,128)(2,1)}) %reduce-scatter.7.cloned.1.call-update) | async-done | bytes 196624 | tf_op jit(solution)/shard_map/reduce_scatter | solution.py:771
  (217 shorter events, 113.7 us)
Async XLA Ops:
  13.3 85.6 %all-to-all-start.1 = ((bf16[8,120,1024]{2,1,0:T(8,128)(2,1)}), bf16[8,120,1024]{2,1,0:T(8,128)(2,1)S(1)}, u32[]{:S(2)}, u32[]{:S(2)}) async-start(bf16[8,120,1024]{2,1,0:T(8,128)(2,1)} %bitcast.139), calls=%async_computation.1 | async-start | bytes 3932160 | tf_op jit(solution)/shard_map/all_to_all | solution.py:696
  95.3 41.6 %collective-permute-start.13 = (bf16[4,512,512]{2,1,0:T(8,128)(2,1)}, bf16[4,512,512]{2,1,0:T(8,128)(2,1)}, u32[]{:S(2)}, u32[]{:S(2)}) collective-permute-start(bf16[4,512,512]{2,1,0:T(8,128)(2,1)} %get-tuple-element.78), channel_id=1, source_target_pairs={{0,1},{1,0},{2,3},{3,2},{4,5},{5,4},{6,7},{7,6},{8,9},{9,8},{10,11... | collective-permute-start | bytes 6291464 | tf_op jit(solution)/shard_map/ppermute | solution.py:630
  95.8 44.8 %collective-permute-start.19 = (bf16[4,512,512]{2,1,0:T(8,128)(2,1)}, bf16[4,512,512]{2,1,0:T(8,128)(2,1)}, u32[]{:S(2)}, u32[]{:S(2)}) collective-permute-start(bf16[4,512,512]{2,1,0:T(8,128)(2,1)} %get-tuple-element.82), channel_id=1, source_target_pairs={{0,1},{1,0},{2,3},{3,2},{4,5},{5,4},{6,7},{7,6},{8,9},{9,8},{10,11... | collective-permute-start | bytes 6291464 | tf_op jit(solution)/shard_map/ppermute | solution.py:630
  98.9 68.9 %all-to-all-start = ((bf16[8,120,1024]{2,1,0:T(8,128)(2,1)}), bf16[8,120,1024]{2,1,0:T(8,128)(2,1)}, u32[]{:S(2)}, u32[]{:S(2)}) async-start(bf16[8,120,1024]{2,1,0:T(8,128)(2,1)} %bitcast.136), calls=%async_computation | async-start | bytes 3932160 | tf_op jit(solution)/shard_map/all_to_all | solution.py:696
  132.8 17.3 %collective-permute-start.16 = (bf16[4,512,512]{2,1,0:T(8,128)(2,1)}, bf16[4,512,512]{2,1,0:T(8,128)(2,1)}, u32[]{:S(2)}, u32[]{:S(2)}) collective-permute-start(bf16[4,512,512]{2,1,0:T(8,128)(2,1)} %get-tuple-element.80), channel_id=1, source_target_pairs={{0,1},{1,0},{2,3},{3,2},{4,5},{5,4},{6,7},{7,6},{8,9},{9,8},{10,11... | collective-permute-start | bytes 6291464 | tf_op jit(solution)/shard_map/ppermute | solution.py:630
  139.1 26.0 %collective-permute-start.14 = (bf16[2,512,512]{2,1,0:T(8,128)(2,1)S(1)}, bf16[2,512,512]{2,1,0:T(8,128)(2,1)S(1)}, u32[]{:S(2)}, u32[]{:S(2)}) collective-permute-start(bf16[2,512,512]{2,1,0:T(8,128)(2,1)S(1)} %slice.176), channel_id=1, source_target_pairs={{0,16},{8,24},{16,0},{24,8},{1,17},{9,25},{17,1},{25,9},{2,18},{10... | collective-permute-start | bytes 3145736 | tf_op jit(solution)/shard_map/ppermute | solution.py:630
  143.9 77.8 %collective-permute-start.20 = (bf16[2,512,512]{2,1,0:T(8,128)(2,1)}, bf16[2,512,512]{2,1,0:T(8,128)(2,1)}, u32[]{:S(2)}, u32[]{:S(2)}) collective-permute-start(bf16[2,512,512]{2,1,0:T(8,128)(2,1)} %slice.184), channel_id=1, source_target_pairs={{0,8},{8,0},{16,24},{24,16},{1,9},{9,1},{17,25},{25,17},{2,10},{10... | collective-permute-start | bytes 3145736 | tf_op jit(solution)/shard_map/ppermute | solution.py:630
  148.7 78.0 %collective-permute-start.11 = (bf16[2,512,512]{2,1,0:T(8,128)(2,1)}, bf16[2,512,512]{2,1,0:T(8,128)(2,1)}, u32[]{:S(2)}, u32[]{:S(2)}) collective-permute-start(bf16[2,512,512]{2,1,0:T(8,128)(2,1)} %slice.172), channel_id=1, source_target_pairs={{0,16},{8,24},{16,0},{24,8},{1,17},{9,25},{17,1},{25,9},{2,18},{10... | collective-permute-start | bytes 3145736 | tf_op jit(solution)/shard_map/ppermute | solution.py:630
  153.7 75.8 %collective-permute-start.17 = (bf16[2,512,512]{2,1,0:T(8,128)(2,1)}, bf16[2,512,512]{2,1,0:T(8,128)(2,1)}, u32[]{:S(2)}, u32[]{:S(2)}) collective-permute-start(bf16[2,512,512]{2,1,0:T(8,128)(2,1)} %slice.180), channel_id=1, source_target_pairs={{0,8},{8,0},{16,24},{24,16},{1,9},{9,1},{17,25},{25,17},{2,10},{10... | collective-permute-start | bytes 3145736 | tf_op jit(solution)/shard_map/ppermute | solution.py:630
  166.3 107.4 %collective-permute-start.15 = (bf16[1,512,512]{2,1,0:T(8,128)(2,1)}, bf16[1,512,512]{2,1,0:T(8,128)(2,1)}, u32[]{:S(2)}, u32[]{:S(2)}) collective-permute-start(bf16[1,512,512]{2,1,0:T(8,128)(2,1)} %slice.178), channel_id=1, source_target_pairs={{0,8},{8,0},{16,24},{24,16},{1,9},{9,1},{17,25},{25,17},{2,10},{10... | collective-permute-start | bytes 1572872 | tf_op jit(solution)/shard_map/ppermute | solution.py:630
  216.4 65.0 %all-to-all-start.3 = ((bf16[8,120,1024]{2,1,0:T(8,128)(2,1)}), bf16[8,120,1024]{2,1,0:T(8,128)(2,1)}, u32[]{:S(2)}, u32[]{:S(2)}) async-start(bf16[8,120,1024]{2,1,0:T(8,128)(2,1)} %bitcast.138), calls=%async_computation.3 | async-start | bytes 3932160 | tf_op jit(solution)/shard_map/all_to_all | solution.py:696
  225.2 51.9 %collective-permute-start.21 = (bf16[1,512,512]{2,1,0:T(8,128)(2,1)}, bf16[1,512,512]{2,1,0:T(8,128)(2,1)}, u32[]{:S(2)}, u32[]{:S(2)}) collective-permute-start(bf16[1,512,512]{2,1,0:T(8,128)(2,1)} %slice.186), channel_id=1, source_target_pairs={{0,16},{8,24},{16,0},{24,8},{1,17},{9,25},{17,1},{25,9},{2,18},{10... | collective-permute-start | bytes 1572872 | tf_op jit(solution)/shard_map/ppermute | solution.py:630
  229.0 49.2 %collective-permute-start.12 = (bf16[1,512,512]{2,1,0:T(8,128)(2,1)}, bf16[1,512,512]{2,1,0:T(8,128)(2,1)}, u32[]{:S(2)}, u32[]{:S(2)}) collective-permute-start(bf16[1,512,512]{2,1,0:T(8,128)(2,1)} %slice.174), channel_id=1, source_target_pairs={{0,8},{8,0},{16,24},{24,16},{1,9},{9,1},{17,25},{25,17},{2,10},{10... | collective-permute-start | bytes 1572872 | tf_op jit(solution)/shard_map/ppermute | solution.py:630
  231.9 47.5 %collective-permute-start.18 = (bf16[1,512,512]{2,1,0:T(8,128)(2,1)}, bf16[1,512,512]{2,1,0:T(8,128)(2,1)}, u32[]{:S(2)}, u32[]{:S(2)}) collective-permute-start(bf16[1,512,512]{2,1,0:T(8,128)(2,1)} %slice.182), channel_id=1, source_target_pairs={{0,16},{8,24},{16,0},{24,8},{1,17},{9,25},{17,1},{25,9},{2,18},{10... | collective-permute-start | bytes 1572872 | tf_op jit(solution)/shard_map/ppermute | solution.py:630
  263.0 237.7 %collective-permute-start.24 = (bf16[2,1024,1024]{2,1,0:T(8,128)(2,1)}, bf16[2,1024,1024]{2,1,0:T(8,128)(2,1)}, u32[]{:S(2)}, u32[]{:S(2)}) collective-permute-start(bf16[2,1024,1024]{2,1,0:T(8,128)(2,1)} %down_grad.3), channel_id=1, source_target_pairs={{0,8},{8,0},{16,24},{24,16},{1,9},{9,1},{17,25},{25,17},{2,10},{10... | collective-permute-start | bytes 12582920 | tf_op jit(solution)/shard_map/ppermute | solution.py:630
  273.7 239.9 %collective-permute-start.22 = (bf16[2,1024,1024]{2,1,0:T(8,128)(2,1)}, bf16[2,1024,1024]{2,1,0:T(8,128)(2,1)}, u32[]{:S(2)}, u32[]{:S(2)}) collective-permute-start(bf16[2,1024,1024]{2,1,0:T(8,128)(2,1)} %up_grad.3), channel_id=1, source_target_pairs={{0,16},{8,24},{16,0},{24,8},{1,17},{9,25},{17,1},{25,9},{2,18},{10... | collective-permute-start | bytes 12582920 | tf_op jit(solution)/shard_map/ppermute | solution.py:630
  281.4 85.5 %all-to-all-start.2 = ((bf16[8,120,1024]{2,1,0:T(8,128)(2,1)}), bf16[8,120,1024]{2,1,0:T(8,128)(2,1)S(1)}, u32[]{:S(2)}, u32[]{:S(2)}) async-start(bf16[8,120,1024]{2,1,0:T(8,128)(2,1)} %bitcast.137), calls=%async_computation.2 | async-start | bytes 3932160 | tf_op jit(solution)/shard_map/all_to_all | solution.py:696
  286.5 211.3 %reduce-scatter.13.cloned.1.call-start = ((), (), s32[]{:S(2)}) async-start(), calls=%async_computation.11 | async-start | bytes 540672
  306.3 203.5 %collective-permute-start.5 = (bf16[4,4,32,1024]{3,2,1,0:T(8,128)(2,1)}, bf16[4,4,32,1024]{3,2,1,0:T(8,128)(2,1)}, u32[]{:S(2)}, u32[]{:S(2)}) collective-permute-start(bf16[4,4,32,1024]{3,2,1,0:T(8,128)(2,1)} %dynamic-slice_bitcast_fusion.1), channel_id=1, source_target_pairs={{0,1},{1,0},{2,3},{3,2},{4,5},{5,4},{6,7},{7,6},{8,9},{9,8},{10,11... | collective-permute-start | bytes 3145736 | tf_op jit(solution)/shard_map/ppermute | solution.py:630
  346.7 210.5 %collective-permute-start = (bf16[4,4,96,1024]{3,2,1,0:T(8,128)(2,1)}, bf16[4,4,96,1024]{3,2,1,0:T(8,128)(2,1)}, u32[]{:S(2)}, u32[]{:S(2)}) collective-permute-start(bf16[4,4,96,1024]{3,2,1,0:T(8,128)(2,1)} %dynamic-slice_bitcast_fusion), channel_id=1, source_target_pairs={{0,1},{1,0},{2,3},{3,2},{4,5},{5,4},{6,7},{7,6},{8,9},{9,8},{10,11... | collective-permute-start | bytes 9437192 | tf_op jit(solution)/shard_map/ppermute | solution.py:630
  364.0 239.8 %reduce-scatter.11.cloned.1.call-start = ((), (), s32[]{:S(2)}) async-start(), calls=%async_computation.10 | async-start | bytes 2621440 | tf_op jit(solution)/shard_map/reduce_scatter | solution.py:735
  366.9 245.3 %reduce-scatter.9.cloned.1.call-start = ((), (), s32[]{:S(2)}) async-start(), calls=%async_computation.9 | async-start | bytes 327680 | tf_op jit(solution)/shard_map/reduce_scatter | solution.py:771
  509.5 104.2 %collective-permute-start.25 = (bf16[1,1024,1024]{2,1,0:T(8,128)(2,1)}, bf16[1,1024,1024]{2,1,0:T(8,128)(2,1)}, u32[]{:S(2)}, u32[]{:S(2)}) collective-permute-start(bf16[1,1024,1024]{2,1,0:T(8,128)(2,1)} %slice.194), channel_id=1, source_target_pairs={{0,16},{8,24},{16,0},{24,8},{1,17},{9,25},{17,1},{25,9},{2,18},{10... | collective-permute-start | bytes 6291464 | tf_op jit(solution)/shard_map/ppermute | solution.py:630
  511.8 45.3 %collective-permute-start.6 = (bf16[2,4,32,512]{3,2,1,0:T(8,128)(2,1)S(1)}, bf16[2,4,32,512]{3,2,1,0:T(8,128)(2,1)S(1)}, u32[]{:S(2)}, u32[]{:S(2)}) collective-permute-start(bf16[2,4,32,512]{3,2,1,0:T(8,128)(2,1)S(1)} %dynamic-slice_bitcast_fusion.5), channel_id=1, source_target_pairs={{0,16},{8,24},{16,0},{24,8},{1,17},{9,25},{17,1},{25,9},{2,18},{10... | collective-permute-start | bytes 786440 | tf_op jit(solution)/shard_map/ppermute | solution.py:630
  520.6 98.4 %collective-permute-start.23 = (bf16[1,1024,1024]{2,1,0:T(8,128)(2,1)}, bf16[1,1024,1024]{2,1,0:T(8,128)(2,1)}, u32[]{:S(2)}, u32[]{:S(2)}) collective-permute-start(bf16[1,1024,1024]{2,1,0:T(8,128)(2,1)} %slice.192), channel_id=1, source_target_pairs={{0,8},{8,0},{16,24},{24,16},{1,9},{9,1},{17,25},{25,17},{2,10},{10... | collective-permute-start | bytes 6291464 | tf_op jit(solution)/shard_map/ppermute | solution.py:630
  520.6 54.3 %collective-permute-start.8 = (bf16[2,4,32,512]{3,2,1,0:T(8,128)(2,1)S(1)}, bf16[2,4,32,512]{3,2,1,0:T(8,128)(2,1)S(1)}, u32[]{:S(2)}, u32[]{:S(2)}) collective-permute-start(bf16[2,4,32,512]{3,2,1,0:T(8,128)(2,1)S(1)} %dynamic-slice_bitcast_fusion.4), channel_id=1, source_target_pairs={{0,8},{8,0},{16,24},{24,16},{1,9},{9,1},{17,25},{25,17},{2,10},{10... | collective-permute-start | bytes 786440 | tf_op jit(solution)/shard_map/ppermute | solution.py:630
  561.1 17.3 %collective-permute-start.1 = (bf16[2,4,96,512]{3,2,1,0:T(8,128)(2,1)S(1)}, bf16[2,4,96,512]{3,2,1,0:T(8,128)(2,1)S(1)}, u32[]{:S(2)}, u32[]{:S(2)}) collective-permute-start(bf16[2,4,96,512]{3,2,1,0:T(8,128)(2,1)S(1)} %dynamic-slice_bitcast_fusion.3), channel_id=1, source_target_pairs={{0,16},{8,24},{16,0},{24,8},{1,17},{9,25},{17,1},{25,9},{2,18},{10... | collective-permute-start | bytes 2359304 | tf_op jit(solution)/shard_map/ppermute | solution.py:630
  562.9 14.8 %collective-permute-start.7 = (bf16[1,4,32,512]{3,2,1,0:T(8,128)(2,1)S(1)}, bf16[1,4,32,512]{3,2,1,0:T(8,128)(2,1)S(1)}, u32[]{:S(2)}, u32[]{:S(2)}) collective-permute-start(bf16[1,4,32,512]{3,2,1,0:T(8,128)(2,1)S(1)} %constant_dynamic-slice_fusion.1), channel_id=1, source_target_pairs={{0,8},{8,0},{16,24},{24,16},{1,9},{9,1},{17,25},{25,17},{2,10},{10... | collective-permute-start | bytes 393224 | tf_op jit(solution)/shard_map/ppermute | solution.py:630
  574.9 17.3 %collective-permute-start.3 = (bf16[2,4,96,512]{3,2,1,0:T(8,128)(2,1)S(1)}, bf16[2,4,96,512]{3,2,1,0:T(8,128)(2,1)S(1)}, u32[]{:S(2)}, u32[]{:S(2)}) collective-permute-start(bf16[2,4,96,512]{3,2,1,0:T(8,128)(2,1)S(1)} %dynamic-slice_bitcast_fusion.2), channel_id=1, source_target_pairs={{0,8},{8,0},{16,24},{24,16},{1,9},{9,1},{17,25},{25,17},{2,10},{10... | collective-permute-start | bytes 2359304 | tf_op jit(solution)/shard_map/ppermute | solution.py:630
  577.7 16.4 %collective-permute-start.9 = (bf16[1,4,32,512]{3,2,1,0:T(8,128)(2,1)S(1)}, bf16[1,4,32,512]{3,2,1,0:T(8,128)(2,1)S(1)}, u32[]{:S(2)}, u32[]{:S(2)}) collective-permute-start(bf16[1,4,32,512]{3,2,1,0:T(8,128)(2,1)S(1)} %constant_dynamic-slice_fusion), channel_id=1, source_target_pairs={{0,16},{8,24},{16,0},{24,8},{1,17},{9,25},{17,1},{25,9},{2,18},{10... | collective-permute-start | bytes 393224 | tf_op jit(solution)/shard_map/ppermute | solution.py:630
  578.7 17.6 %collective-permute-start.2 = (bf16[1,4,96,512]{3,2,1,0:T(8,128)(2,1)S(1)}, bf16[1,4,96,512]{3,2,1,0:T(8,128)(2,1)S(1)}, u32[]{:S(2)}, u32[]{:S(2)}) collective-permute-start(bf16[1,4,96,512]{3,2,1,0:T(8,128)(2,1)S(1)} %constant_dynamic-slice_fusion.3), channel_id=1, source_target_pairs={{0,8},{8,0},{16,24},{24,16},{1,9},{9,1},{17,25},{25,17},{2,10},{10... | collective-permute-start | bytes 1179656 | tf_op jit(solution)/shard_map/ppermute | solution.py:630
  594.9 41.2 %reduce-scatter.7.cloned.1.call-start = ((), (), s32[]{:S(2)}) async-start(), calls=%async_computation.8 | async-start | bytes 983040 | tf_op jit(solution)/shard_map/reduce_scatter | solution.py:771
  (35 other events, 405.2 us)
Sparse Core Ops, SparseCore 0:
  364.2 133.5 reduce-scatter.12
  500.2 40.1 reduce-scatter.10
  595.0 17.1 reduce-scatter.8
  614.4 21.5 reduce-scatter.6

commit v2 on v1

v2 whole, which is shorter than its diff:
```python
import functools

import jax
import jax.numpy as jnp
from jax import lax
from jax.experimental import pallas as pl
from jax.experimental.pallas import tpu as pltpu
from jax.sharding import PartitionSpec as P

HEAD_DIM = 64
EPSILON = 1e-05
MASKED = -1e30
ROW_BLOCK = 256
CHUNKS = 2
WEIGHT = 0.01
LANES = 128
GELU_ROOT = 0.7978845608028654
GELU_CUBE = 0.044715

f32 = jnp.float32
bf16 = jnp.bfloat16


def dot_nn(a, b):
    return lax.dot_general(a, b, (((1,), (0,)), ((), ())), preferred_element_type=f32)


def dot_nt(a, b):
    return lax.dot_general(a, b, (((1,), (1,)), ((), ())), preferred_element_type=f32)


class Line:
    last = None
    others = ()

    @classmethod
    def run(cls, function, *values):
        result = function(*values)
        cls.last = jax.tree.leaves(result)[0]
        return result


def call(kernel, grid, in_specs, out_specs, out_shape, micros, scratch=(), prefetch=0, name=None):
    def apply(*operands):
        specs, count, ordered = list(in_specs), len(operands), kernel
        if Line.last is not None:
            unread = (Line.last,) + Line.others
            Line.others = ()
            specs += [pl.BlockSpec(memory_space=pl.ANY)] * len(unread)
            operands += unread

            def ordered(*refs):
                kernel(*refs[:count], *refs[count + len(unread) :])

        return pl.pallas_call(
            ordered,
            grid_spec=pltpu.PrefetchScalarGridSpec(
                num_scalar_prefetch=prefetch,
                grid=grid,
                in_specs=specs,
                out_specs=out_specs,
                scratch_shapes=list(scratch),
            ),
            out_shape=out_shape,
            compiler_params=pltpu.CompilerParams(
                dimension_semantics=("arbitrary",) * len(grid), vmem_limit_bytes=56 * 1024 * 1024
            ),
            cost_estimate=pl.CostEstimate(
                flops=int(micros * WEIGHT * 1.15e9),
                bytes_accessed=int(micros * WEIGHT * 3e6),
                transcendentals=0,
            ),
            name=name,
        )(*operands)

    return apply


def fixed(shape):
    return pl.BlockSpec(
        shape, lambda *_: (0,) * len(shape), pipeline_mode=pl.Buffered(buffer_count=1)
    )


def kept(shape):
    return pl.BlockSpec(shape, lambda *_: (0,) * len(shape))


def rows_of(height, width):
    return pl.BlockSpec((height, width), lambda i, *_: (i, 0))


def shape_of(shape, dtype):
    return jax.ShapeDtypeStruct(shape, dtype)


def normalized(values):
    average = jnp.mean(values, axis=1, keepdims=True)
    centered = values - average
    root = lax.rsqrt(jnp.mean(centered * centered, axis=1, keepdims=True) + EPSILON)
    return centered * root, root


def gelu_pair(v):
    square = v * v
    t = jnp.tanh(v * (GELU_ROOT + (GELU_ROOT * GELU_CUBE) * square))
    half = 0.5 + 0.5 * t
    slope = half + (v * (0.5 - 0.5 * (t * t))) * (
        GELU_ROOT + (3.0 * GELU_ROOT * GELU_CUBE) * square
    )
    return v * half, slope


def ln_qkv_kernel(x_ref, g_ref, b_ref, w_ref, first_ref, qkv_ref):
    @pl.when(pl.program_id(0) == 0)
    def _():
        def some_rows(i, carry):
            at = pl.ds(pl.multiple_of(i * LANES, LANES), LANES)
            n, _ = normalized(x_ref[at, :].astype(f32))
            first_ref[at, :] = (n * g_ref[...] + b_ref[...]).astype(bf16)
            return carry

        lax.fori_loop(0, x_ref.shape[0] // LANES, some_rows, 0)

    qkv_ref[...] = dot_nn(first_ref[...], w_ref[...]).astype(bf16)


def ln_qkv(tokens, gain, bias, weight):
    rows, d = tokens.shape
    width = weight.shape[1]
    block = 512
    return call(
        ln_qkv_kernel,
        (width // block,),
        [
            fixed((rows, d)),
            fixed((1, d)),
            fixed((1, d)),
            pl.BlockSpec((d, block), lambda i: (0, i)),
        ],
        [kept((rows, d)), pl.BlockSpec((rows, block), lambda i: (0, i))],
        [shape_of((rows, d), bf16), shape_of((rows, width), bf16)],
        micros=11,
        name="ln_qkv",
    )(tokens, gain, bias, weight)


def diagonal_bias(bias_rows):
    size = bias_rows.shape[0]
    key_at = lax.broadcasted_iota(jnp.int32, (size, size), 0)
    query_at = lax.broadcasted_iota(jnp.int32, (size, size), 1)
    return jnp.where(
        key_at == query_at, 0.0, jnp.where(key_at < query_at, bias_rows, MASKED)
    )


def head_lanes(values, head):
    lane = lax.broadcasted_iota(jnp.int32, values.shape, 1)
    inside = (lane >= head * HEAD_DIM) & (lane < (head + 1) * HEAD_DIM)
    return jnp.where(inside, values, jnp.zeros_like(values))


def attend_kernel(bias_ref, q_ref, k_ref, v_ref, ctx_ref, ctx_t_ref, lse_ref):
    rows = q_ref.shape[0]
    v_t = v_ref[...].T
    for i in range(rows // ROW_BLOCK):
        low, high = i * ROW_BLOCK, (i + 1) * ROW_BLOCK
        edge = diagonal_bias(bias_ref[low:high, :])
        q = q_ref[low:high, :] * jnp.asarray(HEAD_DIM**-0.5, bf16)
        sides = []
        for head in range(2):
            q_head = head_lanes(q, head)
            inner = dot_nt(k_ref[low:high, :], q_head) + edge
            top = jnp.max(inner, axis=0, keepdims=True)
            if i:
                outer = dot_nt(k_ref[:low, :], q_head) + bias_ref[:low, :]
                top = jnp.maximum(top, jnp.max(outer, axis=0, keepdims=True))
            inner = jnp.exp(inner - top)
            total = jnp.sum(inner, axis=0, keepdims=True)
            v_head = v_t[head * HEAD_DIM : (head + 1) * HEAD_DIM, :]
            side = dot_nn(v_head[:, low:high], inner.astype(bf16))
            if i:
                outer = jnp.exp(outer - top)
                total = total + jnp.sum(outer, axis=0, keepdims=True)
                side = side + dot_nn(v_head[:, :low], outer.astype(bf16))
            sides.append(side / total)
            lse_ref[0, head : head + 1, low:high] = top + jnp.log(total)
        both = jnp.concatenate(sides, axis=0)
        ctx_t_ref[:, low:high] = both.astype(bf16)
        ctx_ref[low:high, :] = both.T.astype(bf16)


def attend(qkv, bias):
    rows, d = qkv.shape[0], qkv.shape[1] // 3
    pairs = d // LANES

    def third(n):
        return pl.BlockSpec((rows, LANES), lambda h: (0, n * pairs + h))

    return call(
        attend_kernel,
        (pairs,),
        [fixed((rows, 1)), third(0), third(1), third(2)],
        [
            third(0),
            pl.BlockSpec((LANES, rows), lambda h: (h, 0)),
            pl.BlockSpec((1, 8, rows), lambda h: (h, 0, 0)),
        ],
        [
            shape_of((rows, d), bf16),
            shape_of((d, rows), bf16),
            shape_of((pairs, 8, rows), f32),
        ],
        micros=22,
        name="attend",
    )(bias, qkv, qkv, qkv)


def attend_back_kernel(
    bias_ref, lse_ref, q_ref, k_ref, v_ref, do_ref, g_ref, g_t_ref, gk_acc, gv_acc
):
    rows = q_ref.shape[0]
    scale = HEAD_DIM**-0.5
    k_t = k_ref[...].T
    gk_acc[...] = jnp.zeros_like(gk_acc)
    gv_acc[...] = jnp.zeros_like(gv_acc)
    for i in range(rows // ROW_BLOCK):
        low, high = i * ROW_BLOCK, (i + 1) * ROW_BLOCK
        edge = diagonal_bias(bias_ref[low:high, :])
        q = q_ref[low:high, :] * jnp.asarray(scale, bf16)
        do = do_ref[low:high, :]
        sides = []
        for head in range(2):
            q_head = head_lanes(q, head)
            do_head = head_lanes(do, head)
            lse = lse_ref[0, head : head + 1, low:high]
            spans = [(low, high, edge)]
            if i:
                spans.append((0, low, bias_ref[:low, :]))
            probs, grads = [], []
            dots = 0.0
            for start, stop, bias in spans:
                p = jnp.exp(dot_nt(k_ref[start:stop, :], q_head) + bias - lse)
                gp = dot_nt(v_ref[start:stop, :], do_head)
                dots = dots + jnp.sum(p * gp, axis=0, keepdims=True)
                probs.append(p)
                grads.append(gp)
            side = 0.0
            k_head = k_t[head * HEAD_DIM : (head + 1) * HEAD_DIM, :]
            for (start, stop, _), p, gp in zip(spans, probs, grads):
                ds = (p * (gp - dots)).astype(bf16)
                gv_acc[start:stop, :] += dot_nn(p.astype(bf16), do_head)
                gk_acc[start:stop, :] += dot_nn(ds, q_head)
                side = side + dot_nn(k_head[:, start:stop], ds)
            sides.append(side * scale)
        both = jnp.concatenate(sides, axis=0)
        g_t_ref[0, :, low:high] = both.astype(bf16)
        g_ref[0, low:high, :] = both.T.astype(bf16)
    for n, acc in ((1, gk_acc), (2, gv_acc)):
        g_ref[n] = acc[...].astype(bf16)
        g_t_ref[n] = acc[...].T.astype(bf16)


def attend_back(qkv, bias, lse, grad_context):
    rows, d = grad_context.shape
    pairs = d // LANES

    def third(n):
        return pl.BlockSpec((rows, LANES), lambda h: (0, n * pairs + h))

    return call(
        attend_back_kernel,
        (pairs,),
        [
            fixed((rows, 1)),
            pl.BlockSpec((1, 8, rows), lambda h: (h, 0, 0)),
            third(0),
            third(1),
            third(2),
            third(0),
        ],
        [
            pl.BlockSpec((3, rows, LANES), lambda h: (0, 0, h)),
            pl.BlockSpec((3, LANES, rows), lambda h: (0, h, 0)),
        ],
        [shape_of((3, rows, d), bf16), shape_of((3, d, rows), bf16)],
        scratch=[pltpu.VMEM((rows, LANES), f32), pltpu.VMEM((rows, LANES), f32)],
        micros=28,
        name="attend_back",
    )(bias, lse, qkv, qkv, qkv, grad_context)


def after_kernel(
    rb, core_ref, x_ref, ctx_ref, cot_ref, w_ref, g_ref, b_ref, mix_ref,
    middle_ref, second_ref, second_t_ref, gdl_ref, gdl_t_ref, mixing_ref,
):
    d = x_ref.shape[1]
    middle = x_ref[...].astype(f32) + dot_nn(ctx_ref[...], w_ref[...])
    middle_ref[...] = middle
    n, _ = normalized(middle)
    second = (n * g_ref[...] + b_ref[...]).astype(bf16)
    second_ref[...] = second
    logits = dot_nn(second, mix_ref[...])
    gap = logits[:, 1:2] - logits[:, 0:1]
    first_share = 1.0 / (1.0 + jnp.exp(gap))
    other_share = 1.0 / (1.0 + jnp.exp(-gap))
    lane = lax.broadcasted_iota(jnp.int32, mixing_ref.shape, 1)
    mixing_ref[...] = jnp.where(lane == 0, first_share, other_share)
    gdl = (first_share * cot_ref[...].astype(f32)).astype(bf16)
    gdl_ref[...] = gdl
    core = core_ref[0]
    for values, target in ((second, second_t_ref), (gdl, gdl_t_ref)):
        turned = values.astype(f32).T.astype(bf16)
        for piece in range(d // rb):
            place = ((piece % 2) ^ core) * (d // (2 * rb)) + piece // 2
            target[pl.ds(pl.multiple_of(place * rb, rb), rb), :] = turned[
                piece * rb : (piece + 1) * rb, :
            ]


def after(tokens, core, context, cotangent, weight, gain, bias, mix_padded, rb):
    rows, d = tokens.shape
    block = rows_of(ROW_BLOCK, d)
    turned = pl.BlockSpec((d, ROW_BLOCK), lambda i, *_: (0, i))
    return call(
        functools.partial(after_kernel, rb),
        (rows // ROW_BLOCK,),
        [block, block, block, fixed((d, d)), fixed((1, d)), fixed((1, d)), fixed((d, LANES))],
        [block, block, turned, block, turned, rows_of(ROW_BLOCK, LANES)],
        [
            shape_of((rows, d), f32),
            shape_of((rows, d), bf16),
            shape_of((d, rows), bf16),
            shape_of((rows, d), bf16),
            shape_of((d, rows), bf16),
            shape_of((rows, LANES), f32),
        ],
        prefetch=1,
        micros=10,
        name="after",
    )(core, tokens, context, cotangent, weight, gain, bias, mix_padded)


def dense_kernel(
    owner_ref, second_ref, second_t_ref, gdl_ref, gdl_t_ref, up_ref, down_ref,
    hidden_ref, gpre_ref, keep_ref, send_ref, keep_next_ref, send_next_ref,
):
    rows = second_ref.shape[0]
    half = second_t_ref.shape[0] // 2
    levels = keep_ref.shape[1]
    for low in range(0, rows, ROW_BLOCK):
        at = slice(low, low + ROW_BLOCK)
        value, slope = gelu_pair(dot_nn(second_ref[at, :], up_ref[...]))
        hidden_ref[0, at, :] = value.astype(bf16)
        gpre_ref[0, at, :] = (dot_nt(gdl_ref[at, :], down_ref[...]) * slope).astype(bf16)

    def write(keep, send):
        for n, lhs_ref, units_ref in ((0, second_t_ref, gpre_ref), (1, gdl_t_ref, hidden_ref)):
            for target, low in ((keep, 0), (send, half)):
                grad = dot_nn(lhs_ref[low : low + half, :], units_ref[0]).astype(bf16)
                for z in range(levels):
                    target[0, z, n] = grad[z * (half // levels) : (z + 1) * (half // levels)]

    upper = pl.program_id(0) >= pl.num_programs(0) // 2
    pl.when(jnp.logical_not(upper))(lambda: write(keep_ref, send_ref))
    pl.when(upper)(lambda: write(keep_next_ref, send_next_ref))


def dense(second, chunk, owners, levels, second_t, gdl, gdl_t, up, down):
    rows, d = second.shape
    n = owners.shape[0]
    width = up.shape[1] // (n * CHUNKS)
    shape = (levels, 2, d // (2 * levels), width)
    lower = pl.BlockSpec((1,) + shape, lambda t, _: (jnp.minimum(t, n // 2 - 1), 0, 0, 0, 0))
    upper = pl.BlockSpec((1,) + shape, lambda t, _: (jnp.maximum(t - n // 2, 0), 0, 0, 0, 0))
    units = pl.BlockSpec((1, rows, width), lambda t, _: (t, 0, 0))
    return call(
        dense_kernel,
        (n,),
        [
            fixed((rows, d)),
            fixed((d, rows)),
            fixed((rows, d)),
            fixed((d, rows)),
            pl.BlockSpec((d, width), lambda t, owner: (0, owner[t] * CHUNKS + chunk)),
            pl.BlockSpec((width, d), lambda t, owner: (owner[t] * CHUNKS + chunk, 0)),
        ],
        [units, units, lower, lower, upper, upper],
        [shape_of((n, rows, width), bf16)] * 2
        + [shape_of((n // 2,) + shape, bf16)] * 4,
        prefetch=1,
        micros=100,
        name="dense",
    )(owners, second, second_t, gdl, gdl_t, up, down)


def dense_rest_kernel(
    owner_ref, place_ref, hidden0_ref, hidden1_ref, gpre0_ref, gpre1_ref, up_ref, down_ref,
    out_ref, gsec_ref,
):
    width = hidden0_ref.shape[2]

    @pl.when(pl.program_id(0) == 0)
    def _():
        out_ref[...] = jnp.zeros_like(out_ref)
        gsec_ref[...] = jnp.zeros_like(gsec_ref)

    out_ref[...] += dot_nn(hidden0_ref[0], down_ref[:width, :]) + dot_nn(
        hidden1_ref[0], down_ref[width:, :]
    )
    gsec_ref[...] += dot_nt(gpre0_ref[0], up_ref[:, :width]) + dot_nt(
        gpre1_ref[0], up_ref[:, width:]
    )


def dense_rest(hidden0, owners, places, hidden1, gpre0, gpre1, up, down):
    n, rows, width = hidden0.shape
    d = up.shape[0]
    units0 = pl.BlockSpec((1, rows, width), lambda t, owner, place: (t, 0, 0))
    units1 = pl.BlockSpec((1, rows, width), lambda t, owner, place: (place[t], 0, 0))
    return call(
        dense_rest_kernel,
        (n,),
        [
            units0,
            units1,
            units0,
            units1,
            pl.BlockSpec((d, 2 * width), lambda t, owner, _: (0, owner[t])),
            pl.BlockSpec((2 * width, d), lambda t, owner, _: (owner[t], 0)),
        ],
        [kept((rows, d))] * 2,
        [shape_of((rows, d), f32)] * 2,
        prefetch=2,
        micros=3000,
        name="dense_rest",
    )(owners, places, hidden0, hidden1, gpre0, gpre1, up, down)


def shares(logits, experts, me):
    lane = lax.broadcasted_iota(jnp.int32, logits.shape, 1)

    def softmax(inside):
        held = jnp.where(inside, logits, MASKED)
        raised = jnp.where(inside, jnp.exp(held - jnp.max(held, axis=1, keepdims=True)), 0.0)
        return raised / jnp.sum(raised, axis=1, keepdims=True)

    def pick(values, at):
        return jnp.sum(jnp.where(lane == at, values, 0.0), axis=1, keepdims=True)

    gates = softmax(lane < experts)
    mixing = softmax((lane >= experts) & (lane < experts + 2))
    return gates, pick(gates, me), pick(mixing, experts), pick(mixing, experts + 1)


def expert_step(arr_ref, garr_ref, up_ref, down_ref, hidden_ref, gpre_ref, out_acc, gin_acc):
    rows = arr_ref.shape[0]
    step = rows // 3
    for low in range(0, rows, step):
        at = slice(low, low + step)
        value, slope = gelu_pair(dot_nn(arr_ref[at, :], up_ref[...]))
        h = value.astype(bf16)
        g = (dot_nt(garr_ref[at, :], down_ref[...]) * slope).astype(bf16)
        gpre_ref[0, at, :] = g
        out_acc[at, :] += dot_nn(h, down_ref[...])
        gin_acc[at, :] += dot_nt(g, up_ref[...])
        hidden_ref[0, at, :] = h


def expert_first_kernel(
    experts, me_ref, arr_ref, cot_ref, gate_ref, up_ref, down_ref,
    hidden_ref, gpre_ref, garr_ref, logit_ref, out_acc, gin_acc,
):
    rows = arr_ref.shape[0]
    step = rows // 3

    @pl.when(pl.program_id(0) == 0)
    def _():
        out_acc[...] = jnp.zeros_like(out_acc)
        gin_acc[...] = jnp.zeros_like(gin_acc)
        for low in range(0, rows, step):
            at = slice(low, low + step)
            logits = dot_nn(arr_ref[at, :], gate_ref[...])
            logit_ref[at, :] = logits
            _, chosen, _, mix1 = shares(logits, experts, me_ref[0])
            garr_ref[at, :] = ((chosen * mix1) * cot_ref[at, :].astype(f32)).astype(bf16)

    expert_step(arr_ref, garr_ref, up_ref, down_ref, hidden_ref, gpre_ref, out_acc, gin_acc)


def expert_second_kernel(
    experts, me_ref, arr_ref, cot_ref, gate_ref, up_ref, down_ref, garr_ref, logit_ref, out_ref,
    grad_ref, hidden_ref, gpre_ref, sent_ref, gin_ref, gate_grad_ref, out_acc, gin_acc,
):
    rows = arr_ref.shape[0]
    step = rows // 3
    me = me_ref[0]

    @pl.when(pl.program_id(0) == 0)
    def _():
        out_acc[...] = out_ref[...]
        gin_acc[...] = grad_ref[...]

    expert_step(arr_ref, garr_ref, up_ref, down_ref, hidden_ref, gpre_ref, out_acc, gin_acc)

    @pl.when(pl.program_id(0) == pl.num_programs(0) - 1)
    def _():
        gate_grad = 0.0
        lane = lax.broadcasted_iota(jnp.int32, (step, LANES), 1)
        for low in range(0, rows, step):
            at = slice(low, low + step)
            gates, chosen, mix0, mix1 = shares(logit_ref[at, :], experts, me)
            out = out_acc[at, :]
            sent_ref[at, :] = ((chosen * mix1) * out).astype(bf16)
            met = jnp.sum(cot_ref[at, :].astype(f32) * out, axis=1, keepdims=True)
            grad_chosen = mix1 * met
            swing = chosen * met * mix0 * mix1
            grad = gates * grad_chosen * (jnp.where(lane == me, 1.0, 0.0) - chosen)
            grad = grad + jnp.where(lane == experts + 1, swing, 0.0)
            grad = grad - jnp.where(lane == experts, swing, 0.0)
            low_grad = grad.astype(bf16)
            gin_ref[at, :] = (gin_acc[at, :] + dot_nt(low_grad, gate_ref[...])).astype(bf16)
            gate_grad = gate_grad + dot_nn(grad.T.astype(bf16), arr_ref[at, :])
        gate_grad_ref[...] = gate_grad


def expert(arriving, half, n, me, cot, gate_padded, up, down, experts, before=None):
    rows, d = arriving.shape
    width = up.shape[1] // (2 * n)
    units = pl.BlockSpec((1, rows, width), lambda t, *_: (t, 0, 0))
    specs = [
        fixed((rows, d)),
        fixed((rows, d)),
        fixed((d, LANES)),
        pl.BlockSpec((d, width), lambda t, *_: (0, 2 * t + half)),
        pl.BlockSpec((width, d), lambda t, *_: (2 * t + half, 0)),
    ]
    shapes = [shape_of((n, rows, width), bf16)] * 2
    if half == 0:
        return call(
            functools.partial(expert_first_kernel, experts),
            (n,),
            specs,
            [units, units] + [kept((rows, d)), kept((rows, LANES))] + [kept((rows, d))] * 2,
            shapes
            + [shape_of((rows, d), bf16), shape_of((rows, LANES), f32)]
            + [shape_of((rows, d), f32)] * 2,
            prefetch=1,
            micros=4800,
            name="expert_first",
        )(me, arriving, cot, gate_padded, up, down)
    return call(
        functools.partial(expert_second_kernel, experts),
        (n,),
        specs + [fixed((rows, d)), fixed((rows, LANES)), fixed((rows, d)), fixed((rows, d))],
        [units, units] + [kept((rows, d))] * 2 + [kept((LANES, d))],
        shapes + [shape_of((rows, d), bf16)] * 2 + [shape_of((LANES, d), f32)],
        scratch=[pltpu.VMEM((rows, d), f32), pltpu.VMEM((rows, d), f32)],
        prefetch=1,
        micros=100,
        name="expert_second",
    )(me, arriving, cot, gate_padded, up, down, *before)


def between_kernel(
    target_ref, gin_ref, gs_ref, do_ref, middle_ref, mixing_ref, cot_ref,
    second_ref, mix_t_ref, g_ref, w_ref, gatt_ref, gctx_ref, sums_ref,
):
    @pl.when(pl.program_id(0) == 0)
    def _():
        sums_ref[...] = jnp.zeros_like(sums_ref)

    slots = gin_ref.shape[0]
    lane = lax.broadcasted_iota(jnp.int32, (ROW_BLOCK, slots), 1)
    pick = jnp.where(target_ref[...] == lane, 1.0, 0.0).astype(bf16)
    grad = gs_ref[...] + dot_nn(pick, gin_ref[...])
    go = cot_ref[...].astype(f32)
    met = jnp.sum(go * do_ref[...], axis=1, keepdims=True)
    swing = met * mixing_ref[:, 0:1] * mixing_ref[:, 1:2]
    grad = grad + swing * (mix_t_ref[0:1, :] - mix_t_ref[1:2, :])
    n, root = normalized(middle_ref[...])
    sums_ref[0:1, :] += jnp.sum(grad * n, axis=0, keepdims=True)
    sums_ref[1:2, :] += jnp.sum(grad, axis=0, keepdims=True)
    sums_ref[2:3, :] += jnp.sum(second_ref[...].astype(f32) * swing, axis=0, keepdims=True)
    u = grad * g_ref[...]
    u_mean = jnp.mean(u, axis=1, keepdims=True)
    un_mean = jnp.mean(u * n, axis=1, keepdims=True)
    gatt = (go + root * (u - u_mean - n * un_mean)).astype(bf16)
    gatt_ref[...] = gatt
    gctx_ref[...] = dot_nt(gatt, w_ref[...]).astype(bf16)


def between(gs, target, gin, do, middle, mixing, cotangent, second, mix_t, gain, weight):
    rows, d = middle.shape
    slots = gin.shape[0]
    block = rows_of(ROW_BLOCK, d)
    return call(
        between_kernel,
        (rows // ROW_BLOCK,),
        [
            rows_of(ROW_BLOCK, 1), fixed((slots, d)), block, block, block,
            rows_of(ROW_BLOCK, LANES), block, block, fixed((2, d)), fixed((1, d)), fixed((d, d)),
        ],
        [block, block, kept((8, d))],
        [shape_of((rows, d), bf16), shape_of((rows, d), bf16), shape_of((8, d), f32)],
        micros=12,
        name="between",
    )(
        target, gin, gs, do, middle, mixing, cotangent, second, mix_t, gain,
        weight,
    )


def out_kernel(target_ref, back_ref, do_ref, middle_ref, mixing_ref, out_ref):
    slots = back_ref.shape[0]
    lane = lax.broadcasted_iota(jnp.int32, (ROW_BLOCK, slots), 1)
    pick = jnp.where(target_ref[...] == lane, 1.0, 0.0).astype(bf16)
    mixed = mixing_ref[:, 0:1] * do_ref[...] + dot_nn(pick, back_ref[...])
    out_ref[...] = (middle_ref[...] + mixed).astype(bf16)


def outputs_of(do, target, back, middle, mixing):
    rows, d = middle.shape
    slots = back.shape[0]
    block = rows_of(ROW_BLOCK, d)
    return call(
        out_kernel,
        (rows // ROW_BLOCK,),
        [
            rows_of(ROW_BLOCK, 1), fixed((slots, d)), block, block,
            rows_of(ROW_BLOCK, LANES),
        ],
        block,
        shape_of((rows, d), bf16),
        micros=7,
        name="outputs",
    )(target, back, do, middle, mixing)


def first_back_kernel(g_ref, w_ref, x_ref, gatt_ref, gain_ref, gx_ref, sums_ref):
    d = x_ref.shape[1]

    @pl.when(pl.program_id(0) == 0)
    def _():
        sums_ref[...] = jnp.zeros_like(sums_ref)

    grad = dot_nt(g_ref[0], w_ref[:, :d])
    grad = grad + dot_nt(g_ref[1], w_ref[:, d : 2 * d])
    grad = grad + dot_nt(g_ref[2], w_ref[:, 2 * d :])
    n, root = normalized(x_ref[...].astype(f32))
    sums_ref[0:1, :] += jnp.sum(grad * n, axis=0, keepdims=True)
    sums_ref[1:2, :] += jnp.sum(grad, axis=0, keepdims=True)
    u = grad * gain_ref[...]
    u_mean = jnp.mean(u, axis=1, keepdims=True)
    un_mean = jnp.mean(u * n, axis=1, keepdims=True)
    gx_ref[...] = (gatt_ref[...].astype(f32) + root * (u - u_mean - n * un_mean)).astype(bf16)


def first_back(grad_qkv, weight, tokens, gatt, gain):
    rows, d = tokens.shape
    block = rows_of(ROW_BLOCK, d)
    return call(
        first_back_kernel,
        (rows // ROW_BLOCK,),
        [
            pl.BlockSpec((3, ROW_BLOCK, d), lambda i: (0, i, 0)),
            fixed((d, 3 * d)),
            block,
            block,
            fixed((1, d)),
        ],
        [block, kept((8, d))],
        [shape_of((rows, d), bf16), shape_of((8, d), f32)],
        micros=12,
        name="first_back",
    )(grad_qkv, weight, tokens, gatt, gain)


def dot_tn(a, b):
    return lax.dot_general(a, b, (((0,), (0,)), ((), ())), preferred_element_type=f32)


def expert_grad_kernel(
    up_owner_ref, down_owner_ref, arr_ref, gpre_ref, hidden_ref, garr_ref, up_ref, down_ref
):
    width = gpre_ref.shape[2]
    up = dot_tn(arr_ref[...], gpre_ref[0]).astype(bf16)
    for low in range(0, up.shape[0], width):
        up_ref[0, :, low : low + width] = up[low : low + width, :]
    down_ref[0] = dot_tn(hidden_ref[0], garr_ref[...]).astype(bf16)


def expert_grads(arriving, up_owners, down_owners, gpre, hidden, garr):
    _, rows, width = gpre.shape
    d = arriving.shape[1]
    m = up_owners.shape[0]
    return call(
        expert_grad_kernel,
        (m,),
        [
            fixed((rows, d)),
            pl.BlockSpec((1, rows, width), lambda t, up, down: (up[t], 0, 0)),
            pl.BlockSpec((1, rows, width), lambda t, up, down: (down[t], 0, 0)),
            fixed((rows, d)),
        ],
        [pl.BlockSpec((1, width, d), lambda t, *_: (t, 0, 0))] * 2,
        [shape_of((m, width, d), bf16)] * 2,
        prefetch=2,
        micros=7,
        name="expert_grads",
    )(up_owners, down_owners, arriving, gpre, hidden, garr)


def half_sums(terms):
    second = functools.reduce(lambda a, b: a + b, [ref[0].astype(f32) for ref in terms[1:]])
    return terms[0][0].astype(f32), second


def up_final_kernel(*refs):
    *terms, out_ref = refs
    width = terms[0].shape[2]
    for n, total in enumerate(half_sums(terms)):
        out_ref[:, n * width : (n + 1) * width] = total


def down_final_kernel(*refs):
    *terms, out_ref = refs
    for n, total in enumerate(half_sums(terms)):
        out_ref[n] = total


def up_final(*terms):
    _, width, d = terms[0].shape
    block = 128
    return call(
        up_final_kernel,
        (d // width, width // block),
        [pl.BlockSpec((1, block, width), lambda i, r: (0, r, i))] * len(terms),
        pl.BlockSpec((block, 2 * width), lambda i, r: (i * (width // block) + r, 0)),
        shape_of((d, 2 * width), f32),
        micros=1000,
        name="up_final",
    )(*terms)


def down_final(*terms):
    _, width, d = terms[0].shape
    block = 128
    return call(
        down_final_kernel,
        (width // block,),
        [pl.BlockSpec((1, block, d), lambda r: (0, r, 0))] * len(terms),
        pl.BlockSpec((2, block, d), lambda r: (0, r, 0)),
        shape_of((2, width, d), f32),
        micros=1000,
        name="down_final",
    )(*terms).reshape(2 * width, d)


def join_kernel(count, *refs):
    *terms, out_ref = refs
    left, right, lower = terms[:count], terms[count : 2 * count], terms[2 * count :]
    height, width = right[0].shape[2:]
    more = lower[0].shape[2]

    def total(parts):
        return functools.reduce(
            lambda a, b: a + b, [ref[0, 0].astype(f32) for ref in parts]
        ).astype(bf16)

    whole = total(left)
    out_ref[0, :height, :width] = whole[:height]
    out_ref[0, :height, width:] = total(right)
    out_ref[0, height : height + more, :] = total(lower)
    out_ref[0, height + more :, :width] = whole[height:]
    out_ref[0, height + more :, width:] = jnp.zeros_like(whole[height:])


def join(left, right, lower):
    levels, height, width = right.terms[0].shape[1:]
    more, rest = lower.terms[0].shape[2], left.terms[0].shape[2] - height
    if height % 16 or more % 16:
        left, right, lower = [part.finish(bf16) for part in (left, right, lower)]
        both = jnp.concatenate([left[:, :height], right], axis=2)
        last = jnp.pad(left[:, height:], ((0, 0), (0, 0), (0, width)))
        return jnp.concatenate([both, lower, last], axis=1)
    terms = left.terms + right.terms + lower.terms
    return Line.run(
        call(
            functools.partial(join_kernel, len(left.terms)),
            (levels,),
            [
                pl.BlockSpec((1, 1) + term.shape[2:], lambda z: (0, z, 0, 0)) for term in terms
            ],
            pl.BlockSpec((1, height + more + rest, 2 * width), lambda z: (z, 0, 0)),
            shape_of((levels, height + more + rest, 2 * width), bf16),
            micros=3,
            name="join",
        ),
        *terms,
    )


def swap(values, axis, bit):
    n = lax.axis_size(axis)
    return lax.ppermute(values, axis, [(i, i ^ bit) for i in range(n)])


def rows_kernel(sides, owner_ref, place_ref, ep_ref, a_ref, b_ref, *refs):
    *refs, grad_ref = refs
    extra_ref, out_refs = (refs[0], refs[1:]) if len(refs) % 2 else (None, refs)
    levels, height, width = out_refs[sides - 1].shape[1:]
    grad_ref[...] = dot_nn(a_ref[...], b_ref[...]).astype(bf16)
    for which in range(2):
        for z in range(levels):
            place = ep_ref[0] ^ (2 * reversed_bits(z, levels.bit_length() - 1) + 1 - which)
            rows = pl.ds(pl.multiple_of(place * height, height), height)
            for n in range(sides):
                out_refs[which * sides + n][0, z, :height, :] = grad_ref[
                    rows, n * width : (n + 1) * width
                ]
            if extra_ref is not None:
                out_refs[which * sides][0, z, height:, :] = extra_ref[0, place]


def rows_grad(a, b, owners, places, ep, copies, levels, sides, micros, extra=None):
    rows, d = b.shape
    height = a.shape[0] // (2 * copies * levels)
    width = d // sides
    if height % 16:
        away = [2 * reversed_bits(z, levels.bit_length() - 1) for z in range(levels)]

        def parts_of(values):
            values = jnp.take(values, owners, axis=0)
            return [
                jnp.take(values, ep[0] ^ (jnp.array(away, jnp.int32) + other), axis=1)
                for other in (1, 0)
            ]

        parts = parts_of(dot_nn(a, b).astype(bf16).reshape(copies, 2 * levels, height, d))
        result = [
            (part if n == 0 else jnp.take(part, places, axis=0))[
                ..., n * width : (n + 1) * width
            ]
            for part in parts
            for n in range(sides)
        ]
        if extra is not None:
            for which, rest in enumerate(parts_of(extra)):
                result[which * sides] = jnp.concatenate([result[which * sides], rest], axis=2)
        return result

    def shape(side):
        more = 0 if extra is None or side else extra.shape[2]
        return (levels, height + more, width)

    def piece(side):
        return pl.BlockSpec(
            (1,) + shape(side),
            lambda t, owner, place, ep: (place[t] if side else t, 0, 0, 0),
        )

    block = 2 * levels * height
    specs = [pl.BlockSpec((block, rows), lambda t, owner, *_: (owner[t], 0)), fixed((rows, d))]
    operands = [owners, places, ep, a, b]
    if extra is not None:
        specs.append(
            pl.BlockSpec((1,) + extra.shape[1:], lambda t, owner, *_: (owner[t], 0, 0, 0))
        )
        operands.append(extra)
    return call(
        functools.partial(rows_kernel, sides),
        (copies,),
        specs,
        [piece(side) for which in range(2) for side in range(sides)],
        [
            shape_of((copies,) + shape(side), bf16) for which in range(2) for side in range(sides)
        ],
        scratch=[pltpu.VMEM((block, d), bf16)],
        prefetch=3,
        micros=micros,
        name="rows_grad",
    )(*operands)


def add_kernel(*refs):
    *term_refs, out_ref = refs
    total = term_refs[0][...].astype(f32)
    for ref in term_refs[1:]:
        total = total + ref[...].astype(f32)
    out_ref[...] = total.astype(out_ref.dtype)


def add_terms(last, *others, first, count, kind):
    terms = [*others, last]
    shape = terms[0].shape
    columns = shape[-1]
    height = 1
    for extent in shape[1:-1]:
        height *= extent
    block = max(b for b in range(1, height + 1) if height % b == 0 and b * columns <= 1 << 18)
    result = call(
        add_kernel,
        (count, height // block),
        [pl.BlockSpec((1, block, columns), lambda t, r, *_: (first + t, r, 0)) for _ in terms],
        pl.BlockSpec((1, block, columns), lambda t, r, *_: (t, r, 0)),
        shape_of((count, height, columns), kind),
        micros=3,
        name="add_terms",
    )(*[term.reshape(term.shape[0], height, columns) for term in terms])
    return result.reshape((count,) + shape[1:])


class Halving:
    def __init__(self, terms, axis, bits, stride=1):
        self.terms, self.axis, self.bits, self.stride = terms, axis, list(bits), stride
        self.kind, self.extent = terms[0].dtype, 1 << len(self.bits)

    def add(self, first, kind):
        return Line.run(
            functools.partial(add_terms, first=first, count=self.extent, kind=kind),
            self.terms[-1], *self.terms[:-1],
        )

    def step(self, sent=None):
        if self.bits:
            if sent is None:
                self.extent //= 2
                sent = self.add(self.extent, self.kind)
            self.terms.append(swap(sent, self.axis, self.bits.pop(0) * self.stride))

    def finish(self, kind=f32):
        while self.bits:
            self.step()
        return self.add(0, kind)[0]


def reversed_bits(value, count):
    return sum(((value >> i) & 1) << (count - 1 - i) for i in range(count))


def shards(
    tokens, lengths, key_mask, routes, norm1_gain, norm1_bias, qkv_weight, out_weight,
    norm2_gain, norm2_bias, up_weight, down_weight, router_weight, mix_weight, expert_up,
    expert_down, cotangent,
):
    rows, d = tokens.shape
    groups, copies = lax.axis_size("ep"), lax.axis_size("dp")
    experts = expert_up.shape[0] * groups
    capacity = (5 * rows + 4 * experts - 1) // (4 * experts)
    slots = experts * capacity
    ep, dp = lax.axis_index("ep"), lax.axis_index("dp")
    core, level, levels = ep % 2, ep // 2, groups // 2
    count = copies.bit_length() - 1
    up_bits = [1 << i for i in reversed(range(count))]
    down_bits = [1 << i for i in range(count)]
    level_bits = [1 << i for i in range(levels.bit_length() - 1)]
    level_groups = [[2 * z + c for z in range(levels)] for c in range(2)]
    order = jnp.arange(copies, dtype=jnp.int32)
    back_order = jnp.array([reversed_bits(t, count) for t in range(copies)], jnp.int32)
    owners = dp.astype(jnp.int32) ^ order
    back_owners = dp.astype(jnp.int32) ^ back_order
    core_scalar = core.astype(jnp.int32).reshape(1)
    ep_scalar = ep.astype(jnp.int32).reshape(1)

    row_at = jnp.arange(rows, dtype=jnp.int32)
    live = row_at < lengths[0]
    flat_routes = routes[:, 0]
    routed = (flat_routes[:, None] == jnp.arange(experts)[None, :]) & live[:, None]
    ahead = dot_nn(
        (row_at[None, :] < row_at[:, None]).astype(bf16), routed.astype(bf16)
    )
    place = jnp.sum(jnp.where(routed, ahead, 0.0), axis=1).astype(jnp.int32)
    target = jnp.where(live, flat_routes * capacity + place, slots)
    target_column = target[:, None]
    pick = (jnp.arange(slots, dtype=jnp.int32)[:, None] == target[None, :]).astype(bf16)

    def exchange(values):
        return lax.all_to_all(
            values.reshape(groups, slots // groups, d), "ep", 0, 0, tiled=True
        ).reshape(slots, d)

    def sort_rows(values):
        return dot_nn(pick, values).astype(bf16)

    run = Line.run
    Line.last = None
    cot_arriving = exchange(run(sort_rows, cotangent))
    usable = live & (key_mask == 1)
    bias = jnp.where(usable, 0.0, MASKED).astype(f32)[:, None]
    mix_padded = jnp.pad(mix_weight, ((0, 0), (0, LANES - 2)))
    gate_padded = jnp.pad(
        jnp.concatenate([router_weight, mix_weight], axis=1),
        ((0, 0), (0, LANES - 2 - experts)),
    )
    first, qkv = run(ln_qkv, tokens, norm1_gain[None], norm1_bias[None], qkv_weight)
    context, context_t, lse = run(attend, qkv, bias)
    middle, second, second_t, gdl, gdl_t, mixing = run(
        after, tokens, core_scalar, context, cotangent, out_weight, norm2_gain[None],
        norm2_bias[None], mix_padded, d // groups,
    )
    cot_arriving, second = lax.optimization_barrier((cot_arriving, second))
    arriving = exchange(run(sort_rows, second))

    orders = (owners, up_bits), (back_owners, down_bits)
    parts = [
        run(dense, second, chunk, order, levels, second_t, gdl, gdl_t, up_weight, down_weight)
        for chunk, (order, _) in enumerate(orders)
    ]
    sums, lower = [], []
    half = copies // 2
    for (_, _, keep, send, keep_next, send_next), (_, bits) in zip(parts, orders):
        got_next, got = swap(send_next, "ep", 1), swap(send, "ep", 1)
        lower.append(got)
        sums.append(Halving([keep, got], "dp", bits))
        sums[-1].extent = half
        sums[-1].step(
            run(
                functools.partial(add_terms, first=0, count=half, kind=bf16), got_next, keep_next
            )
        )
    Line.others = tuple(lower)
    given = copies, ep_scalar, cot_arriving, gate_padded, expert_up[0], expert_down[0], experts
    m = copies // 2

    def expert_part(first, gpre, hidden):
        at = slice(m, None) if first else slice(0, m)
        return run(expert_grads, arriving, owners[at], back_owners[at], gpre, hidden, garr)

    def swapped(pair):
        return [swap(sent, "dp", bits[0]) for sent, bits in zip(pair, (up_bits, down_bits))]

    hidden0, gpre0, garr, *before = run(expert, arriving, 0, *given)
    got0 = swapped(expert_part(True, gpre0, hidden0))
    hidden1, gpre1, sent, gin, gate_grad = run(expert, arriving, 1, *given, [garr, *before])
    grad_back = exchange(gin)
    dense_out, grad_second = run(
        dense_rest, parts[0][0], owners, back_order, parts[1][0], parts[0][1], parts[1][1], up_weight,
        down_weight,
    )
    for side in sums:
        side.step()
    got1 = swapped(expert_part(True, gpre1, hidden1))

    def halvings(keeps, gots):
        return [
            Halving([keep, got], "dp", bits[1:])
            for keep, got, bits in zip(keeps, gots, (up_bits, down_bits))
        ]

    halves0 = halvings(expert_part(False, gpre0, hidden0), got0)
    for side in halves0:
        side.step()
    pieces = [
        lax.psum_scatter(
            side.finish(bf16), "ep", scatter_dimension=0, axis_index_groups=level_groups
        )
        for side in sums
    ]
    halves1 = halvings(expert_part(False, gpre1, hidden1), got1)
    gatt, grad_context, sums2 = run(
        between, grad_second, target_column, grad_back, dense_out, middle, mixing, cotangent,
        second, mix_weight.T.astype(f32), norm2_gain[None], out_weight,
    )

    sent, gatt = lax.optimization_barrier((sent, gatt))
    expert_back = exchange(sent)

    def own_rows(a, b, all_bits, micros, extra=None):
        sides = len(all_bits)
        result = run(
            rows_grad, a, b, owners, back_order, ep_scalar, copies, levels, sides, micros,
            extra,
        )
        return [
            Halving([keep, swap(send, "ep", 1)], "dp", bits)
            for send, keep, bits in zip(result[:sides], result[sides:], all_bits)
        ]

    (out_side,) = own_rows(context_t, gatt, [up_bits], 3)
    grad_qkv, grad_qkv_t = run(attend_back, qkv, bias, lse, grad_context)
    done0 = [side.finish(bf16)[None] for side in halves0]
    for side in halves1:
        side.step()
    grad_inputs, sums1 = run(first_back, grad_qkv, qkv_weight, tokens, gatt, norm1_gain[None])
    home_mix = jnp.concatenate(
        [jnp.zeros((experts, d), f32), sums2[2:3], -sums2[2:3]], axis=0
    )
    small = jnp.concatenate(
        [sums1[:2], sums2[:2], gate_grad[: experts + 2] + home_mix], axis=0
    )
    kinds = small.shape[0]
    small = small.reshape(kinds, copies, groups, -1).transpose(1, 2, 0, 3)
    own = small.shape[3]
    small = small.reshape(copies, groups, 1, kinds * own).astype(bf16)
    small = jnp.pad(small, ((0, 0), (0, 0), (0, 15), (0, d // 2 - kinds * own)))
    qkv_sides = own_rows(
        grad_qkv_t.reshape(3 * d, rows), first, [up_bits, down_bits], 7, small
    )
    expert_up_sum, expert_down_sum = [
        run(final, first_half, *second_half.terms)
        for final, first_half, second_half in zip((up_final, down_final), done0, halves1)
    ]
    for side in qkv_sides:
        side.step()
    out_side.step()
    outputs = run(outputs_of, dense_out, target_column, expert_back, middle, mixing)
    for side in qkv_sides:
        side.step()
    out_side.step()
    whole = Halving([join(*qkv_sides, out_side)], "ep", level_bits, 2).finish()
    height = 3 * d // (copies * groups)
    qkv_sum, out_sum = whole[:height].T, whole[height : height + own]
    small = whole[height + own, : kinds * own].reshape(kinds, own).T
    pieces = [piece.astype(f32) for piece in pieces]
    up_sum, down_sum = [jnp.concatenate([piece[n] for piece in pieces], axis=1) for n in range(2)]
    down_sum = down_sum.T
    Line.last = None
    return (
        outputs, grad_inputs, small[:, 0], small[:, 1], qkv_sum, out_sum, small[:, 2],
        small[:, 3], up_sum, down_sum, small[:, 4 : 4 + experts], small[:, 4 + experts :],
        expert_up_sum[None], expert_down_sum[None],
    )


def solution(mesh):
    split = ("dp", "ep")
    return jax.shard_map(
        shards,
        mesh=mesh,
        in_specs=(
            P(split, None), P(split), P(split), P(split, None), P(), P(), P(), P(), P(), P(),
            P(), P(), P(), P(), P("ep", None, None), P("ep", None, None), P(split, None),
        ),
        out_specs=(
            P(split, None), P(split, None), P(split), P(split), P(None, split), P(split, None),
            P(split), P(split), P("ep", "dp"), P("dp", "ep"), P(split, None), P(split, None),
            P("ep", None, "dp"), P("ep", "dp", None),
        ),
        check_vma=False,
    )
```

time: 656 us -> 518 us (0.79)
  waiting for transfers between devices: 217 us -> 47.2 us
  Pallas kernels: 248 us -> 350 us
  other arithmetic: 60.2 us -> 7.88 us
  matrix products: 18.5 us -> 9.84 us
  local copies, waits for them, and re-layouts: 40.2 us -> 32.1 us
    unnamed x5 -> x2, waiting for transfers between devices: 121 us -> 0.03 us
    pallas_call x14 -> x42, Pallas kernels: 248 us -> 350 us  [apply(): pl.pallas_call(ordered, grid_spec=pltpu.PrefetchScalarGridSpec(num_scalar...]
    convert_element_type x24 -> x2, other arithmetic: 48.6 us -> 1.97 us  [shards(): pieces = [piece.astype(f32) for piece in pieces]]
    ppermute x26 -> x27, waiting for transfers between devices: 77.8 us -> 38.3 us  [swap(): return lax.ppermute(values, axis, [(i, i ^ bit) for i in range(n)])]
    reduce_scatter x3 -> x2, waiting for transfers between devices: 17.8 us -> 0.02 us  [shards(): lax.psum_scatter(side.finish(bf16), 'ep', scatter_dimension=0, axis_index...]
    all_to_all x4, waiting for transfers between devices: 0.01 us -> 8.85 us  [exchange(): lax.all_to_all(values.reshape(groups, slots // groups, d), 'ep', 0, 0, ti...]
    dot_general x5 -> x3, matrix products: 18.5 us -> 9.84 us  [dot_nn(): lax.dot_general(a, b, (((1,), (0,)), ((), ())), preferred_element_type=f32)]
    slice x15 -> x4, local copies, waits for them, and re-layouts: 11.5 us -> 3.52 us  [the longest x1 1.57 us: shards(): qkv_sum, out_sum = (whole[:height].T, whole[height:height + own])]
  transfers between devices with their start and end apart: 34 -> 33, of which waited for: 10 -> 7; matrix products, arithmetic and copies ran while one was open for 16% -> 4% of each run, Pallas kernels for 38% -> 68%
where the time goes in v2:
time: 518 us; the launch traced here: 509 us
  Pallas kernels  350 us (68%)
  waiting for transfers between devices  47.2 us (9%)
  starting transfers between devices  47 us (9%)
  local copies, waits for them, and re-layouts  32.1 us (6%)
  between operations  15.2 us (3%)
  matrix products  9.84 us (2%)
  other arithmetic  7.88 us (2%)
    pallas_call x42, Pallas kernels, apply(): pl.pallas_call(ordered, grid_spec=pltpu.PrefetchScalarGridSpec(num_scalar...  350 us
    ppermute x27, waiting for transfers between devices, swap(): return lax.ppermute(values, axis, [(i, i ^ bit) for i in range(n)])  38.3 us
    ppermute x27, starting transfers between devices, swap(): return lax.ppermute(values, axis, [(i, i ^ bit) for i in range(n)])  25.2 us
    all_to_all x4, starting transfers between devices, exchange(): lax.all_to_all(values.reshape(groups, slots // groups, d), 'ep', 0, 0, ti...  21.7 us
    unnamed x60, local copies, waits for them, and re-layouts  15.7 us
  transfers between devices with their start and end apart: 33, of which 7 were waited for; matrix products, arithmetic and copies ran while one was open for 4% of the time, Pallas kernels for 68%

profile of v2, /device:TPU:0, one launch (start us, length us, event | category | flops | bytes accessed | tf_op | source)
XLA Modules:
  0.0 509.1 jit_solution(16598123739115485496)
XLA Ops:
  10.1 4.4 fusion.3.refs_4_
  14.4 6.5 %all-to-all-start = ((bf16[8,120,1024]{2,1,0:T(8,128)(2,1)}), bf16[8,120,1024]{2,1,0:T(8,128)(2,1)S(1)}, u32[]{:S(2)}, u32[]{:S(2)}) async-start(bf16[8,120,1024]{2,1,0:T(8,128)(2,1)} %bitcast.2), calls=%async_computation | async-start | bytes 3932160 | tf_op jit(solution)/shard_map/all_to_all | solution.py:979
  22.8 11.5 %ln_qkv.1 = (bf16[768,1024]{1,0:T(8,128)(2,1)}, bf16[768,3072]{1,0:T(8,128)(2,1)}) custom-call(bf16[768,1024]{1,0:T(8,128)(2,1)} %refs_2_.1, f32[1,1024]{1,0:T(1,128)} %bitcast.162, f32[1,1024]{1,0:T(1,128)} %bitcast.165, bf16[1024,3072]{1,0:T(8,128)(2,1)} %refs_1_.6, bf16[960,1024]{1,0:T(8,128)(2,1)} %fusion.3.refs_4_), custom_call_target="tpu_custom_call" | custom-call | flops 126500000 | bytes 330000 | tf_op jit(solution)/shard_map/ln_qkv/pallas_call | solution.py:55
  34.3 22.5 %attend.1 = (bf16[768,1024]{1,0:T(8,128)(2,1)}, bf16[1024,768]{1,0:T(8,128)(2,1)}, f32[8,8,768]{2,1,0:T(8,128)}) custom-call(f32[768,1]{1,0:T(8,128)} %broadcast_in_dim.60.refs_0_, bf16[768,3072]{1,0:T(8,128)(2,1)} %get-tuple-element.75.refs_1_.refs_2_.refs_3_.refs_4_, bf16[768,3072]{1,0:T(8,128)(2,1)} %get-tuple-element.75.refs_1_.refs_2_.refs_3_.refs_4_, ...), custom_call_target="tpu_custom_call" | custom-call | flops 253000000 | bytes 660000 | tf_op jit(solution)/shard_map/attend/pallas_call | solution.py:55
  56.8 9.7 %after.1 = (f32[768,1024]{1,0:T(8,128)}, bf16[768,1024]{1,0:T(8,128)(2,1)}, bf16[1024,768]{1,0:T(8,128)(2,1)}, bf16[768,1024]{1,0:T(8,128)(2,1)}, bf16[1024,768]{1,0:T(8,128)(2,1)}, /*index=5*/f32[768,128]{1,0:T(8,128)}) custom-call(s32[1]{0:T(128)} %bitcast.4.refs_0_, bf16[768,1024]{1,0:T(8,128)(2,1)} %refs_2_.1, ...), custom_call_target="tpu_custom_call" | custom-call | flops 115000000 | bytes 300000 | tf_op jit(solution)/shard_map/after/pallas_call | solution.py:55
  67.1 5.1 %fusion.4.refs_7_ = bf16[960,1024]{1,0:T(8,128)(2,1)} fusion(bf16[768,1024]{1,0:T(8,128)(2,1)} %get-tuple-element.79.refs_1_.refs_7_, s32[768]{0:T(1024)S(1)} %add_select_fusion), kind=kOutput, calls=%fused_computation.6 | convolution fusion | flops 1511669760 | bytes 3542016 | tf_op jit(solution)/shard_map/dot_general | solution.py:25
  72.3 5.1 all-to-all-start.1
  77.9 22.7 %dense.2 = (bf16[4,768,512]{2,1,0:T(8,128)(2,1)}, bf16[4,768,512]{2,1,0:T(8,128)(2,1)}, bf16[2,4,2,128,512]{4,3,2,1,0:T(8,128)(2,1)}, bf16[2,4,2,128,512]{4,3,2,...) custom-call(s32[4]{0:T(128)} %get-tuple-element.208.refs_0_, ...), custom_call_target="tpu_custom_call" | custom-call | flops 1150000000 | bytes 3000000 | tf_op jit(solution)/shard_map/dense/pallas_call | solution.py:55
  101.1 22.8 %dense.3 = (bf16[4,768,512]{2,1,0:T(8,128)(2,1)}, bf16[4,768,512]{2,1,0:T(8,128)(2,1)}, bf16[2,4,2,128,512]{4,3,2,1,0:T(8,128)(2,1)}, bf16[2,4,2,128,512]{4,3,2,...) custom-call(s32[4]{0:T(128)} %get-tuple-element.209.refs_0_, ...), custom_call_target="tpu_custom_call" | custom-call | flops 1150000000 | bytes 3000000 | tf_op jit(solution)/shard_map/dense/pallas_call | solution.py:55
  132.5 4.3 add_terms.22
  139.6 27.7 %expert_first.1 = (bf16[4,960,512]{2,1,0:T(8,128)(2,1)}, bf16[4,960,512]{2,1,0:T(8,128)(2,1)}, bf16[960,1024]{1,0:T(8,128)(2,1)}, f32[960,128]{1,0:T(8,128)}, f32[960,1024]{1,0:T(8,128)}, /*index=5*/f32[960,1024]{1,0:T(8,128)}) custom-call(s32[1]{0:T(128)} %bitcast.1.refs_0_.refs_2_, bf16[960,1024]{1,0:T(8,128)(2,1)} %bitcast.93, ...), custom_call_target="tpu_custom_call" | custom-call | flops 55199997952 | bytes 144000000 | tf_op jit(solution)/shard_map/expert_first/pallas_call | solution.py:55
  167.4 9.3 %expert_grads.4 = (bf16[2,512,1024]{2,1,0:T(8,128)(2,1)}, bf16[2,512,1024]{2,1,0:T(8,128)(2,1)}) custom-call(s32[2]{0:T(128)} %get-tuple-element.207.refs_0_, s32[2]{0:T(128)} %get-tuple-element.205.refs_1_, bf16[960,1024]{1,0:T(8,128)(2,1)} %bitcast.94, bf16[4,960,512]{2,1,0:T(8,128)(2,1)} %get-tuple-element.96.refs_3_, ...), custom_call_target="tpu_custom_call" | custom-call | flops 80500000 | bytes 210000 | tf_op jit(solution)/shard_map/expert_grads/pallas_call | solution.py:55
  177.6 30.3 %expert_second.1 = (bf16[4,960,512]{2,1,0:T(8,128)(2,1)}, bf16[4,960,512]{2,1,0:T(8,128)(2,1)}, bf16[960,1024]{1,0:T(8,128)(2,1)}, bf16[960,1024]{1,0:T(8,128)(2,1)}, f32[128,1024]{1,0:T(8,128)}) custom-call(s32[1]{0:T(128)} %bitcast.1.refs_0_.refs_2_, bf16[960,1024]{1,0:T(8,128)(2,1)} %bitcast.95, bf16[960,1024]{1,0:T(8,128)(2,1)} %bitcast.125, ...), custom_call_target="tpu_custom_call" | custom-call | flops 1150000000 | bytes 3000000 | tf_op jit(solution)/shard_map/expert_second/pallas_call | solution.py:55
  208.0 5.0 all-to-all-start.2
  213.0 20.1 %dense_rest.1 = (f32[768,1024]{1,0:T(8,128)}, f32[768,1024]{1,0:T(8,128)}) custom-call(s32[4]{0:T(128)} %get-tuple-element.208.refs_0_, s32[4]{0:T(128)} %constant.36.clone.refs_1_, bf16[4,768,512]{2,1,0:T(8,128)(2,1)} %get-tuple-element.84.refs_7_.refs_2_, bf16[4,768,512]{2,1,0:T(8,128)(2,1)} %get-tuple-element.89.refs_2_.refs_3_, ...), custom_call_target="tpu_custom_call" | custom-call | flops 34500001792 | bytes 90000000 | tf_op jit(solution)/shard_map/dense_rest/pallas_call | solution.py:55
  241.8 9.2 %expert_grads.5 = (bf16[2,512,1024]{2,1,0:T(8,128)(2,1)}, bf16[2,512,1024]{2,1,0:T(8,128)(2,1)}) custom-call(s32[2]{0:T(128)} %get-tuple-element.207.refs_0_, s32[2]{0:T(128)} %get-tuple-element.205.refs_1_, bf16[960,1024]{1,0:T(8,128)(2,1)} %bitcast.96, bf16[4,960,512]{2,1,0:T(8,128)(2,1)} %get-tuple-element.108.refs_3_, ...), custom_call_target="tpu_custom_call" | custom-call | flops 80500000 | bytes 210000 | tf_op jit(solution)/shard_map/expert_grads/pallas_call | solution.py:55
  251.6 9.2 %expert_grads.6 = (bf16[2,512,1024]{2,1,0:T(8,128)(2,1)}, bf16[2,512,1024]{2,1,0:T(8,128)(2,1)}) custom-call(s32[2]{0:T(128)} %get-tuple-element.206.refs_0_, s32[2]{0:T(128)} %get-tuple-element.204.refs_1_, bf16[960,1024]{1,0:T(8,128)(2,1)} %bitcast.97, bf16[4,960,512]{2,1,0:T(8,128)(2,1)} %get-tuple-element.96.refs_3_, ...), custom_call_target="tpu_custom_call" | custom-call | flops 80500000 | bytes 210000 | tf_op jit(solution)/shard_map/expert_grads/pallas_call | solution.py:55
  283.3 9.7 %expert_grads.7 = (bf16[2,512,1024]{2,1,0:T(8,128)(2,1)}, bf16[2,512,1024]{2,1,0:T(8,128)(2,1)}) custom-call(s32[2]{0:T(128)} %get-tuple-element.206.refs_0_, s32[2]{0:T(128)} %get-tuple-element.204.refs_1_, bf16[960,1024]{1,0:T(8,128)(2,1)} %bitcast.98, bf16[4,960,512]{2,1,0:T(8,128)(2,1)} %get-tuple-element.108.refs_3_, ...), custom_call_target="tpu_custom_call" | custom-call | flops 80500000 | bytes 210000 | tf_op jit(solution)/shard_map/expert_grads/pallas_call | solution.py:55
  293.0 11.9 %between.1 = (bf16[768,1024]{1,0:T(8,128)(2,1)}, bf16[768,1024]{1,0:T(8,128)(2,1)}, f32[8,1024]{1,0:T(8,128)}) custom-call(s32[768,1]{1,0:T(8,128)} %fusion.9.refs_0_, bf16[960,1024]{1,0:T(8,128)(2,1)} %bitcast.20.refs_1_, f32[768,1024]{1,0:T(8,128)} %get-tuple-element.104.refs_2_, f32[768,1024]{1,0:T(8,128)} %get-tuple-element.105.refs_3_.refs_2_, ...), custom_call_target="tpu_custom_call" | custom-call | flops 138000000 | bytes 360000 | tf_op jit(solution)/shard_map/between/pallas_call | solution.py:55
  304.9 6.1 %rows_grad.2 = (bf16[4,4,32,1024]{3,2,1,0:T(8,128)(2,1)}, bf16[4,4,32,1024]{3,2,1,0:T(8,128)(2,1)}) custom-call(s32[4]{0:T(128)} %get-tuple-element.208.refs_0_, s32[4]{0:T(128)} %constant.36.clone.refs_1_, s32[1]{0:T(128)} %bitcast.1.refs_0_.refs_2_, bf16[1024,768]{1,0:T(8,128)(2,1)} %get-tuple-element.118.refs_3_, ...), custom_call_target="tpu_custom_call" | custom-call | flops 34500000 | bytes 90000 | tf_op jit(solution)/shard_map/rows_grad/pallas_call | solution.py:55
  311.0 28.4 %attend_back.1 = (bf16[3,768,1024]{2,1,0:T(8,128)(2,1)}, bf16[3,1024,768]{2,1,0:T(8,128)(2,1)}) custom-call(f32[768,1]{1,0:T(8,128)} %broadcast_in_dim.60.refs_0_, f32[8,8,768]{2,1,0:T(8,128)} %get-tuple-element.122.refs_1_, bf16[768,3072]{1,0:T(8,128)(2,1)} %get-tuple-element.75.refs_1_.refs_2_.refs_3_.refs_4_, ...), custom_call_target="tpu_custom_call" | custom-call | flops 322000000 | bytes 840000 | tf_op jit(solution)/shard_map/attend_back/pallas_call | solution.py:55
  339.4 8.6 %collective-permute-done.14.refs_2_ = bf16[1,512,1024]{2,1,0:T(8,128)(2,1)} collective-permute-done((bf16[1,512,1024]{2,1,0:T(8,128)(2,1)S(1)}, bf16[1,512,1024]{2,1,0:T(8,128)(2,1)}, u32[]{:S(2)}, u32[]{:S(2)}) %collective-permute-start.14) | collective-permute-done | bytes 1048608 | tf_op jit(solution)/shard_map/ppermute | solution.py:806
  359.0 5.1 %all-to-all-start.3 = ((bf16[8,120,1024]{2,1,0:T(8,128)(2,1)}), bf16[8,120,1024]{2,1,0:T(8,128)(2,1)}, u32[]{:S(2)}, u32[]{:S(2)}) async-start(bf16[8,120,1024]{2,1,0:T(8,128)(2,1)} %bitcast.34), calls=%async_computation.3 | async-start | bytes 3932160 | tf_op jit(solution)/shard_map/all_to_all | solution.py:979
  370.1 11.5 %first_back.1 = (bf16[768,1024]{1,0:T(8,128)(2,1)}, f32[8,1024]{1,0:T(8,128)}) custom-call(bf16[3,768,1024]{2,1,0:T(8,128)(2,1)} %get-tuple-element.125.refs_3_.refs_0_, bf16[1024,3072]{1,0:T(8,128)(2,1)} %refs_1_.6, bf16[768,1024]{1,0:T(8,128)(2,1)} %refs_2_.1, bf16[768,1024]{1,0:T(8,128)(2,1)} %get-tuple-element.119.refs_4_.refs_5_.refs_3_, ...), custom_call_target="tpu_custom_call" | custom-call | flops 138000000 | bytes 360000 | tf_op jit(solution)/shard_map/first_back/pallas_call | solution.py:55
  384.6 10.1 %rows_grad.3 = (bf16[4,4,112,512]{3,2,1,0:T(8,128)(2,1)}, bf16[4,4,96,512]{3,2,1,0:T(8,128)(2,1)}, bf16[4,4,112,512]{3,2,1,0:T(8,128)(2,1)}, bf16[4,4,96,512]{3,2,1,0:T(8,128)(2,1)}) custom-call(s32[4]{0:T(128)} %get-tuple-element.208.refs_0_, s32[4]{0:T(128)} %constant.36.clone.refs_1_, s32[1]{0:T(128)} %bitcast.1.refs_0_.refs_2_, ...), custom_call_target="tpu_custom_call" | custom-call | flops 80500000 | bytes 210000 | tf_op jit(solution)/shard_map/rows_grad/pallas_call | solution.py:55
  395.1 6.7 %up_final.1.refs_4_ = f32[1024,1024]{1,0:T(8,128)} custom-call(bf16[1,512,1024]{2,1,0:T(8,128)(2,1)} %add_terms.29.refs_3_.refs_0_, bf16[2,512,1024]{2,1,0:T(8,128)(2,1)} %get-tuple-element.115.refs_11_.refs_0_.refs_1_, bf16[2,512,1024]{2,1,0:T(8,128)(2,1)} %collective-permute-done.12.refs_1_.refs_2_, bf16[1,512,1024]{2,1,0:T(8,128)(2,1)} %collective-permute-done.18.refs_3_, ...), custom_call_target="tpu_custom_call" | custom-call | flops 11500000256 | bytes 30000000 | tf_op jit(solution)/shard_map/up_final/pallas_call | solution.py:55
  401.8 4.7 down_final.1
  419.1 8.1 %all-to-all-done.3 = bf16[8,120,1024]{2,1,0:T(8,128)(2,1)} async-done(((bf16[8,120,1024]{2,1,0:T(8,128)(2,1)}), bf16[8,120,1024]{2,1,0:T(8,128)(2,1)}, u32[]{:S(2)}, u32[]{:S(2)}) %all-to-all-start.3) | async-done | bytes 1966112 | tf_op jit(solution)/shard_map/all_to_all | solution.py:979
  427.2 6.9 %outputs.1.refs_3_ = bf16[768,1024]{1,0:T(8,128)(2,1)} custom-call(s32[768,1]{1,0:T(8,128)} %fusion.9.refs_0_, bf16[960,1024]{1,0:T(8,128)(2,1)} %bitcast.35.refs_1_, f32[768,1024]{1,0:T(8,128)} %get-tuple-element.105.refs_3_.refs_2_, f32[768,1024]{1,0:T(8,128)} %get-tuple-element.106.refs_4_.refs_3_, f32[768,128]{1,0:T(8,128)} %get-tuple-element.107.refs_5_.refs_4_, ...), custom_call_target="tpu_custom_call" | custom-call | flops 80500000 | bytes 210000 | tf_op jit(solution)/shard_map/outputs/pallas_call | solution.py:55
  449.1 6.2 %collective-permute-done.24.refs_11_ = bf16[1,4,32,1024]{3,2,1,0:T(8,128)(2,1)S(1)} collective-permute-done((bf16[1,4,32,1024]{3,2,1,0:T(8,128)(2,1)}, bf16[1,4,32,1024]{3,2,1,0:T(8,128)(2,1)S(1)}, u32[]{:S(2)}, u32[]{:S(2)}) %collective-permute-start.24) | collective-permute-done | bytes 262176 | tf_op jit(solution)/shard_map/ppermute | solution.py:806
  465.7 11.5 %collective-permute-done.25.refs_1_ = bf16[2,144,1024]{2,1,0:T(8,128)(2,1)S(1)} collective-permute-done((bf16[2,144,1024]{2,1,0:T(8,128)(2,1)}, bf16[2,144,1024]{2,1,0:T(8,128)(2,1)S(1)}, u32[]{:S(2)}, u32[]{:S(2)}) %collective-permute-start.25) | collective-permute-done | bytes 589856 | tf_op jit(solution)/shard_map/ppermute | solution.py:806
  482.0 11.4 %collective-permute-done.26.refs_2_ = bf16[1,144,1024]{2,1,0:T(8,128)(2,1)S(1)} collective-permute-done((bf16[1,144,1024]{2,1,0:T(8,128)(2,1)}, bf16[1,144,1024]{2,1,0:T(8,128)(2,1)S(1)}, u32[]{:S(2)}, u32[]{:S(2)}) %collective-permute-start.26) | collective-permute-done | bytes 294944 | tf_op jit(solution)/shard_map/ppermute | solution.py:806
  (183 shorter events, 121.7 us)
Async XLA Ops:
  14.4 52.7 %all-to-all-start = ((bf16[8,120,1024]{2,1,0:T(8,128)(2,1)}), bf16[8,120,1024]{2,1,0:T(8,128)(2,1)S(1)}, u32[]{:S(2)}, u32[]{:S(2)}) async-start(bf16[8,120,1024]{2,1,0:T(8,128)(2,1)} %bitcast.2), calls=%async_computation | async-start | bytes 3932160 | tf_op jit(solution)/shard_map/all_to_all | solution.py:979
  72.3 66.0 %all-to-all-start.1 = ((bf16[8,120,1024]{2,1,0:T(8,128)(2,1)}), bf16[8,120,1024]{2,1,0:T(8,128)(2,1)S(1)}, u32[]{:S(2)}, u32[]{:S(2)}) async-start(bf16[8,120,1024]{2,1,0:T(8,128)(2,1)} %bitcast.123), calls=%async_computation.1 | async-start | bytes 3932160 | tf_op jit(solution)/shard_map/all_to_all | solution.py:979
  100.6 26.1 %collective-permute-start.1 = (bf16[2,4,2,128,512]{4,3,2,1,0:T(8,128)(2,1)}, bf16[2,4,2,128,512]{4,3,2,1,0:T(8,128)(2,1)}, u32[]{:S(2)}, u32[]{:S(2)}) collective-permute-start(bf16[2,4,2,128,512]{4,3,2,1,0:T(8,128)(2,1)} %get-tuple-element.88), channel_id=1, source_target_pairs={{0,1},{1,0},{2,3},{3,2},{4,5},{5,4},{6,7},{7,6},{8,9},{9,8},{10,11... | collective-permute-start | bytes 6291464 | tf_op jit(solution)/shard_map/ppermute | solution.py:806
  123.8 8.6 %collective-permute-start = (bf16[2,4,2,128,512]{4,3,2,1,0:T(8,128)(2,1)}, bf16[2,4,2,128,512]{4,3,2,1,0:T(8,128)(2,1)}, u32[]{:S(2)}, u32[]{:S(2)}) collective-permute-start(bf16[2,4,2,128,512]{4,3,2,1,0:T(8,128)(2,1)} %get-tuple-element.86), channel_id=1, source_target_pairs={{0,1},{1,0},{2,3},{3,2},{4,5},{5,4},{6,7},{7,6},{8,9},{9,8},{10,11... | collective-permute-start | bytes 6291464 | tf_op jit(solution)/shard_map/ppermute | solution.py:806
  123.9 14.4 %collective-permute-start.3 = (bf16[2,4,2,128,512]{4,3,2,1,0:T(8,128)(2,1)}, bf16[2,4,2,128,512]{4,3,2,1,0:T(8,128)(2,1)}, u32[]{:S(2)}, u32[]{:S(2)}) collective-permute-start(bf16[2,4,2,128,512]{4,3,2,1,0:T(8,128)(2,1)} %get-tuple-element.91), channel_id=1, source_target_pairs={{0,1},{1,0},{2,3},{3,2},{4,5},{5,4},{6,7},{7,6},{8,9},{9,8},{10,11... | collective-permute-start | bytes 6291464 | tf_op jit(solution)/shard_map/ppermute | solution.py:806
  124.4 13.9 %collective-permute-start.2 = (bf16[2,4,2,128,512]{4,3,2,1,0:T(8,128)(2,1)}, bf16[2,4,2,128,512]{4,3,2,1,0:T(8,128)(2,1)}, u32[]{:S(2)}, u32[]{:S(2)}) collective-permute-start(bf16[2,4,2,128,512]{4,3,2,1,0:T(8,128)(2,1)} %get-tuple-element.90), channel_id=1, source_target_pairs={{0,1},{1,0},{2,3},{3,2},{4,5},{5,4},{6,7},{7,6},{8,9},{9,8},{10,11... | collective-permute-start | bytes 6291464 | tf_op jit(solution)/shard_map/ppermute | solution.py:806
  130.9 102.2 %collective-permute-start.5 = (bf16[2,4,2,128,512]{4,3,2,1,0:T(8,128)(2,1)}, bf16[2,4,2,128,512]{4,3,2,1,0:T(8,128)(2,1)}, u32[]{:S(2)}, u32[]{:S(2)}) collective-permute-start(bf16[2,4,2,128,512]{4,3,2,1,0:T(8,128)(2,1)} %bitcast.121), channel_id=1, source_target_pairs={{0,16},{8,24},{16,0},{24,8},{1,17},{9,25},{17,1},{25,9},{2,18},{10... | collective-permute-start | bytes 6291464 | tf_op jit(solution)/shard_map/ppermute | solution.py:806
  136.8 100.7 %collective-permute-start.4 = (bf16[2,4,2,128,512]{4,3,2,1,0:T(8,128)(2,1)}, bf16[2,4,2,128,512]{4,3,2,1,0:T(8,128)(2,1)}, u32[]{:S(2)}, u32[]{:S(2)}) collective-permute-start(bf16[2,4,2,128,512]{4,3,2,1,0:T(8,128)(2,1)} %bitcast.142), channel_id=1, source_target_pairs={{0,8},{8,0},{16,24},{24,16},{1,9},{9,1},{17,25},{25,17},{2,10},{10... | collective-permute-start | bytes 6291464 | tf_op jit(solution)/shard_map/ppermute | solution.py:806
  176.6 84.2 %collective-permute-start.9 = (bf16[2,512,1024]{2,1,0:T(8,128)(2,1)}, bf16[2,512,1024]{2,1,0:T(8,128)(2,1)}, u32[]{:S(2)}, u32[]{:S(2)}) collective-permute-start(bf16[2,512,1024]{2,1,0:T(8,128)(2,1)} %get-tuple-element.98.refs_10_), channel_id=1, source_target_pairs={{0,16},{8,24},{16,0},{24,8},{1,17},{9,25},{17,1},{25,9},{2,18},{10... | collective-permute-start | bytes 6291464 | tf_op jit(solution)/shard_map/ppermute | solution.py:806
  177.1 86.1 %collective-permute-start.8 = (bf16[2,512,1024]{2,1,0:T(8,128)(2,1)}, bf16[2,512,1024]{2,1,0:T(8,128)(2,1)S(1)}, u32[]{:S(2)}, u32[]{:S(2)}) collective-permute-start(bf16[2,512,1024]{2,1,0:T(8,128)(2,1)} %get-tuple-element.113), channel_id=1, source_target_pairs={{0,8},{8,0},{16,24},{24,16},{1,9},{9,1},{17,25},{25,17},{2,10},{10... | collective-permute-start | bytes 6291464 | tf_op jit(solution)/shard_map/ppermute | solution.py:806
  208.0 85.0 %all-to-all-start.2 = ((bf16[8,120,1024]{2,1,0:T(8,128)(2,1)}), bf16[8,120,1024]{2,1,0:T(8,128)(2,1)}, u32[]{:S(2)}, u32[]{:S(2)}) async-start(bf16[8,120,1024]{2,1,0:T(8,128)(2,1)} %bitcast.147), calls=%async_computation.2 | async-start | bytes 3932160 | tf_op jit(solution)/shard_map/all_to_all | solution.py:979
  213.0 250.7 %reduce-scatter.5.cloned.1.call-start = ((), (), s32[]{:S(2)}) async-start(), calls=%async_computation.7 | async-start | bytes 1310720 | tf_op jit(solution)/shard_map/reduce_scatter | solution.py:1055
  236.0 31.0 %collective-permute-start.7 = (bf16[1,4,2,128,512]{4,3,2,1,0:T(8,128)(2,1)}, bf16[1,4,2,128,512]{4,3,2,1,0:T(8,128)(2,1)S(1)}, u32[]{:S(2)}, u32[]{:S(2)}) collective-permute-start(bf16[1,4,2,128,512]{4,3,2,1,0:T(8,128)(2,1)} %bitcast.129), channel_id=1, source_target_pairs={{0,8},{8,0},{16,24},{24,16},{1,9},{9,1},{17,25},{25,17},{2,10},{10... | collective-permute-start | bytes 3145736 | tf_op jit(solution)/shard_map/ppermute | solution.py:806
  240.3 30.9 %collective-permute-start.6 = (bf16[1,4,2,128,512]{4,3,2,1,0:T(8,128)(2,1)}, bf16[1,4,2,128,512]{4,3,2,1,0:T(8,128)(2,1)S(1)}, u32[]{:S(2)}, u32[]{:S(2)}) collective-permute-start(bf16[1,4,2,128,512]{4,3,2,1,0:T(8,128)(2,1)} %bitcast.131), channel_id=1, source_target_pairs={{0,16},{8,24},{16,0},{24,8},{1,17},{9,25},{17,1},{25,9},{2,18},{10... | collective-permute-start | bytes 3145736 | tf_op jit(solution)/shard_map/ppermute | solution.py:806
  251.1 103.5 %collective-permute-start.12 = (bf16[2,512,1024]{2,1,0:T(8,128)(2,1)}, bf16[2,512,1024]{2,1,0:T(8,128)(2,1)}, u32[]{:S(2)}, u32[]{:S(2)}) collective-permute-start(bf16[2,512,1024]{2,1,0:T(8,128)(2,1)} %get-tuple-element.111.refs_6_), channel_id=1, source_target_pairs={{0,16},{8,24},{16,0},{24,8},{1,17},{9,25},{17,1},{25,9},{2,18},{10... | collective-permute-start | bytes 6291464 | tf_op jit(solution)/shard_map/ppermute | solution.py:806
  277.9 186.8 %reduce-scatter.3.cloned.1.call-start = ((), (), s32[]{:S(2)}) async-start(), calls=%async_computation.6 | async-start | bytes 1310720 | tf_op jit(solution)/shard_map/reduce_scatter | solution.py:1055
  277.9 88.2 %collective-permute-start.11 = (bf16[2,512,1024]{2,1,0:T(8,128)(2,1)}, bf16[2,512,1024]{2,1,0:T(8,128)(2,1)}, u32[]{:S(2)}, u32[]{:S(2)}) collective-permute-start(bf16[2,512,1024]{2,1,0:T(8,128)(2,1)} %get-tuple-element.127), channel_id=1, source_target_pairs={{0,8},{8,0},{16,24},{24,16},{1,9},{9,1},{17,25},{25,17},{2,10},{10... | collective-permute-start | bytes 6291464 | tf_op jit(solution)/shard_map/ppermute | solution.py:806
  278.5 69.4 %collective-permute-start.14 = (bf16[1,512,1024]{2,1,0:T(8,128)(2,1)S(1)}, bf16[1,512,1024]{2,1,0:T(8,128)(2,1)}, u32[]{:S(2)}, u32[]{:S(2)}) collective-permute-start(bf16[1,512,1024]{2,1,0:T(8,128)(2,1)S(1)} %copy-done.7), channel_id=1, source_target_pairs={{0,8},{8,0},{16,24},{24,16},{1,9},{9,1},{17,25},{25,17},{2,10},{10... | collective-permute-start | bytes 3145736 | tf_op jit(solution)/shard_map/ppermute | solution.py:806
  280.0 70.7 %collective-permute-start.13 = (bf16[1,512,1024]{2,1,0:T(8,128)(2,1)S(1)}, bf16[1,512,1024]{2,1,0:T(8,128)(2,1)S(1)}, u32[]{:S(2)}, u32[]{:S(2)}) collective-permute-start(bf16[1,512,1024]{2,1,0:T(8,128)(2,1)S(1)} %copy-done.6), channel_id=1, source_target_pairs={{0,16},{8,24},{16,0},{24,8},{1,17},{9,25},{17,1},{25,9},{2,18},{10... | collective-permute-start | bytes 3145736 | tf_op jit(solution)/shard_map/ppermute | solution.py:806
  357.1 38.0 %collective-permute-start.18 = (bf16[1,512,1024]{2,1,0:T(8,128)(2,1)}, bf16[1,512,1024]{2,1,0:T(8,128)(2,1)}, u32[]{:S(2)}, u32[]{:S(2)}) collective-permute-start(bf16[1,512,1024]{2,1,0:T(8,128)(2,1)} %add_terms.31.refs_2_), channel_id=1, source_target_pairs={{0,8},{8,0},{16,24},{24,16},{1,9},{9,1},{17,25},{25,17},{2,10},{10... | collective-permute-start | bytes 3145736 | tf_op jit(solution)/shard_map/ppermute | solution.py:806
  359.0 68.3 %all-to-all-start.3 = ((bf16[8,120,1024]{2,1,0:T(8,128)(2,1)}), bf16[8,120,1024]{2,1,0:T(8,128)(2,1)}, u32[]{:S(2)}, u32[]{:S(2)}) async-start(bf16[8,120,1024]{2,1,0:T(8,128)(2,1)} %bitcast.34), calls=%async_computation.3 | async-start | bytes 3932160 | tf_op jit(solution)/shard_map/all_to_all | solution.py:979
  365.6 50.0 %collective-permute-start.10 = (bf16[4,4,32,1024]{3,2,1,0:T(8,128)(2,1)S(1)}, bf16[4,4,32,1024]{3,2,1,0:T(8,128)(2,1)}, u32[]{:S(2)}, u32[]{:S(2)}) collective-permute-start(bf16[4,4,32,1024]{3,2,1,0:T(8,128)(2,1)S(1)} %copy-done.12), channel_id=1, source_target_pairs={{0,1},{1,0},{2,3},{3,2},{4,5},{5,4},{6,7},{7,6},{8,9},{9,8},{10,11... | collective-permute-start | bytes 3145736 | tf_op jit(solution)/shard_map/ppermute | solution.py:806
  368.6 33.2 %collective-permute-start.17 = (bf16[1,512,1024]{2,1,0:T(8,128)(2,1)}, bf16[1,512,1024]{2,1,0:T(8,128)(2,1)}, u32[]{:S(2)}, u32[]{:S(2)}) collective-permute-start(bf16[1,512,1024]{2,1,0:T(8,128)(2,1)} %add_terms.32.refs_5_), channel_id=1, source_target_pairs={{0,16},{8,24},{16,0},{24,8},{1,17},{9,25},{17,1},{25,9},{2,18},{10... | collective-permute-start | bytes 3145736 | tf_op jit(solution)/shard_map/ppermute | solution.py:806
  394.6 12.0 %collective-permute-start.16 = (bf16[4,4,112,512]{3,2,1,0:T(8,128)(2,1)}, bf16[4,4,112,512]{3,2,1,0:T(8,128)(2,1)S(1)}, u32[]{:S(2)}, u32[]{:S(2)}) collective-permute-start(bf16[4,4,112,512]{3,2,1,0:T(8,128)(2,1)} %get-tuple-element.135.refs_4_), channel_id=1, source_target_pairs={{0,1},{1,0},{2,3},{3,2},{4,5},{5,4},{6,7},{7,6},{8,9},{9,8},{10,11... | collective-permute-start | bytes 5505032 | tf_op jit(solution)/shard_map/ppermute | solution.py:806
  394.6 16.1 %collective-permute-start.15 = (bf16[4,4,96,512]{3,2,1,0:T(8,128)(2,1)}, bf16[4,4,96,512]{3,2,1,0:T(8,128)(2,1)S(1)}, u32[]{:S(2)}, u32[]{:S(2)}) collective-permute-start(bf16[4,4,96,512]{3,2,1,0:T(8,128)(2,1)} %get-tuple-element.133), channel_id=1, source_target_pairs={{0,1},{1,0},{2,3},{3,2},{4,5},{5,4},{6,7},{7,6},{8,9},{9,8},{10,11... | collective-permute-start | bytes 4718600 | tf_op jit(solution)/shard_map/ppermute | solution.py:806
  410.2 23.9 %collective-permute-start.19 = (bf16[2,4,112,512]{3,2,1,0:T(8,128)(2,1)}, bf16[2,4,112,512]{3,2,1,0:T(8,128)(2,1)S(1)}, u32[]{:S(2)}, u32[]{:S(2)}) collective-permute-start(bf16[2,4,112,512]{3,2,1,0:T(8,128)(2,1)} %bitcast.133), channel_id=1, source_target_pairs={{0,16},{8,24},{16,0},{24,8},{1,17},{9,25},{17,1},{25,9},{2,18},{10... | collective-permute-start | bytes 2752520 | tf_op jit(solution)/shard_map/ppermute | solution.py:806
  414.1 24.8 %collective-permute-start.21 = (bf16[2,4,96,512]{3,2,1,0:T(8,128)(2,1)}, bf16[2,4,96,512]{3,2,1,0:T(8,128)(2,1)S(1)}, u32[]{:S(2)}, u32[]{:S(2)}) collective-permute-start(bf16[2,4,96,512]{3,2,1,0:T(8,128)(2,1)} %bitcast.136), channel_id=1, source_target_pairs={{0,8},{8,0},{16,24},{24,16},{1,9},{9,1},{17,25},{25,17},{2,10},{10... | collective-permute-start | bytes 2359304 | tf_op jit(solution)/shard_map/ppermute | solution.py:806
  417.6 26.4 %collective-permute-start.23 = (bf16[2,4,32,1024]{3,2,1,0:T(8,128)(2,1)}, bf16[2,4,32,1024]{3,2,1,0:T(8,128)(2,1)S(1)}, u32[]{:S(2)}, u32[]{:S(2)}) collective-permute-start(bf16[2,4,32,1024]{3,2,1,0:T(8,128)(2,1)} %bitcast.140), channel_id=1, source_target_pairs={{0,16},{8,24},{16,0},{24,8},{1,17},{9,25},{17,1},{25,9},{2,18},{10... | collective-permute-start | bytes 1572872 | tf_op jit(solution)/shard_map/ppermute | solution.py:806
  437.3 17.9 %collective-permute-start.20 = (bf16[1,4,112,512]{3,2,1,0:T(8,128)(2,1)}, bf16[1,4,112,512]{3,2,1,0:T(8,128)(2,1)S(1)}, u32[]{:S(2)}, u32[]{:S(2)}) collective-permute-start(bf16[1,4,112,512]{3,2,1,0:T(8,128)(2,1)} %bitcast.148), channel_id=1, source_target_pairs={{0,8},{8,0},{16,24},{24,16},{1,9},{9,1},{17,25},{25,17},{2,10},{10... | collective-permute-start | bytes 1376264 | tf_op jit(solution)/shard_map/ppermute | solution.py:806
  441.9 13.4 %collective-permute-start.22 = (bf16[1,4,96,512]{3,2,1,0:T(8,128)(2,1)}, bf16[1,4,96,512]{3,2,1,0:T(8,128)(2,1)S(1)}, u32[]{:S(2)}, u32[]{:S(2)}) collective-permute-start(bf16[1,4,96,512]{3,2,1,0:T(8,128)(2,1)} %bitcast.150), channel_id=1, source_target_pairs={{0,16},{8,24},{16,0},{24,8},{1,17},{9,25},{17,1},{25,9},{2,18},{10... | collective-permute-start | bytes 1179656 | tf_op jit(solution)/shard_map/ppermute | solution.py:806
  462.9 14.3 %collective-permute-start.25 = (bf16[2,144,1024]{2,1,0:T(8,128)(2,1)}, bf16[2,144,1024]{2,1,0:T(8,128)(2,1)S(1)}, u32[]{:S(2)}, u32[]{:S(2)}) collective-permute-start(bf16[2,144,1024]{2,1,0:T(8,128)(2,1)} %add_terms.39.refs_2_), channel_id=1, source_target_pairs={{0,2},{1,3},{2,0},{3,1},{4,6},{5,7},{6,4},{7,5},{8,10},{9,11},{10,... | collective-permute-start | bytes 1769480 | tf_op jit(solution)/shard_map/ppermute | solution.py:806
  479.9 13.5 %collective-permute-start.26 = (bf16[1,144,1024]{2,1,0:T(8,128)(2,1)}, bf16[1,144,1024]{2,1,0:T(8,128)(2,1)S(1)}, u32[]{:S(2)}, u32[]{:S(2)}) collective-permute-start(bf16[1,144,1024]{2,1,0:T(8,128)(2,1)} %add_terms.40.refs_3_), channel_id=1, source_target_pairs={{0,4},{1,5},{2,6},{3,7},{4,0},{5,1},{6,2},{7,3},{8,12},{9,13},{10,... | collective-permute-start | bytes 884744 | tf_op jit(solution)/shard_map/ppermute | solution.py:806
  (30 other events, 150.1 us)
Sparse Core Ops, SparseCore 0:
  278.0 27.6 reduce-scatter.4
  359.1 44.1 reduce-scatter.2

commit v3 on v2

--- a/solution.py
+++ b/solution.py
@@ -13,9 +13,12 @@
 ROW_BLOCK = 256
 CHUNKS = 2
 WEIGHT = 0.01
+EXPERT_PARTS = 1
+DENSE_BLOCK = 256
 LANES = 128
 GELU_ROOT = 0.7978845608028654
 GELU_CUBE = 0.044715
+LOG2_E = 1.4426950408889634
 
 f32 = jnp.float32
 bf16 = jnp.bfloat16
@@ -63,7 +66,7 @@
             ),
             out_shape=out_shape,
             compiler_params=pltpu.CompilerParams(
-                dimension_semantics=("arbitrary",) * len(grid), vmem_limit_bytes=56 * 1024 * 1024
+                dimension_semantics=("arbitrary",) * len(grid), vmem_limit_bytes=63 * 1024 * 1024
             ),
             cost_estimate=pl.CostEstimate(
                 flops=int(micros * WEIGHT * 1.15e9),
@@ -128,7 +131,7 @@
 def ln_qkv(tokens, gain, bias, weight):
     rows, d = tokens.shape
     width = weight.shape[1]
-    block = 512
+    block = 1024
     return call(
         ln_qkv_kernel,
         (width // block,),
@@ -166,7 +169,7 @@
     for i in range(rows // ROW_BLOCK):
         low, high = i * ROW_BLOCK, (i + 1) * ROW_BLOCK
         edge = diagonal_bias(bias_ref[low:high, :])
-        q = q_ref[low:high, :] * jnp.asarray(HEAD_DIM**-0.5, bf16)
+        q = (q_ref[low:high, :].astype(f32) * (HEAD_DIM**-0.5 * LOG2_E)).astype(bf16)
         sides = []
         for head in range(2):
             q_head = head_lanes(q, head)
@@ -175,16 +178,16 @@
             if i:
                 outer = dot_nt(k_ref[:low, :], q_head) + bias_ref[:low, :]
                 top = jnp.maximum(top, jnp.max(outer, axis=0, keepdims=True))
-            inner = jnp.exp(inner - top)
+            inner = jnp.exp2(inner - top)
             total = jnp.sum(inner, axis=0, keepdims=True)
             v_head = v_t[head * HEAD_DIM : (head + 1) * HEAD_DIM, :]
             side = dot_nn(v_head[:, low:high], inner.astype(bf16))
             if i:
-                outer = jnp.exp(outer - top)
+                outer = jnp.exp2(outer - top)
                 total = total + jnp.sum(outer, axis=0, keepdims=True)
                 side = side + dot_nn(v_head[:, :low], outer.astype(bf16))
             sides.append(side / total)
-            lse_ref[0, head : head + 1, low:high] = top + jnp.log(total)
+            lse_ref[0, head : head + 1, low:high] = top + jnp.log2(total)
         both = jnp.concatenate(sides, axis=0)
         ctx_t_ref[:, low:high] = both.astype(bf16)
         ctx_ref[low:high, :] = both.T.astype(bf16)
@@ -228,10 +231,12 @@
         low, high = i * ROW_BLOCK, (i + 1) * ROW_BLOCK
         edge = diagonal_bias(bias_ref[low:high, :])
         q = q_ref[low:high, :] * jnp.asarray(scale, bf16)
+        raised = (q_ref[low:high, :].astype(f32) * (scale * LOG2_E)).astype(bf16)
         do = do_ref[low:high, :]
         sides = []
         for head in range(2):
             q_head = head_lanes(q, head)
+            raised_head = head_lanes(raised, head)
             do_head = head_lanes(do, head)
             lse = lse_ref[0, head : head + 1, low:high]
             spans = [(low, high, edge)]
@@ -240,7 +245,7 @@
             probs, grads = [], []
             dots = 0.0
             for start, stop, bias in spans:
-                p = jnp.exp(dot_nt(k_ref[start:stop, :], q_head) + bias - lse)
+                p = jnp.exp2(dot_nt(k_ref[start:stop, :], raised_head) + bias - lse)
                 gp = dot_nt(v_ref[start:stop, :], do_head)
                 dots = dots + jnp.sum(p * gp, axis=0, keepdims=True)
                 probs.append(p)
@@ -348,8 +353,8 @@
     rows = second_ref.shape[0]
     half = second_t_ref.shape[0] // 2
     levels = keep_ref.shape[1]
-    for low in range(0, rows, ROW_BLOCK):
-        at = slice(low, low + ROW_BLOCK)
+    for low in range(0, rows, DENSE_BLOCK):
+        at = slice(low, low + DENSE_BLOCK)
         value, slope = gelu_pair(dot_nn(second_ref[at, :], up_ref[...]))
         hidden_ref[0, at, :] = value.astype(bf16)
         gpre_ref[0, at, :] = (dot_nt(gdl_ref[at, :], down_ref[...]) * slope).astype(bf16)
@@ -455,7 +460,7 @@
 
 def expert_step(arr_ref, garr_ref, up_ref, down_ref, hidden_ref, gpre_ref, out_acc, gin_acc):
     rows = arr_ref.shape[0]
-    step = rows // 3
+    step = rows // EXPERT_PARTS
     for low in range(0, rows, step):
         at = slice(low, low + step)
         value, slope = gelu_pair(dot_nn(arr_ref[at, :], up_ref[...]))
@@ -472,7 +477,7 @@
     hidden_ref, gpre_ref, garr_ref, logit_ref, out_acc, gin_acc,
 ):
     rows = arr_ref.shape[0]
-    step = rows // 3
+    step = rows // EXPERT_PARTS
 
     @pl.when(pl.program_id(0) == 0)
     def _():
@@ -493,7 +498,7 @@
     grad_ref, hidden_ref, gpre_ref, sent_ref, gin_ref, gate_grad_ref, out_acc, gin_acc,
 ):
     rows = arr_ref.shape[0]
-    step = rows // 3
+    step = rows // EXPERT_PARTS
     me = me_ref[0]
 
     @pl.when(pl.program_id(0) == 0)
@@ -632,7 +637,7 @@
         ],
         block,
         shape_of((rows, d), bf16),
-        micros=7,
+        micros=1000,
         name="outputs",
     )(target, back, do, middle, mixing)
 
@@ -738,7 +743,7 @@
         [pl.BlockSpec((1, block, width), lambda i, r: (0, r, i))] * len(terms),
         pl.BlockSpec((block, 2 * width), lambda i, r: (i * (width // block) + r, 0)),
         shape_of((d, 2 * width), f32),
-        micros=1000,
+        micros=7,
         name="up_final",
     )(*terms)
 
@@ -752,7 +757,7 @@
         [pl.BlockSpec((1, block, d), lambda r: (0, r, 0))] * len(terms),
         pl.BlockSpec((2, block, d), lambda r: (0, r, 0)),
         shape_of((2, width, d), f32),
-        micros=1000,
+        micros=7,
         name="down_final",
     )(*terms).reshape(2 * width, d)
 
@@ -1034,12 +1039,11 @@
     got0 = swapped(expert_part(True, gpre0, hidden0))
     hidden1, gpre1, sent, gin, gate_grad = run(expert, arriving, 1, *given, [garr, *before])
     grad_back = exchange(gin)
+    Line.others = tuple(side.terms[-1] for side in sums)
     dense_out, grad_second = run(
         dense_rest, parts[0][0], owners, back_order, parts[1][0], parts[0][1], parts[1][1], up_weight,
         down_weight,
     )
-    for side in sums:
-        side.step()
     got1 = swapped(expert_part(True, gpre1, hidden1))
 
     def halvings(keeps, gots):
@@ -1051,12 +1055,6 @@
     halves0 = halvings(expert_part(False, gpre0, hidden0), got0)
     for side in halves0:
         side.step()
-    pieces = [
-        lax.psum_scatter(
-            side.finish(bf16), "ep", scatter_dimension=0, axis_index_groups=level_groups
-        )
-        for side in sums
-    ]
     halves1 = halvings(expert_part(False, gpre1, hidden1), got1)
     gatt, grad_context, sums2 = run(
         between, grad_second, target_column, grad_back, dense_out, middle, mixing, cotangent,
@@ -1080,9 +1078,16 @@
     (out_side,) = own_rows(context_t, gatt, [up_bits], 3)
     grad_qkv, grad_qkv_t = run(attend_back, qkv, bias, lse, grad_context)
     done0 = [side.finish(bf16)[None] for side in halves0]
-    for side in halves1:
+    for side in sums + halves1:
         side.step()
     grad_inputs, sums1 = run(first_back, grad_qkv, qkv_weight, tokens, gatt, norm1_gain[None])
+    pieces = [
+        lax.psum_scatter(
+            side.finish(bf16).reshape(d, -1), "ep", scatter_dimension=0,
+            axis_index_groups=level_groups, tiled=True,
+        ).reshape(2, d // groups, -1)
+        for side in sums
+    ]
     home_mix = jnp.concatenate(
         [jnp.zeros((experts, d), f32), sums2[2:3], -sums2[2:3]], axis=0
     )
@@ -1097,14 +1102,15 @@
     qkv_sides = own_rows(
         grad_qkv_t.reshape(3 * d, rows), first, [up_bits, down_bits], 7, small
     )
+    Line.others = tuple(side.terms[-1] for side in halves1)
+    outputs = run(outputs_of, dense_out, target_column, expert_back, middle, mixing)
+    for side in qkv_sides:
+        side.step()
+    out_side.step()
     expert_up_sum, expert_down_sum = [
         run(final, first_half, *second_half.terms)
         for final, first_half, second_half in zip((up_final, down_final), done0, halves1)
     ]
-    for side in qkv_sides:
-        side.step()
-    out_side.step()
-    outputs = run(outputs_of, dense_out, target_column, expert_back, middle, mixing)
     for side in qkv_sides:
         side.step()
     out_side.step()

time: 518 us -> 494 us (0.954)
  local copies, waits for them, and re-layouts: 32.1 us -> 21.9 us
  waiting for transfers between devices: 47.2 us -> 41.9 us
    unnamed x60 -> x32, local copies, waits for them, and re-layouts: 15.7 us -> 6.53 us
    all_to_all x4, waiting for transfers between devices: 8.85 us -> 1.79 us  [exchange(): lax.all_to_all(values.reshape(groups, slots // groups, d), 'ep', 0, 0, ti...]
    pallas_call x42, Pallas kernels: 350 us -> 345 us  [apply(): pl.pallas_call(ordered, grid_spec=pltpu.PrefetchScalarGridSpec(num_scalar...]
  transfers between devices with their start and end apart: 33 -> 33, of which waited for: 7 -> 10; matrix products, arithmetic and copies ran while one was open for 4% -> 3% of each run, Pallas kernels for 68% -> 71%
where the time goes in v3:
time: 494 us; the launch traced here: 486 us
  Pallas kernels  345 us (70%)
  starting transfers between devices  46.2 us (9%)
  waiting for transfers between devices  41.9 us (8%)
  local copies, waits for them, and re-layouts  21.9 us (4%)
  between operations  15.1 us (3%)
  matrix products  9.14 us (2%)
  other arithmetic  6.86 us (1%)
    pallas_call x42, Pallas kernels, apply(): pl.pallas_call(ordered, grid_spec=pltpu.PrefetchScalarGridSpec(num_scalar...  345 us
    ppermute x27, waiting for transfers between devices, swap(): return lax.ppermute(values, axis, [(i, i ^ bit) for i in range(n)])  40 us
    ppermute x27, starting transfers between devices, swap(): return lax.ppermute(values, axis, [(i, i ^ bit) for i in range(n)])  24.3 us
    all_to_all x4, starting transfers between devices, exchange(): lax.all_to_all(values.reshape(groups, slots // groups, d), 'ep', 0, 0, ti...  21.9 us
  transfers between devices with their start and end apart: 33, of which 10 were waited for; matrix products, arithmetic and copies ran while one was open for 3% of the time, Pallas kernels for 71%

profile of v3, /device:TPU:0, one launch (start us, length us, event | category | flops | bytes accessed | tf_op | source)
XLA Modules:
  0.0 485.7 jit_solution(4528929740087748883)
XLA Ops:
  10.1 4.4 fusion.3.refs_4_
  14.4 6.5 %all-to-all-start = ((bf16[8,120,1024]{2,1,0:T(8,128)(2,1)}), bf16[8,120,1024]{2,1,0:T(8,128)(2,1)}, u32[]{:S(2)}, u32[]{:S(2)}) async-start(bf16[8,120,1024]{2,1,0:T(8,128)(2,1)} %bitcast.2), calls=%async_computation | async-start | bytes 3932160 | tf_op jit(solution)/shard_map/all_to_all | solution.py:984
  22.8 10.6 %ln_qkv.1 = (bf16[768,1024]{1,0:T(8,128)(2,1)}, bf16[768,3072]{1,0:T(8,128)(2,1)}) custom-call(bf16[768,1024]{1,0:T(8,128)(2,1)} %refs_2_.1, f32[1,1024]{1,0:T(1,128)} %bitcast.139, f32[1,1024]{1,0:T(1,128)} %bitcast.142, bf16[1024,3072]{1,0:T(8,128)(2,1)} %refs_1_.6, bf16[960,1024]{1,0:T(8,128)(2,1)} %fusion.3.refs_4_), custom_call_target="tpu_custom_call" | custom-call | flops 126500000 | bytes 330000 | tf_op jit(solution)/shard_map/ln_qkv/pallas_call | solution.py:58
  33.5 22.3 %attend.1 = (bf16[768,1024]{1,0:T(8,128)(2,1)}, bf16[1024,768]{1,0:T(8,128)(2,1)}, f32[8,8,768]{2,1,0:T(8,128)}) custom-call(f32[768,1]{1,0:T(8,128)} %broadcast_in_dim.60.refs_0_, bf16[768,3072]{1,0:T(8,128)(2,1)} %get-tuple-element.75.refs_1_.refs_2_.refs_3_.refs_4_, bf16[768,3072]{1,0:T(8,128)(2,1)} %get-tuple-element.75.refs_1_.refs_2_.refs_3_.refs_4_, ...), custom_call_target="tpu_custom_call" | custom-call | flops 253000000 | bytes 660000 | tf_op jit(solution)/shard_map/attend/pallas_call | solution.py:58
  55.8 9.7 %after.1 = (f32[768,1024]{1,0:T(8,128)}, bf16[768,1024]{1,0:T(8,128)(2,1)}, bf16[1024,768]{1,0:T(8,128)(2,1)}, bf16[768,1024]{1,0:T(8,128)(2,1)}, bf16[1024,768]{1,0:T(8,128)(2,1)}, /*index=5*/f32[768,128]{1,0:T(8,128)}) custom-call(s32[1]{0:T(128)} %bitcast.4.refs_0_, bf16[768,1024]{1,0:T(8,128)(2,1)} %refs_2_.1, ...), custom_call_target="tpu_custom_call" | custom-call | flops 115000000 | bytes 300000 | tf_op jit(solution)/shard_map/after/pallas_call | solution.py:58
  67.2 4.4 fusion.4.refs_7_
  71.7 5.0 %all-to-all-start.1 = ((bf16[8,120,1024]{2,1,0:T(8,128)(2,1)}), bf16[8,120,1024]{2,1,0:T(8,128)(2,1)}, u32[]{:S(2)}, u32[]{:S(2)}) async-start(bf16[8,120,1024]{2,1,0:T(8,128)(2,1)} %bitcast.9), calls=%async_computation.1 | async-start | bytes 3932160 | tf_op jit(solution)/shard_map/all_to_all | solution.py:984
  77.2 22.7 %dense.2 = (bf16[4,768,512]{2,1,0:T(8,128)(2,1)}, bf16[4,768,512]{2,1,0:T(8,128)(2,1)}, bf16[2,4,2,128,512]{4,3,2,1,0:T(8,128)(2,1)}, bf16[2,4,2,128,512]{4,3,2,...) custom-call(s32[4]{0:T(128)} %get-tuple-element.208.refs_0_, ...), custom_call_target="tpu_custom_call" | custom-call | flops 1150000000 | bytes 3000000 | tf_op jit(solution)/shard_map/dense/pallas_call | solution.py:58
  100.3 22.7 %dense.3 = (bf16[4,768,512]{2,1,0:T(8,128)(2,1)}, bf16[4,768,512]{2,1,0:T(8,128)(2,1)}, bf16[2,4,2,128,512]{4,3,2,1,0:T(8,128)(2,1)}, bf16[2,4,2,128,512]{4,3,2,...) custom-call(s32[4]{0:T(128)} %get-tuple-element.209.refs_0_, ...), custom_call_target="tpu_custom_call" | custom-call | flops 1150000000 | bytes 3000000 | tf_op jit(solution)/shard_map/dense/pallas_call | solution.py:58
  137.5 25.7 %expert_first.1 = (bf16[4,960,512]{2,1,0:T(8,128)(2,1)}, bf16[4,960,512]{2,1,0:T(8,128)(2,1)}, bf16[960,1024]{1,0:T(8,128)(2,1)}, f32[960,128]{1,0:T(8,128)}, f32[960,1024]{1,0:T(8,128)}, /*index=5*/f32[960,1024]{1,0:T(8,128)}) custom-call(s32[1]{0:T(128)} %bitcast.1.refs_0_.refs_2_, bf16[960,1024]{1,0:T(8,128)(2,1)} %bitcast.10.refs_1_.refs_2_, ...), custom_call_target="tpu_custom_call" | custom-call | flops 55199997952 | bytes 144000000 | tf_op jit(solution)/shard_map/expert_first/pallas_call | solution.py:58
  163.2 9.2 %expert_grads.4 = (bf16[2,512,1024]{2,1,0:T(8,128)(2,1)}, bf16[2,512,1024]{2,1,0:T(8,128)(2,1)}) custom-call(s32[2]{0:T(128)} %get-tuple-element.207.refs_0_, s32[2]{0:T(128)} %get-tuple-element.205.refs_1_, bf16[960,1024]{1,0:T(8,128)(2,1)} %bitcast.10.refs_1_.refs_2_, bf16[4,960,512]{2,1,0:T(8,128)(2,1)} %get-tuple-element.96.refs_3_, ...), custom_call_target="tpu_custom_call" | custom-call | flops 80500000 | bytes 210000 | tf_op jit(solution)/shard_map/expert_grads/pallas_call | solution.py:58
  173.4 28.6 %expert_second.1 = (bf16[4,960,512]{2,1,0:T(8,128)(2,1)}, bf16[4,960,512]{2,1,0:T(8,128)(2,1)}, bf16[960,1024]{1,0:T(8,128)(2,1)}, bf16[960,1024]{1,0:T(8,128)(2,1)}, f32[128,1024]{1,0:T(8,128)}) custom-call(s32[1]{0:T(128)} %bitcast.1.refs_0_.refs_2_, bf16[960,1024]{1,0:T(8,128)(2,1)} %bitcast.10.refs_1_.refs_2_, bf16[960,1024]{1,0:T(8,128)(2,1)} %bitcast.3.refs_2_, ...), custom_call_target="tpu_custom_call" | custom-call | flops 1150000000 | bytes 3000000 | tf_op jit(solution)/shard_map/expert_second/pallas_call | solution.py:58
  202.0 5.3 %all-to-all-start.2 = ((bf16[8,120,1024]{2,1,0:T(8,128)(2,1)}), bf16[8,120,1024]{2,1,0:T(8,128)(2,1)}, u32[]{:S(2)}, u32[]{:S(2)}) async-start(bf16[8,120,1024]{2,1,0:T(8,128)(2,1)} %bitcast.126), calls=%async_computation.2 | async-start | bytes 3932160 | tf_op jit(solution)/shard_map/all_to_all | solution.py:984
  207.4 19.9 %dense_rest.1 = (f32[768,1024]{1,0:T(8,128)}, f32[768,1024]{1,0:T(8,128)}) custom-call(s32[4]{0:T(128)} %get-tuple-element.208.refs_0_, s32[4]{0:T(128)} %constant.36.clone.refs_1_, bf16[4,768,512]{2,1,0:T(8,128)(2,1)} %get-tuple-element.84.refs_7_.refs_2_, bf16[4,768,512]{2,1,0:T(8,128)(2,1)} %get-tuple-element.89.refs_2_.refs_3_, ...), custom_call_target="tpu_custom_call" | custom-call | flops 34500001792 | bytes 90000000 | tf_op jit(solution)/shard_map/dense_rest/pallas_call | solution.py:58
  227.2 9.2 %expert_grads.5 = (bf16[2,512,1024]{2,1,0:T(8,128)(2,1)}, bf16[2,512,1024]{2,1,0:T(8,128)(2,1)}) custom-call(s32[2]{0:T(128)} %get-tuple-element.207.refs_0_, s32[2]{0:T(128)} %get-tuple-element.205.refs_1_, bf16[960,1024]{1,0:T(8,128)(2,1)} %bitcast.10.refs_1_.refs_2_, bf16[4,960,512]{2,1,0:T(8,128)(2,1)} %get-tuple-element.108.refs_3_, ...), custom_call_target="tpu_custom_call" | custom-call | flops 80500000 | bytes 210000 | tf_op jit(solution)/shard_map/expert_grads/pallas_call | solution.py:58
  239.5 9.2 %expert_grads.6 = (bf16[2,512,1024]{2,1,0:T(8,128)(2,1)}, bf16[2,512,1024]{2,1,0:T(8,128)(2,1)}) custom-call(s32[2]{0:T(128)} %get-tuple-element.206.refs_0_, s32[2]{0:T(128)} %get-tuple-element.204.refs_1_, bf16[960,1024]{1,0:T(8,128)(2,1)} %bitcast.10.refs_1_.refs_2_, bf16[4,960,512]{2,1,0:T(8,128)(2,1)} %get-tuple-element.96.refs_3_, ...), custom_call_target="tpu_custom_call" | custom-call | flops 80500000 | bytes 210000 | tf_op jit(solution)/shard_map/expert_grads/pallas_call | solution.py:58
  256.4 9.2 %expert_grads.7 = (bf16[2,512,1024]{2,1,0:T(8,128)(2,1)}, bf16[2,512,1024]{2,1,0:T(8,128)(2,1)}) custom-call(s32[2]{0:T(128)} %get-tuple-element.206.refs_0_, s32[2]{0:T(128)} %get-tuple-element.204.refs_1_, bf16[960,1024]{1,0:T(8,128)(2,1)} %bitcast.10.refs_1_.refs_2_, bf16[4,960,512]{2,1,0:T(8,128)(2,1)} %get-tuple-element.108.refs_3_, ...), custom_call_target="tpu_custom_call" | custom-call | flops 80500000 | bytes 210000 | tf_op jit(solution)/shard_map/expert_grads/pallas_call | solution.py:58
  265.6 11.8 %between.1 = (bf16[768,1024]{1,0:T(8,128)(2,1)}, bf16[768,1024]{1,0:T(8,128)(2,1)}, f32[8,1024]{1,0:T(8,128)}) custom-call(s32[768,1]{1,0:T(8,128)} %fusion.9.refs_0_, bf16[960,1024]{1,0:T(8,128)(2,1)} %bitcast.20.refs_1_, f32[768,1024]{1,0:T(8,128)} %get-tuple-element.104.refs_2_, f32[768,1024]{1,0:T(8,128)} %get-tuple-element.105.refs_6_.refs_3_.refs_2_, ...), custom_call_target="tpu_custom_call" | custom-call | flops 138000000 | bytes 360000 | tf_op jit(solution)/shard_map/between/pallas_call | solution.py:58
  277.4 5.1 %all-to-all-start.3 = ((bf16[8,120,1024]{2,1,0:T(8,128)(2,1)}), bf16[8,120,1024]{2,1,0:T(8,128)(2,1)}, u32[]{:S(2)}, u32[]{:S(2)}) async-start(bf16[8,120,1024]{2,1,0:T(8,128)(2,1)} %bitcast.125), calls=%async_computation.3 | async-start | bytes 3932160 | tf_op jit(solution)/shard_map/all_to_all | solution.py:984
  282.6 6.5 %rows_grad.2 = (bf16[4,4,32,1024]{3,2,1,0:T(8,128)(2,1)}, bf16[4,4,32,1024]{3,2,1,0:T(8,128)(2,1)}) custom-call(s32[4]{0:T(128)} %get-tuple-element.208.refs_0_, s32[4]{0:T(128)} %constant.36.clone.refs_1_, s32[1]{0:T(128)} %bitcast.1.refs_0_.refs_2_, bf16[1024,768]{1,0:T(8,128)(2,1)} %get-tuple-element.118.refs_3_, ...), custom_call_target="tpu_custom_call" | custom-call | flops 34500000 | bytes 90000 | tf_op jit(solution)/shard_map/rows_grad/pallas_call | solution.py:58
  289.0 28.3 %attend_back.1 = (bf16[3,768,1024]{2,1,0:T(8,128)(2,1)}, bf16[3,1024,768]{2,1,0:T(8,128)(2,1)}) custom-call(f32[768,1]{1,0:T(8,128)} %broadcast_in_dim.60.refs_0_, f32[8,8,768]{2,1,0:T(8,128)} %get-tuple-element.116.refs_1_, bf16[768,3072]{1,0:T(8,128)(2,1)} %get-tuple-element.75.refs_1_.refs_2_.refs_3_.refs_4_, ...), custom_call_target="tpu_custom_call" | custom-call | flops 322000000 | bytes 840000 | tf_op jit(solution)/shard_map/attend_back/pallas_call | solution.py:58
  336.6 11.5 %first_back.1 = (bf16[768,1024]{1,0:T(8,128)(2,1)}, f32[8,1024]{1,0:T(8,128)}) custom-call(bf16[3,768,1024]{2,1,0:T(8,128)(2,1)} %get-tuple-element.122.refs_3_.refs_0_, bf16[1024,3072]{1,0:T(8,128)(2,1)} %refs_1_.6, bf16[768,1024]{1,0:T(8,128)(2,1)} %refs_2_.1, bf16[768,1024]{1,0:T(8,128)(2,1)} %get-tuple-element.119.refs_4_.refs_5_.refs_3_, ...), custom_call_target="tpu_custom_call" | custom-call | flops 138000000 | bytes 360000 | tf_op jit(solution)/shard_map/first_back/pallas_call | solution.py:58
  365.7 10.2 %rows_grad.3 = (bf16[4,4,112,512]{3,2,1,0:T(8,128)(2,1)}, bf16[4,4,96,512]{3,2,1,0:T(8,128)(2,1)}, bf16[4,4,112,512]{3,2,1,0:T(8,128)(2,1)}, bf16[4,4,96,512]{3,2,1,0:T(8,128)(2,1)}) custom-call(s32[4]{0:T(128)} %get-tuple-element.208.refs_0_, s32[4]{0:T(128)} %constant.36.clone.refs_1_, s32[1]{0:T(128)} %bitcast.1.refs_0_.refs_2_, ...), custom_call_target="tpu_custom_call" | custom-call | flops 80500000 | bytes 210000 | tf_op jit(solution)/shard_map/rows_grad/pallas_call | solution.py:58
  376.6 7.3 %collective-permute-done.15.refs_7_.refs_3_ = bf16[1,512,1024]{2,1,0:T(8,128)(2,1)} collective-permute-done((bf16[1,512,1024]{2,1,0:T(8,128)(2,1)}, bf16[1,512,1024]{2,1,0:T(8,128)(2,1)}, u32[]{:S(2)}, u32[]{:S(2)}) %collective-permute-start.15) | collective-permute-done | bytes 1048608 | tf_op jit(solution)/shard_map/ppermute | solution.py:811
  385.1 6.9 %outputs.1.refs_2_ = bf16[768,1024]{1,0:T(8,128)(2,1)} custom-call(s32[768,1]{1,0:T(8,128)} %fusion.9.refs_0_, bf16[960,1024]{1,0:T(8,128)(2,1)} %bitcast.23.refs_1_, f32[768,1024]{1,0:T(8,128)} %get-tuple-element.105.refs_6_.refs_3_.refs_2_, f32[768,1024]{1,0:T(8,128)} %get-tuple-element.106.refs_4_.refs_3_, f32[768,128]{1,0:T(8,128)} %get-tuple-element.107.refs_5_.refs_4_, ...), custom_call_target="tpu_custom_call" | custom-call | flops 11500000256 | bytes 30000000 | tf_op jit(solution)/shard_map/outputs/pallas_call | solution.py:58
  401.5 6.7 %up_final.1.refs_4_ = f32[1024,1024]{1,0:T(8,128)} custom-call(bf16[1,512,1024]{2,1,0:T(8,128)(2,1)} %add_terms.25.refs_3_.refs_0_, bf16[2,512,1024]{2,1,0:T(8,128)(2,1)} %get-tuple-element.113.refs_11_.refs_0_.refs_1_, bf16[2,512,1024]{2,1,0:T(8,128)(2,1)} %collective-permute-done.9.refs_1_.refs_2_, ...), custom_call_target="tpu_custom_call" | custom-call | flops 80500000 | bytes 210000 | tf_op jit(solution)/shard_map/up_final/pallas_call | solution.py:58
  408.3 4.8 down_final.1
  413.0 4.9 %collective-permute-done.17.refs_2_ = bf16[2,4,112,512]{3,2,1,0:T(8,128)(2,1)S(1)} collective-permute-done((bf16[2,4,112,512]{3,2,1,0:T(8,128)(2,1)}, bf16[2,4,112,512]{3,2,1,0:T(8,128)(2,1)S(1)}, u32[]{:S(2)}, u32[]{:S(2)}) %collective-permute-start.17) | collective-permute-done | bytes 917536 | tf_op jit(solution)/shard_map/ppermute | solution.py:811
  424.7 4.6 collective-permute-done.23.refs_10_
  432.1 5.6 %collective-permute-done.24.refs_11_ = bf16[1,4,32,1024]{3,2,1,0:T(8,128)(2,1)S(1)} collective-permute-done((bf16[1,4,32,1024]{3,2,1,0:T(8,128)(2,1)}, bf16[1,4,32,1024]{3,2,1,0:T(8,128)(2,1)S(1)}, u32[]{:S(2)}, u32[]{:S(2)}) %collective-permute-start.24) | collective-permute-done | bytes 262176 | tf_op jit(solution)/shard_map/ppermute | solution.py:811
  449.0 7.4 %collective-permute-done.25.refs_1_ = bf16[2,144,1024]{2,1,0:T(8,128)(2,1)S(1)} collective-permute-done((bf16[2,144,1024]{2,1,0:T(8,128)(2,1)}, bf16[2,144,1024]{2,1,0:T(8,128)(2,1)S(1)}, u32[]{:S(2)}, u32[]{:S(2)}) %collective-permute-start.25) | collective-permute-done | bytes 589856 | tf_op jit(solution)/shard_map/ppermute | solution.py:811
  465.5 4.5 collective-permute-done.26.refs_2_
  (151 shorter events, 119.8 us)
Async XLA Ops:
  14.4 52.8 %all-to-all-start = ((bf16[8,120,1024]{2,1,0:T(8,128)(2,1)}), bf16[8,120,1024]{2,1,0:T(8,128)(2,1)}, u32[]{:S(2)}, u32[]{:S(2)}) async-start(bf16[8,120,1024]{2,1,0:T(8,128)(2,1)} %bitcast.2), calls=%async_computation | async-start | bytes 3932160 | tf_op jit(solution)/shard_map/all_to_all | solution.py:984
  71.7 65.8 %all-to-all-start.1 = ((bf16[8,120,1024]{2,1,0:T(8,128)(2,1)}), bf16[8,120,1024]{2,1,0:T(8,128)(2,1)}, u32[]{:S(2)}, u32[]{:S(2)}) async-start(bf16[8,120,1024]{2,1,0:T(8,128)(2,1)} %bitcast.9), calls=%async_computation.1 | async-start | bytes 3932160 | tf_op jit(solution)/shard_map/all_to_all | solution.py:984
  99.9 26.0 %collective-permute-start.1 = (bf16[2,4,2,128,512]{4,3,2,1,0:T(8,128)(2,1)}, bf16[2,4,2,128,512]{4,3,2,1,0:T(8,128)(2,1)}, u32[]{:S(2)}, u32[]{:S(2)}) collective-permute-start(bf16[2,4,2,128,512]{4,3,2,1,0:T(8,128)(2,1)} %get-tuple-element.88), channel_id=1, source_target_pairs={{0,1},{1,0},{2,3},{3,2},{4,5},{5,4},{6,7},{7,6},{8,9},{9,8},{10,11... | collective-permute-start | bytes 6291464 | tf_op jit(solution)/shard_map/ppermute | solution.py:811
  123.0 8.6 %collective-permute-start = (bf16[2,4,2,128,512]{4,3,2,1,0:T(8,128)(2,1)}, bf16[2,4,2,128,512]{4,3,2,1,0:T(8,128)(2,1)}, u32[]{:S(2)}, u32[]{:S(2)}) collective-permute-start(bf16[2,4,2,128,512]{4,3,2,1,0:T(8,128)(2,1)} %get-tuple-element.86), channel_id=1, source_target_pairs={{0,1},{1,0},{2,3},{3,2},{4,5},{5,4},{6,7},{7,6},{8,9},{9,8},{10,11... | collective-permute-start | bytes 6291464 | tf_op jit(solution)/shard_map/ppermute | solution.py:811
  123.1 14.4 %collective-permute-start.3 = (bf16[2,4,2,128,512]{4,3,2,1,0:T(8,128)(2,1)}, bf16[2,4,2,128,512]{4,3,2,1,0:T(8,128)(2,1)}, u32[]{:S(2)}, u32[]{:S(2)}) collective-permute-start(bf16[2,4,2,128,512]{4,3,2,1,0:T(8,128)(2,1)} %get-tuple-element.91), channel_id=1, source_target_pairs={{0,1},{1,0},{2,3},{3,2},{4,5},{5,4},{6,7},{7,6},{8,9},{9,8},{10,11... | collective-permute-start | bytes 6291464 | tf_op jit(solution)/shard_map/ppermute | solution.py:811
  123.6 13.9 %collective-permute-start.2 = (bf16[2,4,2,128,512]{4,3,2,1,0:T(8,128)(2,1)}, bf16[2,4,2,128,512]{4,3,2,1,0:T(8,128)(2,1)}, u32[]{:S(2)}, u32[]{:S(2)}) collective-permute-start(bf16[2,4,2,128,512]{4,3,2,1,0:T(8,128)(2,1)} %get-tuple-element.90), channel_id=1, source_target_pairs={{0,1},{1,0},{2,3},{3,2},{4,5},{5,4},{6,7},{7,6},{8,9},{9,8},{10,11... | collective-permute-start | bytes 6291464 | tf_op jit(solution)/shard_map/ppermute | solution.py:811
  130.1 77.2 %collective-permute-start.4 = (bf16[2,4,2,128,512]{4,3,2,1,0:T(8,128)(2,1)}, bf16[2,4,2,128,512]{4,3,2,1,0:T(8,128)(2,1)}, u32[]{:S(2)}, u32[]{:S(2)}) collective-permute-start(bf16[2,4,2,128,512]{4,3,2,1,0:T(8,128)(2,1)} %bitcast.106), channel_id=1, source_target_pairs={{0,16},{8,24},{16,0},{24,8},{1,17},{9,25},{17,1},{25,9},{2,18},{10... | collective-permute-start | bytes 6291464 | tf_op jit(solution)/shard_map/ppermute | solution.py:811
  136.0 71.4 %collective-permute-start.5 = (bf16[2,4,2,128,512]{4,3,2,1,0:T(8,128)(2,1)}, bf16[2,4,2,128,512]{4,3,2,1,0:T(8,128)(2,1)}, u32[]{:S(2)}, u32[]{:S(2)}) collective-permute-start(bf16[2,4,2,128,512]{4,3,2,1,0:T(8,128)(2,1)} %bitcast.119), channel_id=1, source_target_pairs={{0,8},{8,0},{16,24},{24,16},{1,9},{9,1},{17,25},{25,17},{2,10},{10... | collective-permute-start | bytes 6291464 | tf_op jit(solution)/shard_map/ppermute | solution.py:811
  172.4 76.3 %collective-permute-start.7 = (bf16[2,512,1024]{2,1,0:T(8,128)(2,1)}, bf16[2,512,1024]{2,1,0:T(8,128)(2,1)}, u32[]{:S(2)}, u32[]{:S(2)}) collective-permute-start(bf16[2,512,1024]{2,1,0:T(8,128)(2,1)} %get-tuple-element.98.refs_10_), channel_id=1, source_target_pairs={{0,16},{8,24},{16,0},{24,8},{1,17},{9,25},{17,1},{25,9},{2,18},{10... | collective-permute-start | bytes 6291464 | tf_op jit(solution)/shard_map/ppermute | solution.py:811
  172.9 78.8 %collective-permute-start.6 = (bf16[2,512,1024]{2,1,0:T(8,128)(2,1)}, bf16[2,512,1024]{2,1,0:T(8,128)(2,1)}, u32[]{:S(2)}, u32[]{:S(2)}) collective-permute-start(bf16[2,512,1024]{2,1,0:T(8,128)(2,1)} %get-tuple-element.111), channel_id=1, source_target_pairs={{0,8},{8,0},{16,24},{24,16},{1,9},{9,1},{17,25},{25,17},{2,10},{10... | collective-permute-start | bytes 6291464 | tf_op jit(solution)/shard_map/ppermute | solution.py:811
  202.0 63.6 %all-to-all-start.2 = ((bf16[8,120,1024]{2,1,0:T(8,128)(2,1)}), bf16[8,120,1024]{2,1,0:T(8,128)(2,1)}, u32[]{:S(2)}, u32[]{:S(2)}) async-start(bf16[8,120,1024]{2,1,0:T(8,128)(2,1)} %bitcast.126), calls=%async_computation.2 | async-start | bytes 3932160 | tf_op jit(solution)/shard_map/all_to_all | solution.py:984
  236.5 95.2 %collective-permute-start.9 = (bf16[2,512,1024]{2,1,0:T(8,128)(2,1)}, bf16[2,512,1024]{2,1,0:T(8,128)(2,1)}, u32[]{:S(2)}, u32[]{:S(2)}) collective-permute-start(bf16[2,512,1024]{2,1,0:T(8,128)(2,1)} %get-tuple-element.109.refs_6_), channel_id=1, source_target_pairs={{0,16},{8,24},{16,0},{24,8},{1,17},{9,25},{17,1},{25,9},{2,18},{10... | collective-permute-start | bytes 6291464 | tf_op jit(solution)/shard_map/ppermute | solution.py:811
  238.0 96.1 %collective-permute-start.8 = (bf16[2,512,1024]{2,1,0:T(8,128)(2,1)}, bf16[2,512,1024]{2,1,0:T(8,128)(2,1)}, u32[]{:S(2)}, u32[]{:S(2)}) collective-permute-start(bf16[2,512,1024]{2,1,0:T(8,128)(2,1)} %get-tuple-element.124), channel_id=1, source_target_pairs={{0,8},{8,0},{16,24},{24,16},{1,9},{9,1},{17,25},{25,17},{2,10},{10... | collective-permute-start | bytes 6291464 | tf_op jit(solution)/shard_map/ppermute | solution.py:811
  251.1 66.2 %collective-permute-start.11 = (bf16[1,512,1024]{2,1,0:T(8,128)(2,1)}, bf16[1,512,1024]{2,1,0:T(8,128)(2,1)}, u32[]{:S(2)}, u32[]{:S(2)}) collective-permute-start(bf16[1,512,1024]{2,1,0:T(8,128)(2,1)} %add_terms.23.refs_2_), channel_id=1, source_target_pairs={{0,8},{8,0},{16,24},{24,16},{1,9},{9,1},{17,25},{25,17},{2,10},{10... | collective-permute-start | bytes 3145736 | tf_op jit(solution)/shard_map/ppermute | solution.py:811
  254.1 66.0 %collective-permute-start.10 = (bf16[1,512,1024]{2,1,0:T(8,128)(2,1)}, bf16[1,512,1024]{2,1,0:T(8,128)(2,1)}, u32[]{:S(2)}, u32[]{:S(2)}) collective-permute-start(bf16[1,512,1024]{2,1,0:T(8,128)(2,1)} %add_terms.24.refs_6_), channel_id=1, source_target_pairs={{0,16},{8,24},{16,0},{24,8},{1,17},{9,25},{17,1},{25,9},{2,18},{10... | collective-permute-start | bytes 3145736 | tf_op jit(solution)/shard_map/ppermute | solution.py:811
  277.4 107.7 %all-to-all-start.3 = ((bf16[8,120,1024]{2,1,0:T(8,128)(2,1)}), bf16[8,120,1024]{2,1,0:T(8,128)(2,1)}, u32[]{:S(2)}, u32[]{:S(2)}) async-start(bf16[8,120,1024]{2,1,0:T(8,128)(2,1)} %bitcast.125), calls=%async_computation.3 | async-start | bytes 3932160 | tf_op jit(solution)/shard_map/all_to_all | solution.py:984
  282.5 164.8 %reduce-scatter.5.cloned.1.call-start = ((), (), s32[]{:S(2)}) async-start(), calls=%async_computation.7 | async-start | bytes 1310720 | tf_op jit(solution)/shard_map/reduce_scatter | solution.py:1085
  325.8 25.8 %collective-permute-start.13 = (bf16[1,4,2,128,512]{4,3,2,1,0:T(8,128)(2,1)}, bf16[1,4,2,128,512]{4,3,2,1,0:T(8,128)(2,1)}, u32[]{:S(2)}, u32[]{:S(2)}) collective-permute-start(bf16[1,4,2,128,512]{4,3,2,1,0:T(8,128)(2,1)} %bitcast.111), channel_id=1, source_target_pairs={{0,8},{8,0},{16,24},{24,16},{1,9},{9,1},{17,25},{25,17},{2,10},{10... | collective-permute-start | bytes 3145736 | tf_op jit(solution)/shard_map/ppermute | solution.py:811
  330.2 25.6 %collective-permute-start.12 = (bf16[1,4,2,128,512]{4,3,2,1,0:T(8,128)(2,1)}, bf16[1,4,2,128,512]{4,3,2,1,0:T(8,128)(2,1)}, u32[]{:S(2)}, u32[]{:S(2)}) collective-permute-start(bf16[1,4,2,128,512]{4,3,2,1,0:T(8,128)(2,1)} %bitcast.109), channel_id=1, source_target_pairs={{0,16},{8,24},{16,0},{24,8},{1,17},{9,25},{17,1},{25,9},{2,18},{10... | collective-permute-start | bytes 3145736 | tf_op jit(solution)/shard_map/ppermute | solution.py:811
  359.0 102.7 %reduce-scatter.3.cloned.1.call-start = ((), (), s32[]{:S(2)}) async-start(), calls=%async_computation.6 | async-start | bytes 1310720 | tf_op jit(solution)/shard_map/reduce_scatter | solution.py:1085
  359.1 24.8 %collective-permute-start.15 = (bf16[1,512,1024]{2,1,0:T(8,128)(2,1)}, bf16[1,512,1024]{2,1,0:T(8,128)(2,1)}, u32[]{:S(2)}, u32[]{:S(2)}) collective-permute-start(bf16[1,512,1024]{2,1,0:T(8,128)(2,1)} %add_terms.30.refs_5_), channel_id=1, source_target_pairs={{0,16},{8,24},{16,0},{24,8},{1,17},{9,25},{17,1},{25,9},{2,18},{10... | collective-permute-start | bytes 3145736 | tf_op jit(solution)/shard_map/ppermute | solution.py:811
  360.6 24.5 %collective-permute-start.14 = (bf16[1,512,1024]{2,1,0:T(8,128)(2,1)}, bf16[1,512,1024]{2,1,0:T(8,128)(2,1)}, u32[]{:S(2)}, u32[]{:S(2)}) collective-permute-start(bf16[1,512,1024]{2,1,0:T(8,128)(2,1)} %add_terms.29.refs_2_), channel_id=1, source_target_pairs={{0,8},{8,0},{16,24},{24,16},{1,9},{9,1},{17,25},{25,17},{2,10},{10... | collective-permute-start | bytes 3145736 | tf_op jit(solution)/shard_map/ppermute | solution.py:811
  376.0 16.1 %collective-permute-start.16 = (bf16[4,4,112,512]{3,2,1,0:T(8,128)(2,1)}, bf16[4,4,112,512]{3,2,1,0:T(8,128)(2,1)}, u32[]{:S(2)}, u32[]{:S(2)}) collective-permute-start(bf16[4,4,112,512]{3,2,1,0:T(8,128)(2,1)} %get-tuple-element.131.refs_5_), channel_id=1, source_target_pairs={{0,1},{1,0},{2,3},{3,2},{4,5},{5,4},{6,7},{7,6},{8,9},{9,8},{10,11... | collective-permute-start | bytes 5505032 | tf_op jit(solution)/shard_map/ppermute | solution.py:811
  376.0 18.9 %collective-permute-start.19 = (bf16[4,4,96,512]{3,2,1,0:T(8,128)(2,1)}, bf16[4,4,96,512]{3,2,1,0:T(8,128)(2,1)}, u32[]{:S(2)}, u32[]{:S(2)}) collective-permute-start(bf16[4,4,96,512]{3,2,1,0:T(8,128)(2,1)} %get-tuple-element.135), channel_id=1, source_target_pairs={{0,1},{1,0},{2,3},{3,2},{4,5},{5,4},{6,7},{7,6},{8,9},{9,8},{10,11... | collective-permute-start | bytes 4718600 | tf_op jit(solution)/shard_map/ppermute | solution.py:811
  376.5 21.6 %collective-permute-start.18 = (bf16[4,4,32,1024]{3,2,1,0:T(8,128)(2,1)}, bf16[4,4,32,1024]{3,2,1,0:T(8,128)(2,1)}, u32[]{:S(2)}, u32[]{:S(2)}) collective-permute-start(bf16[4,4,32,1024]{3,2,1,0:T(8,128)(2,1)} %get-tuple-element.120.refs_6_), channel_id=1, source_target_pairs={{0,1},{1,0},{2,3},{3,2},{4,5},{5,4},{6,7},{7,6},{8,9},{9,8},{10,11... | collective-permute-start | bytes 3145736 | tf_op jit(solution)/shard_map/ppermute | solution.py:811
  394.4 23.5 %collective-permute-start.17 = (bf16[2,4,112,512]{3,2,1,0:T(8,128)(2,1)}, bf16[2,4,112,512]{3,2,1,0:T(8,128)(2,1)S(1)}, u32[]{:S(2)}, u32[]{:S(2)}) collective-permute-start(bf16[2,4,112,512]{3,2,1,0:T(8,128)(2,1)} %bitcast.114), channel_id=1, source_target_pairs={{0,16},{8,24},{16,0},{24,8},{1,17},{9,25},{17,1},{25,9},{2,18},{10... | collective-permute-start | bytes 2752520 | tf_op jit(solution)/shard_map/ppermute | solution.py:811
  397.1 25.0 %collective-permute-start.21 = (bf16[2,4,96,512]{3,2,1,0:T(8,128)(2,1)}, bf16[2,4,96,512]{3,2,1,0:T(8,128)(2,1)}, u32[]{:S(2)}, u32[]{:S(2)}) collective-permute-start(bf16[2,4,96,512]{3,2,1,0:T(8,128)(2,1)} %bitcast.116), channel_id=1, source_target_pairs={{0,8},{8,0},{16,24},{24,16},{1,9},{9,1},{17,25},{25,17},{2,10},{10... | collective-permute-start | bytes 2359304 | tf_op jit(solution)/shard_map/ppermute | solution.py:811
  400.0 29.2 %collective-permute-start.23 = (bf16[2,4,32,1024]{3,2,1,0:T(8,128)(2,1)}, bf16[2,4,32,1024]{3,2,1,0:T(8,128)(2,1)}, u32[]{:S(2)}, u32[]{:S(2)}) collective-permute-start(bf16[2,4,32,1024]{3,2,1,0:T(8,128)(2,1)} %bitcast.123), channel_id=1, source_target_pairs={{0,16},{8,24},{16,0},{24,8},{1,17},{9,25},{17,1},{25,9},{2,18},{10... | collective-permute-start | bytes 1572872 | tf_op jit(solution)/shard_map/ppermute | solution.py:811
  421.1 17.4 %collective-permute-start.20 = (bf16[1,4,112,512]{3,2,1,0:T(8,128)(2,1)}, bf16[1,4,112,512]{3,2,1,0:T(8,128)(2,1)S(1)}, u32[]{:S(2)}, u32[]{:S(2)}) collective-permute-start(bf16[1,4,112,512]{3,2,1,0:T(8,128)(2,1)} %bitcast.127), channel_id=1, source_target_pairs={{0,8},{8,0},{16,24},{24,16},{1,9},{9,1},{17,25},{25,17},{2,10},{10... | collective-permute-start | bytes 1376264 | tf_op jit(solution)/shard_map/ppermute | solution.py:811
  424.2 13.6 %collective-permute-start.22 = (bf16[1,4,96,512]{3,2,1,0:T(8,128)(2,1)}, bf16[1,4,96,512]{3,2,1,0:T(8,128)(2,1)S(1)}, u32[]{:S(2)}, u32[]{:S(2)}) collective-permute-start(bf16[1,4,96,512]{3,2,1,0:T(8,128)(2,1)} %bitcast.129), channel_id=1, source_target_pairs={{0,16},{8,24},{16,0},{24,8},{1,17},{9,25},{17,1},{25,9},{2,18},{10... | collective-permute-start | bytes 1179656 | tf_op jit(solution)/shard_map/ppermute | solution.py:811
  446.0 10.4 %collective-permute-start.25 = (bf16[2,144,1024]{2,1,0:T(8,128)(2,1)}, bf16[2,144,1024]{2,1,0:T(8,128)(2,1)S(1)}, u32[]{:S(2)}, u32[]{:S(2)}) collective-permute-start(bf16[2,144,1024]{2,1,0:T(8,128)(2,1)} %add_terms.39.refs_2_), channel_id=1, source_target_pairs={{0,2},{1,3},{2,0},{3,1},{4,6},{5,7},{6,4},{7,5},{8,10},{9,11},{10,... | collective-permute-start | bytes 1769480 | tf_op jit(solution)/shard_map/ppermute | solution.py:811
  459.1 11.0 %collective-permute-start.26 = (bf16[1,144,1024]{2,1,0:T(8,128)(2,1)}, bf16[1,144,1024]{2,1,0:T(8,128)(2,1)S(1)}, u32[]{:S(2)}, u32[]{:S(2)}) collective-permute-start(bf16[1,144,1024]{2,1,0:T(8,128)(2,1)} %add_terms.40.refs_3_), channel_id=1, source_target_pairs={{0,4},{1,5},{2,6},{3,7},{4,0},{5,1},{6,2},{7,3},{8,12},{9,13},{10,... | collective-permute-start | bytes 884744 | tf_op jit(solution)/shard_map/ppermute | solution.py:811
  (16 other events, 109.2 us)
Sparse Core Ops, SparseCore 0:
  359.1 27.4 reduce-scatter.4
  389.0 25.7 reduce-scatter.2

commit v4 on v3

--- a/solution.py
+++ b/solution.py
@@ -736,7 +736,7 @@
 
 def up_final(*terms):
     _, width, d = terms[0].shape
-    block = 128
+    block = 256
     return call(
         up_final_kernel,
         (d // width, width // block),
@@ -750,7 +750,7 @@
 
 def down_final(*terms):
     _, width, d = terms[0].shape
-    block = 128
+    block = 256
     return call(
         down_final_kernel,
         (width // block,),
@@ -903,7 +903,7 @@
     height = 1
     for extent in shape[1:-1]:
         height *= extent
-    block = max(b for b in range(1, height + 1) if height % b == 0 and b * columns <= 1 << 18)
+    block = max(b for b in range(1, height + 1) if height % b == 0 and b * columns <= 1 << 19)
     result = call(
         add_kernel,
         (count, height // block),

time: 494 us -> 495 us (level)
  transfers between devices with their start and end apart: 33 -> 33, of which waited for: 10 -> 10; matrix products, arithmetic and copies ran while one was open for 3% -> 3% of each run, Pallas kernels for 71% -> 70%
where the time goes in v4:
time: 495 us; the launch traced here: 486 us
  Pallas kernels  344 us (69%)
  starting transfers between devices  46.4 us (9%)
  waiting for transfers between devices  43.6 us (9%)
  local copies, waits for them, and re-layouts  21.9 us (4%)
  between operations  15.1 us (3%)
  matrix products  9.14 us (2%)
  other arithmetic  6.86 us (1%)
    pallas_call x42, Pallas kernels, apply(): pl.pallas_call(ordered, grid_spec=pltpu.PrefetchScalarGridSpec(num_scalar...  344 us
    ppermute x27, waiting for transfers between devices, swap(): return lax.ppermute(values, axis, [(i, i ^ bit) for i in range(n)])  41.7 us
    ppermute x27, starting transfers between devices, swap(): return lax.ppermute(values, axis, [(i, i ^ bit) for i in range(n)])  24.4 us
    all_to_all x4, starting transfers between devices, exchange(): lax.all_to_all(values.reshape(groups, slots // groups, d), 'ep', 0, 0, ti...  21.9 us
  transfers between devices with their start and end apart: 33, of which 10 were waited for; matrix products, arithmetic and copies ran while one was open for 3% of the time, Pallas kernels for 70%

profile of v4, /device:TPU:0, one launch (start us, length us, event | category | flops | bytes accessed | tf_op | source)
XLA Modules:
  0.0 486.5 jit_solution(11987611446362188454)
XLA Ops:
  10.1 4.4 fusion.3.refs_4_
  14.4 6.5 %all-to-all-start = ((bf16[8,120,1024]{2,1,0:T(8,128)(2,1)}), bf16[8,120,1024]{2,1,0:T(8,128)(2,1)}, u32[]{:S(2)}, u32[]{:S(2)}) async-start(bf16[8,120,1024]{2,1,0:T(8,128)(2,1)} %bitcast.2), calls=%async_computation | async-start | bytes 3932160 | tf_op jit(solution)/shard_map/all_to_all | solution.py:984
  22.8 10.6 %ln_qkv.1 = (bf16[768,1024]{1,0:T(8,128)(2,1)}, bf16[768,3072]{1,0:T(8,128)(2,1)}) custom-call(bf16[768,1024]{1,0:T(8,128)(2,1)} %refs_2_.1, f32[1,1024]{1,0:T(1,128)} %bitcast.139, f32[1,1024]{1,0:T(1,128)} %bitcast.142, bf16[1024,3072]{1,0:T(8,128)(2,1)} %refs_1_.6, bf16[960,1024]{1,0:T(8,128)(2,1)} %fusion.3.refs_4_), custom_call_target="tpu_custom_call" | custom-call | flops 126500000 | bytes 330000 | tf_op jit(solution)/shard_map/ln_qkv/pallas_call | solution.py:58
  33.5 22.3 %attend.1 = (bf16[768,1024]{1,0:T(8,128)(2,1)}, bf16[1024,768]{1,0:T(8,128)(2,1)}, f32[8,8,768]{2,1,0:T(8,128)}) custom-call(f32[768,1]{1,0:T(8,128)} %broadcast_in_dim.60.refs_0_, bf16[768,3072]{1,0:T(8,128)(2,1)} %get-tuple-element.75.refs_1_.refs_2_.refs_3_.refs_4_, bf16[768,3072]{1,0:T(8,128)(2,1)} %get-tuple-element.75.refs_1_.refs_2_.refs_3_.refs_4_, ...), custom_call_target="tpu_custom_call" | custom-call | flops 253000000 | bytes 660000 | tf_op jit(solution)/shard_map/attend/pallas_call | solution.py:58
  55.8 9.7 %after.1 = (f32[768,1024]{1,0:T(8,128)}, bf16[768,1024]{1,0:T(8,128)(2,1)}, bf16[1024,768]{1,0:T(8,128)(2,1)}, bf16[768,1024]{1,0:T(8,128)(2,1)}, bf16[1024,768]{1,0:T(8,128)(2,1)}, /*index=5*/f32[768,128]{1,0:T(8,128)}) custom-call(s32[1]{0:T(128)} %bitcast.4.refs_0_, bf16[768,1024]{1,0:T(8,128)(2,1)} %refs_2_.1, ...), custom_call_target="tpu_custom_call" | custom-call | flops 115000000 | bytes 300000 | tf_op jit(solution)/shard_map/after/pallas_call | solution.py:58
  67.2 4.4 fusion.4.refs_7_
  71.7 5.0 %all-to-all-start.1 = ((bf16[8,120,1024]{2,1,0:T(8,128)(2,1)}), bf16[8,120,1024]{2,1,0:T(8,128)(2,1)}, u32[]{:S(2)}, u32[]{:S(2)}) async-start(bf16[8,120,1024]{2,1,0:T(8,128)(2,1)} %bitcast.9), calls=%async_computation.1 | async-start | bytes 3932160 | tf_op jit(solution)/shard_map/all_to_all | solution.py:984
  77.2 22.7 %dense.2 = (bf16[4,768,512]{2,1,0:T(8,128)(2,1)}, bf16[4,768,512]{2,1,0:T(8,128)(2,1)}, bf16[2,4,2,128,512]{4,3,2,1,0:T(8,128)(2,1)}, bf16[2,4,2,128,512]{4,3,2,...) custom-call(s32[4]{0:T(128)} %get-tuple-element.208.refs_0_, ...), custom_call_target="tpu_custom_call" | custom-call | flops 1150000000 | bytes 3000000 | tf_op jit(solution)/shard_map/dense/pallas_call | solution.py:58
  100.3 22.7 %dense.3 = (bf16[4,768,512]{2,1,0:T(8,128)(2,1)}, bf16[4,768,512]{2,1,0:T(8,128)(2,1)}, bf16[2,4,2,128,512]{4,3,2,1,0:T(8,128)(2,1)}, bf16[2,4,2,128,512]{4,3,2,...) custom-call(s32[4]{0:T(128)} %get-tuple-element.209.refs_0_, ...), custom_call_target="tpu_custom_call" | custom-call | flops 1150000000 | bytes 3000000 | tf_op jit(solution)/shard_map/dense/pallas_call | solution.py:58
  135.6 25.7 %expert_first.1 = (bf16[4,960,512]{2,1,0:T(8,128)(2,1)}, bf16[4,960,512]{2,1,0:T(8,128)(2,1)}, bf16[960,1024]{1,0:T(8,128)(2,1)}, f32[960,128]{1,0:T(8,128)}, f32[960,1024]{1,0:T(8,128)}, /*index=5*/f32[960,1024]{1,0:T(8,128)}) custom-call(s32[1]{0:T(128)} %bitcast.1.refs_0_.refs_2_, bf16[960,1024]{1,0:T(8,128)(2,1)} %bitcast.10.refs_1_.refs_2_, ...), custom_call_target="tpu_custom_call" | custom-call | flops 55199997952 | bytes 144000000 | tf_op jit(solution)/shard_map/expert_first/pallas_call | solution.py:58
  161.3 9.2 %expert_grads.4 = (bf16[2,512,1024]{2,1,0:T(8,128)(2,1)}, bf16[2,512,1024]{2,1,0:T(8,128)(2,1)}) custom-call(s32[2]{0:T(128)} %get-tuple-element.207.refs_0_, s32[2]{0:T(128)} %get-tuple-element.205.refs_1_, bf16[960,1024]{1,0:T(8,128)(2,1)} %bitcast.10.refs_1_.refs_2_, bf16[4,960,512]{2,1,0:T(8,128)(2,1)} %get-tuple-element.96.refs_3_, ...), custom_call_target="tpu_custom_call" | custom-call | flops 80500000 | bytes 210000 | tf_op jit(solution)/shard_map/expert_grads/pallas_call | solution.py:58
  171.5 28.6 %expert_second.1 = (bf16[4,960,512]{2,1,0:T(8,128)(2,1)}, bf16[4,960,512]{2,1,0:T(8,128)(2,1)}, bf16[960,1024]{1,0:T(8,128)(2,1)}, bf16[960,1024]{1,0:T(8,128)(2,1)}, f32[128,1024]{1,0:T(8,128)}) custom-call(s32[1]{0:T(128)} %bitcast.1.refs_0_.refs_2_, bf16[960,1024]{1,0:T(8,128)(2,1)} %bitcast.10.refs_1_.refs_2_, bf16[960,1024]{1,0:T(8,128)(2,1)} %bitcast.3.refs_2_, ...), custom_call_target="tpu_custom_call" | custom-call | flops 1150000000 | bytes 3000000 | tf_op jit(solution)/shard_map/expert_second/pallas_call | solution.py:58
  200.1 5.4 %all-to-all-start.2 = ((bf16[8,120,1024]{2,1,0:T(8,128)(2,1)}), bf16[8,120,1024]{2,1,0:T(8,128)(2,1)}, u32[]{:S(2)}, u32[]{:S(2)}) async-start(bf16[8,120,1024]{2,1,0:T(8,128)(2,1)} %bitcast.126), calls=%async_computation.2 | async-start | bytes 3932160 | tf_op jit(solution)/shard_map/all_to_all | solution.py:984
  205.5 19.9 %dense_rest.1 = (f32[768,1024]{1,0:T(8,128)}, f32[768,1024]{1,0:T(8,128)}) custom-call(s32[4]{0:T(128)} %get-tuple-element.208.refs_0_, s32[4]{0:T(128)} %constant.36.clone.refs_1_, bf16[4,768,512]{2,1,0:T(8,128)(2,1)} %get-tuple-element.84.refs_7_.refs_2_, bf16[4,768,512]{2,1,0:T(8,128)(2,1)} %get-tuple-element.89.refs_2_.refs_3_, ...), custom_call_target="tpu_custom_call" | custom-call | flops 34500001792 | bytes 90000000 | tf_op jit(solution)/shard_map/dense_rest/pallas_call | solution.py:58
  225.4 9.2 %expert_grads.5 = (bf16[2,512,1024]{2,1,0:T(8,128)(2,1)}, bf16[2,512,1024]{2,1,0:T(8,128)(2,1)}) custom-call(s32[2]{0:T(128)} %get-tuple-element.207.refs_0_, s32[2]{0:T(128)} %get-tuple-element.205.refs_1_, bf16[960,1024]{1,0:T(8,128)(2,1)} %bitcast.10.refs_1_.refs_2_, bf16[4,960,512]{2,1,0:T(8,128)(2,1)} %get-tuple-element.108.refs_3_, ...), custom_call_target="tpu_custom_call" | custom-call | flops 80500000 | bytes 210000 | tf_op jit(solution)/shard_map/expert_grads/pallas_call | solution.py:58
  237.6 9.2 %expert_grads.6 = (bf16[2,512,1024]{2,1,0:T(8,128)(2,1)}, bf16[2,512,1024]{2,1,0:T(8,128)(2,1)}) custom-call(s32[2]{0:T(128)} %get-tuple-element.206.refs_0_, s32[2]{0:T(128)} %get-tuple-element.204.refs_1_, bf16[960,1024]{1,0:T(8,128)(2,1)} %bitcast.10.refs_1_.refs_2_, bf16[4,960,512]{2,1,0:T(8,128)(2,1)} %get-tuple-element.96.refs_3_, ...), custom_call_target="tpu_custom_call" | custom-call | flops 80500000 | bytes 210000 | tf_op jit(solution)/shard_map/expert_grads/pallas_call | solution.py:58
  255.1 9.2 %expert_grads.7 = (bf16[2,512,1024]{2,1,0:T(8,128)(2,1)}, bf16[2,512,1024]{2,1,0:T(8,128)(2,1)}) custom-call(s32[2]{0:T(128)} %get-tuple-element.206.refs_0_, s32[2]{0:T(128)} %get-tuple-element.204.refs_1_, bf16[960,1024]{1,0:T(8,128)(2,1)} %bitcast.10.refs_1_.refs_2_, bf16[4,960,512]{2,1,0:T(8,128)(2,1)} %get-tuple-element.108.refs_3_, ...), custom_call_target="tpu_custom_call" | custom-call | flops 80500000 | bytes 210000 | tf_op jit(solution)/shard_map/expert_grads/pallas_call | solution.py:58
  264.4 11.8 %between.1 = (bf16[768,1024]{1,0:T(8,128)(2,1)}, bf16[768,1024]{1,0:T(8,128)(2,1)}, f32[8,1024]{1,0:T(8,128)}) custom-call(s32[768,1]{1,0:T(8,128)} %fusion.9.refs_0_, bf16[960,1024]{1,0:T(8,128)(2,1)} %bitcast.20.refs_1_, f32[768,1024]{1,0:T(8,128)} %get-tuple-element.104.refs_2_, f32[768,1024]{1,0:T(8,128)} %get-tuple-element.105.refs_6_.refs_3_.refs_2_, ...), custom_call_target="tpu_custom_call" | custom-call | flops 138000000 | bytes 360000 | tf_op jit(solution)/shard_map/between/pallas_call | solution.py:58
  276.2 5.1 %all-to-all-start.3 = ((bf16[8,120,1024]{2,1,0:T(8,128)(2,1)}), bf16[8,120,1024]{2,1,0:T(8,128)(2,1)}, u32[]{:S(2)}, u32[]{:S(2)}) async-start(bf16[8,120,1024]{2,1,0:T(8,128)(2,1)} %bitcast.125), calls=%async_computation.3 | async-start | bytes 3932160 | tf_op jit(solution)/shard_map/all_to_all | solution.py:984
  281.3 6.5 %rows_grad.2 = (bf16[4,4,32,1024]{3,2,1,0:T(8,128)(2,1)}, bf16[4,4,32,1024]{3,2,1,0:T(8,128)(2,1)}) custom-call(s32[4]{0:T(128)} %get-tuple-element.208.refs_0_, s32[4]{0:T(128)} %constant.36.clone.refs_1_, s32[1]{0:T(128)} %bitcast.1.refs_0_.refs_2_, bf16[1024,768]{1,0:T(8,128)(2,1)} %get-tuple-element.118.refs_3_, ...), custom_call_target="tpu_custom_call" | custom-call | flops 34500000 | bytes 90000 | tf_op jit(solution)/shard_map/rows_grad/pallas_call | solution.py:58
  287.8 28.3 %attend_back.1 = (bf16[3,768,1024]{2,1,0:T(8,128)(2,1)}, bf16[3,1024,768]{2,1,0:T(8,128)(2,1)}) custom-call(f32[768,1]{1,0:T(8,128)} %broadcast_in_dim.60.refs_0_, f32[8,8,768]{2,1,0:T(8,128)} %get-tuple-element.116.refs_1_, bf16[768,3072]{1,0:T(8,128)(2,1)} %get-tuple-element.75.refs_1_.refs_2_.refs_3_.refs_4_, ...), custom_call_target="tpu_custom_call" | custom-call | flops 322000000 | bytes 840000 | tf_op jit(solution)/shard_map/attend_back/pallas_call | solution.py:58
  337.5 11.5 %first_back.1 = (bf16[768,1024]{1,0:T(8,128)(2,1)}, f32[8,1024]{1,0:T(8,128)}) custom-call(bf16[3,768,1024]{2,1,0:T(8,128)(2,1)} %get-tuple-element.122.refs_3_.refs_0_, bf16[1024,3072]{1,0:T(8,128)(2,1)} %refs_1_.6, bf16[768,1024]{1,0:T(8,128)(2,1)} %refs_2_.1, bf16[768,1024]{1,0:T(8,128)(2,1)} %get-tuple-element.119.refs_4_.refs_5_.refs_3_, ...), custom_call_target="tpu_custom_call" | custom-call | flops 138000000 | bytes 360000 | tf_op jit(solution)/shard_map/first_back/pallas_call | solution.py:58
  366.5 10.2 %rows_grad.3 = (bf16[4,4,112,512]{3,2,1,0:T(8,128)(2,1)}, bf16[4,4,96,512]{3,2,1,0:T(8,128)(2,1)}, bf16[4,4,112,512]{3,2,1,0:T(8,128)(2,1)}, bf16[4,4,96,512]{3,2,1,0:T(8,128)(2,1)}) custom-call(s32[4]{0:T(128)} %get-tuple-element.208.refs_0_, s32[4]{0:T(128)} %constant.36.clone.refs_1_, s32[1]{0:T(128)} %bitcast.1.refs_0_.refs_2_, ...), custom_call_target="tpu_custom_call" | custom-call | flops 80500000 | bytes 210000 | tf_op jit(solution)/shard_map/rows_grad/pallas_call | solution.py:58
  377.4 7.3 %collective-permute-done.15.refs_7_.refs_3_ = bf16[1,512,1024]{2,1,0:T(8,128)(2,1)} collective-permute-done((bf16[1,512,1024]{2,1,0:T(8,128)(2,1)}, bf16[1,512,1024]{2,1,0:T(8,128)(2,1)}, u32[]{:S(2)}, u32[]{:S(2)}) %collective-permute-start.15) | collective-permute-done | bytes 1048608 | tf_op jit(solution)/shard_map/ppermute | solution.py:811
  385.9 6.9 %outputs.1.refs_2_ = bf16[768,1024]{1,0:T(8,128)(2,1)} custom-call(s32[768,1]{1,0:T(8,128)} %fusion.9.refs_0_, bf16[960,1024]{1,0:T(8,128)(2,1)} %bitcast.23.refs_1_, f32[768,1024]{1,0:T(8,128)} %get-tuple-element.105.refs_6_.refs_3_.refs_2_, f32[768,1024]{1,0:T(8,128)} %get-tuple-element.106.refs_4_.refs_3_, f32[768,128]{1,0:T(8,128)} %get-tuple-element.107.refs_5_.refs_4_, ...), custom_call_target="tpu_custom_call" | custom-call | flops 11500000256 | bytes 30000000 | tf_op jit(solution)/shard_map/outputs/pallas_call | solution.py:58
  402.4 4.8 up_final.1.refs_4_
  410.9 7.8 %collective-permute-done.17.refs_2_ = bf16[2,4,112,512]{3,2,1,0:T(8,128)(2,1)S(1)} collective-permute-done((bf16[2,4,112,512]{3,2,1,0:T(8,128)(2,1)}, bf16[2,4,112,512]{3,2,1,0:T(8,128)(2,1)S(1)}, u32[]{:S(2)}, u32[]{:S(2)}) %collective-permute-start.17) | collective-permute-done | bytes 917536 | tf_op jit(solution)/shard_map/ppermute | solution.py:811
  425.5 4.6 collective-permute-done.23.refs_10_
  432.9 5.6 %collective-permute-done.24.refs_11_ = bf16[1,4,32,1024]{3,2,1,0:T(8,128)(2,1)S(1)} collective-permute-done((bf16[1,4,32,1024]{3,2,1,0:T(8,128)(2,1)}, bf16[1,4,32,1024]{3,2,1,0:T(8,128)(2,1)S(1)}, u32[]{:S(2)}, u32[]{:S(2)}) %collective-permute-start.24) | collective-permute-done | bytes 262176 | tf_op jit(solution)/shard_map/ppermute | solution.py:811
  440.7 4.2 join.1.refs_0_.refs_1_
  449.8 7.4 %collective-permute-done.25.refs_1_ = bf16[2,144,1024]{2,1,0:T(8,128)(2,1)S(1)} collective-permute-done((bf16[2,144,1024]{2,1,0:T(8,128)(2,1)}, bf16[2,144,1024]{2,1,0:T(8,128)(2,1)S(1)}, u32[]{:S(2)}, u32[]{:S(2)}) %collective-permute-start.25) | collective-permute-done | bytes 589856 | tf_op jit(solution)/shard_map/ppermute | solution.py:811
  466.3 4.5 collective-permute-done.26.refs_2_
  (151 shorter events, 120.3 us)
Async XLA Ops:
  14.4 52.8 %all-to-all-start = ((bf16[8,120,1024]{2,1,0:T(8,128)(2,1)}), bf16[8,120,1024]{2,1,0:T(8,128)(2,1)}, u32[]{:S(2)}, u32[]{:S(2)}) async-start(bf16[8,120,1024]{2,1,0:T(8,128)(2,1)} %bitcast.2), calls=%async_computation | async-start | bytes 3932160 | tf_op jit(solution)/shard_map/all_to_all | solution.py:984
  71.7 63.9 %all-to-all-start.1 = ((bf16[8,120,1024]{2,1,0:T(8,128)(2,1)}), bf16[8,120,1024]{2,1,0:T(8,128)(2,1)}, u32[]{:S(2)}, u32[]{:S(2)}) async-start(bf16[8,120,1024]{2,1,0:T(8,128)(2,1)} %bitcast.9), calls=%async_computation.1 | async-start | bytes 3932160 | tf_op jit(solution)/shard_map/all_to_all | solution.py:984
  99.9 26.0 %collective-permute-start.1 = (bf16[2,4,2,128,512]{4,3,2,1,0:T(8,128)(2,1)}, bf16[2,4,2,128,512]{4,3,2,1,0:T(8,128)(2,1)}, u32[]{:S(2)}, u32[]{:S(2)}) collective-permute-start(bf16[2,4,2,128,512]{4,3,2,1,0:T(8,128)(2,1)} %get-tuple-element.88), channel_id=1, source_target_pairs={{0,1},{1,0},{2,3},{3,2},{4,5},{5,4},{6,7},{7,6},{8,9},{9,8},{10,11... | collective-permute-start | bytes 6291464 | tf_op jit(solution)/shard_map/ppermute | solution.py:811
  123.0 7.7 %collective-permute-start = (bf16[2,4,2,128,512]{4,3,2,1,0:T(8,128)(2,1)}, bf16[2,4,2,128,512]{4,3,2,1,0:T(8,128)(2,1)}, u32[]{:S(2)}, u32[]{:S(2)}) collective-permute-start(bf16[2,4,2,128,512]{4,3,2,1,0:T(8,128)(2,1)} %get-tuple-element.86), channel_id=1, source_target_pairs={{0,1},{1,0},{2,3},{3,2},{4,5},{5,4},{6,7},{7,6},{8,9},{9,8},{10,11... | collective-permute-start | bytes 6291464 | tf_op jit(solution)/shard_map/ppermute | solution.py:811
  123.1 12.5 %collective-permute-start.3 = (bf16[2,4,2,128,512]{4,3,2,1,0:T(8,128)(2,1)}, bf16[2,4,2,128,512]{4,3,2,1,0:T(8,128)(2,1)}, u32[]{:S(2)}, u32[]{:S(2)}) collective-permute-start(bf16[2,4,2,128,512]{4,3,2,1,0:T(8,128)(2,1)} %get-tuple-element.91), channel_id=1, source_target_pairs={{0,1},{1,0},{2,3},{3,2},{4,5},{5,4},{6,7},{7,6},{8,9},{9,8},{10,11... | collective-permute-start | bytes 6291464 | tf_op jit(solution)/shard_map/ppermute | solution.py:811
  123.6 12.1 %collective-permute-start.2 = (bf16[2,4,2,128,512]{4,3,2,1,0:T(8,128)(2,1)}, bf16[2,4,2,128,512]{4,3,2,1,0:T(8,128)(2,1)}, u32[]{:S(2)}, u32[]{:S(2)}) collective-permute-start(bf16[2,4,2,128,512]{4,3,2,1,0:T(8,128)(2,1)} %get-tuple-element.90), channel_id=1, source_target_pairs={{0,1},{1,0},{2,3},{3,2},{4,5},{5,4},{6,7},{7,6},{8,9},{9,8},{10,11... | collective-permute-start | bytes 6291464 | tf_op jit(solution)/shard_map/ppermute | solution.py:811
  129.2 76.3 %collective-permute-start.4 = (bf16[2,4,2,128,512]{4,3,2,1,0:T(8,128)(2,1)}, bf16[2,4,2,128,512]{4,3,2,1,0:T(8,128)(2,1)}, u32[]{:S(2)}, u32[]{:S(2)}) collective-permute-start(bf16[2,4,2,128,512]{4,3,2,1,0:T(8,128)(2,1)} %bitcast.106), channel_id=1, source_target_pairs={{0,16},{8,24},{16,0},{24,8},{1,17},{9,25},{17,1},{25,9},{2,18},{10... | collective-permute-start | bytes 6291464 | tf_op jit(solution)/shard_map/ppermute | solution.py:811
  134.1 71.4 %collective-permute-start.5 = (bf16[2,4,2,128,512]{4,3,2,1,0:T(8,128)(2,1)}, bf16[2,4,2,128,512]{4,3,2,1,0:T(8,128)(2,1)}, u32[]{:S(2)}, u32[]{:S(2)}) collective-permute-start(bf16[2,4,2,128,512]{4,3,2,1,0:T(8,128)(2,1)} %bitcast.119), channel_id=1, source_target_pairs={{0,8},{8,0},{16,24},{24,16},{1,9},{9,1},{17,25},{25,17},{2,10},{10... | collective-permute-start | bytes 6291464 | tf_op jit(solution)/shard_map/ppermute | solution.py:811
  170.5 76.3 %collective-permute-start.7 = (bf16[2,512,1024]{2,1,0:T(8,128)(2,1)}, bf16[2,512,1024]{2,1,0:T(8,128)(2,1)}, u32[]{:S(2)}, u32[]{:S(2)}) collective-permute-start(bf16[2,512,1024]{2,1,0:T(8,128)(2,1)} %get-tuple-element.98.refs_10_), channel_id=1, source_target_pairs={{0,16},{8,24},{16,0},{24,8},{1,17},{9,25},{17,1},{25,9},{2,18},{10... | collective-permute-start | bytes 6291464 | tf_op jit(solution)/shard_map/ppermute | solution.py:811
  171.0 79.1 %collective-permute-start.6 = (bf16[2,512,1024]{2,1,0:T(8,128)(2,1)}, bf16[2,512,1024]{2,1,0:T(8,128)(2,1)}, u32[]{:S(2)}, u32[]{:S(2)}) collective-permute-start(bf16[2,512,1024]{2,1,0:T(8,128)(2,1)} %get-tuple-element.111), channel_id=1, source_target_pairs={{0,8},{8,0},{16,24},{24,16},{1,9},{9,1},{17,25},{25,17},{2,10},{10... | collective-permute-start | bytes 6291464 | tf_op jit(solution)/shard_map/ppermute | solution.py:811
  200.1 64.2 %all-to-all-start.2 = ((bf16[8,120,1024]{2,1,0:T(8,128)(2,1)}), bf16[8,120,1024]{2,1,0:T(8,128)(2,1)}, u32[]{:S(2)}, u32[]{:S(2)}) async-start(bf16[8,120,1024]{2,1,0:T(8,128)(2,1)} %bitcast.126), calls=%async_computation.2 | async-start | bytes 3932160 | tf_op jit(solution)/shard_map/all_to_all | solution.py:984
  234.6 97.4 %collective-permute-start.9 = (bf16[2,512,1024]{2,1,0:T(8,128)(2,1)}, bf16[2,512,1024]{2,1,0:T(8,128)(2,1)}, u32[]{:S(2)}, u32[]{:S(2)}) collective-permute-start(bf16[2,512,1024]{2,1,0:T(8,128)(2,1)} %get-tuple-element.109.refs_6_), channel_id=1, source_target_pairs={{0,16},{8,24},{16,0},{24,8},{1,17},{9,25},{17,1},{25,9},{2,18},{10... | collective-permute-start | bytes 6291464 | tf_op jit(solution)/shard_map/ppermute | solution.py:811
  236.1 98.7 %collective-permute-start.8 = (bf16[2,512,1024]{2,1,0:T(8,128)(2,1)}, bf16[2,512,1024]{2,1,0:T(8,128)(2,1)}, u32[]{:S(2)}, u32[]{:S(2)}) collective-permute-start(bf16[2,512,1024]{2,1,0:T(8,128)(2,1)} %get-tuple-element.124), channel_id=1, source_target_pairs={{0,8},{8,0},{16,24},{24,16},{1,9},{9,1},{17,25},{25,17},{2,10},{10... | collective-permute-start | bytes 6291464 | tf_op jit(solution)/shard_map/ppermute | solution.py:811
  249.5 66.5 %collective-permute-start.11 = (bf16[1,512,1024]{2,1,0:T(8,128)(2,1)}, bf16[1,512,1024]{2,1,0:T(8,128)(2,1)}, u32[]{:S(2)}, u32[]{:S(2)}) collective-permute-start(bf16[1,512,1024]{2,1,0:T(8,128)(2,1)} %add_terms.23.refs_2_), channel_id=1, source_target_pairs={{0,8},{8,0},{16,24},{24,16},{1,9},{9,1},{17,25},{25,17},{2,10},{10... | collective-permute-start | bytes 3145736 | tf_op jit(solution)/shard_map/ppermute | solution.py:811
  252.9 66.5 %collective-permute-start.10 = (bf16[1,512,1024]{2,1,0:T(8,128)(2,1)}, bf16[1,512,1024]{2,1,0:T(8,128)(2,1)}, u32[]{:S(2)}, u32[]{:S(2)}) collective-permute-start(bf16[1,512,1024]{2,1,0:T(8,128)(2,1)} %add_terms.24.refs_6_), channel_id=1, source_target_pairs={{0,16},{8,24},{16,0},{24,8},{1,17},{9,25},{17,1},{25,9},{2,18},{10... | collective-permute-start | bytes 3145736 | tf_op jit(solution)/shard_map/ppermute | solution.py:811
  276.2 109.7 %all-to-all-start.3 = ((bf16[8,120,1024]{2,1,0:T(8,128)(2,1)}), bf16[8,120,1024]{2,1,0:T(8,128)(2,1)}, u32[]{:S(2)}, u32[]{:S(2)}) async-start(bf16[8,120,1024]{2,1,0:T(8,128)(2,1)} %bitcast.125), calls=%async_computation.3 | async-start | bytes 3932160 | tf_op jit(solution)/shard_map/all_to_all | solution.py:984
  281.3 166.8 %reduce-scatter.5.cloned.1.call-start = ((), (), s32[]{:S(2)}) async-start(), calls=%async_computation.7 | async-start | bytes 1310720 | tf_op jit(solution)/shard_map/reduce_scatter | solution.py:1085
  325.7 25.8 %collective-permute-start.13 = (bf16[1,4,2,128,512]{4,3,2,1,0:T(8,128)(2,1)}, bf16[1,4,2,128,512]{4,3,2,1,0:T(8,128)(2,1)}, u32[]{:S(2)}, u32[]{:S(2)}) collective-permute-start(bf16[1,4,2,128,512]{4,3,2,1,0:T(8,128)(2,1)} %bitcast.111), channel_id=1, source_target_pairs={{0,8},{8,0},{16,24},{24,16},{1,9},{9,1},{17,25},{25,17},{2,10},{10... | collective-permute-start | bytes 3145736 | tf_op jit(solution)/shard_map/ppermute | solution.py:811
  330.5 25.6 %collective-permute-start.12 = (bf16[1,4,2,128,512]{4,3,2,1,0:T(8,128)(2,1)}, bf16[1,4,2,128,512]{4,3,2,1,0:T(8,128)(2,1)}, u32[]{:S(2)}, u32[]{:S(2)}) collective-permute-start(bf16[1,4,2,128,512]{4,3,2,1,0:T(8,128)(2,1)} %bitcast.109), channel_id=1, source_target_pairs={{0,16},{8,24},{16,0},{24,8},{1,17},{9,25},{17,1},{25,9},{2,18},{10... | collective-permute-start | bytes 3145736 | tf_op jit(solution)/shard_map/ppermute | solution.py:811
  359.8 102.7 %reduce-scatter.3.cloned.1.call-start = ((), (), s32[]{:S(2)}) async-start(), calls=%async_computation.6 | async-start | bytes 1310720 | tf_op jit(solution)/shard_map/reduce_scatter | solution.py:1085
  359.9 24.8 %collective-permute-start.15 = (bf16[1,512,1024]{2,1,0:T(8,128)(2,1)}, bf16[1,512,1024]{2,1,0:T(8,128)(2,1)}, u32[]{:S(2)}, u32[]{:S(2)}) collective-permute-start(bf16[1,512,1024]{2,1,0:T(8,128)(2,1)} %add_terms.30.refs_5_), channel_id=1, source_target_pairs={{0,16},{8,24},{16,0},{24,8},{1,17},{9,25},{17,1},{25,9},{2,18},{10... | collective-permute-start | bytes 3145736 | tf_op jit(solution)/shard_map/ppermute | solution.py:811
  361.4 24.5 %collective-permute-start.14 = (bf16[1,512,1024]{2,1,0:T(8,128)(2,1)}, bf16[1,512,1024]{2,1,0:T(8,128)(2,1)}, u32[]{:S(2)}, u32[]{:S(2)}) collective-permute-start(bf16[1,512,1024]{2,1,0:T(8,128)(2,1)} %add_terms.29.refs_2_), channel_id=1, source_target_pairs={{0,8},{8,0},{16,24},{24,16},{1,9},{9,1},{17,25},{25,17},{2,10},{10... | collective-permute-start | bytes 3145736 | tf_op jit(solution)/shard_map/ppermute | solution.py:811
  376.8 16.1 %collective-permute-start.16 = (bf16[4,4,112,512]{3,2,1,0:T(8,128)(2,1)}, bf16[4,4,112,512]{3,2,1,0:T(8,128)(2,1)}, u32[]{:S(2)}, u32[]{:S(2)}) collective-permute-start(bf16[4,4,112,512]{3,2,1,0:T(8,128)(2,1)} %get-tuple-element.131.refs_5_), channel_id=1, source_target_pairs={{0,1},{1,0},{2,3},{3,2},{4,5},{5,4},{6,7},{7,6},{8,9},{9,8},{10,11... | collective-permute-start | bytes 5505032 | tf_op jit(solution)/shard_map/ppermute | solution.py:811
  376.8 18.9 %collective-permute-start.19 = (bf16[4,4,96,512]{3,2,1,0:T(8,128)(2,1)}, bf16[4,4,96,512]{3,2,1,0:T(8,128)(2,1)}, u32[]{:S(2)}, u32[]{:S(2)}) collective-permute-start(bf16[4,4,96,512]{3,2,1,0:T(8,128)(2,1)} %get-tuple-element.135), channel_id=1, source_target_pairs={{0,1},{1,0},{2,3},{3,2},{4,5},{5,4},{6,7},{7,6},{8,9},{9,8},{10,11... | collective-permute-start | bytes 4718600 | tf_op jit(solution)/shard_map/ppermute | solution.py:811
  377.3 21.6 %collective-permute-start.18 = (bf16[4,4,32,1024]{3,2,1,0:T(8,128)(2,1)}, bf16[4,4,32,1024]{3,2,1,0:T(8,128)(2,1)}, u32[]{:S(2)}, u32[]{:S(2)}) collective-permute-start(bf16[4,4,32,1024]{3,2,1,0:T(8,128)(2,1)} %get-tuple-element.120.refs_6_), channel_id=1, source_target_pairs={{0,1},{1,0},{2,3},{3,2},{4,5},{5,4},{6,7},{7,6},{8,9},{9,8},{10,11... | collective-permute-start | bytes 3145736 | tf_op jit(solution)/shard_map/ppermute | solution.py:811
  395.2 23.5 %collective-permute-start.17 = (bf16[2,4,112,512]{3,2,1,0:T(8,128)(2,1)}, bf16[2,4,112,512]{3,2,1,0:T(8,128)(2,1)S(1)}, u32[]{:S(2)}, u32[]{:S(2)}) collective-permute-start(bf16[2,4,112,512]{3,2,1,0:T(8,128)(2,1)} %bitcast.114), channel_id=1, source_target_pairs={{0,16},{8,24},{16,0},{24,8},{1,17},{9,25},{17,1},{25,9},{2,18},{10... | collective-permute-start | bytes 2752520 | tf_op jit(solution)/shard_map/ppermute | solution.py:811
  397.9 25.0 %collective-permute-start.21 = (bf16[2,4,96,512]{3,2,1,0:T(8,128)(2,1)}, bf16[2,4,96,512]{3,2,1,0:T(8,128)(2,1)}, u32[]{:S(2)}, u32[]{:S(2)}) collective-permute-start(bf16[2,4,96,512]{3,2,1,0:T(8,128)(2,1)} %bitcast.116), channel_id=1, source_target_pairs={{0,8},{8,0},{16,24},{24,16},{1,9},{9,1},{17,25},{25,17},{2,10},{10... | collective-permute-start | bytes 2359304 | tf_op jit(solution)/shard_map/ppermute | solution.py:811
  400.8 29.2 %collective-permute-start.23 = (bf16[2,4,32,1024]{3,2,1,0:T(8,128)(2,1)}, bf16[2,4,32,1024]{3,2,1,0:T(8,128)(2,1)}, u32[]{:S(2)}, u32[]{:S(2)}) collective-permute-start(bf16[2,4,32,1024]{3,2,1,0:T(8,128)(2,1)} %bitcast.123), channel_id=1, source_target_pairs={{0,16},{8,24},{16,0},{24,8},{1,17},{9,25},{17,1},{25,9},{2,18},{10... | collective-permute-start | bytes 1572872 | tf_op jit(solution)/shard_map/ppermute | solution.py:811
  421.9 17.4 %collective-permute-start.20 = (bf16[1,4,112,512]{3,2,1,0:T(8,128)(2,1)}, bf16[1,4,112,512]{3,2,1,0:T(8,128)(2,1)S(1)}, u32[]{:S(2)}, u32[]{:S(2)}) collective-permute-start(bf16[1,4,112,512]{3,2,1,0:T(8,128)(2,1)} %bitcast.127), channel_id=1, source_target_pairs={{0,8},{8,0},{16,24},{24,16},{1,9},{9,1},{17,25},{25,17},{2,10},{10... | collective-permute-start | bytes 1376264 | tf_op jit(solution)/shard_map/ppermute | solution.py:811
  425.0 13.5 %collective-permute-start.22 = (bf16[1,4,96,512]{3,2,1,0:T(8,128)(2,1)}, bf16[1,4,96,512]{3,2,1,0:T(8,128)(2,1)S(1)}, u32[]{:S(2)}, u32[]{:S(2)}) collective-permute-start(bf16[1,4,96,512]{3,2,1,0:T(8,128)(2,1)} %bitcast.129), channel_id=1, source_target_pairs={{0,16},{8,24},{16,0},{24,8},{1,17},{9,25},{17,1},{25,9},{2,18},{10... | collective-permute-start | bytes 1179656 | tf_op jit(solution)/shard_map/ppermute | solution.py:811
  446.8 10.4 %collective-permute-start.25 = (bf16[2,144,1024]{2,1,0:T(8,128)(2,1)}, bf16[2,144,1024]{2,1,0:T(8,128)(2,1)S(1)}, u32[]{:S(2)}, u32[]{:S(2)}) collective-permute-start(bf16[2,144,1024]{2,1,0:T(8,128)(2,1)} %add_terms.39.refs_2_), channel_id=1, source_target_pairs={{0,2},{1,3},{2,0},{3,1},{4,6},{5,7},{6,4},{7,5},{8,10},{9,11},{10,... | collective-permute-start | bytes 1769480 | tf_op jit(solution)/shard_map/ppermute | solution.py:811
  459.9 11.0 %collective-permute-start.26 = (bf16[1,144,1024]{2,1,0:T(8,128)(2,1)}, bf16[1,144,1024]{2,1,0:T(8,128)(2,1)S(1)}, u32[]{:S(2)}, u32[]{:S(2)}) collective-permute-start(bf16[1,144,1024]{2,1,0:T(8,128)(2,1)} %add_terms.40.refs_3_), channel_id=1, source_target_pairs={{0,4},{1,5},{2,6},{3,7},{4,0},{5,1},{6,2},{7,3},{8,12},{9,13},{10,... | collective-permute-start | bytes 884744 | tf_op jit(solution)/shard_map/ppermute | solution.py:811
  (16 other events, 109.8 us)
Sparse Core Ops, SparseCore 0:
  359.9 27.5 reduce-scatter.4
  389.9 25.6 reduce-scatter.2
